TPU v7x, 32 devices: a whole 2x2x4 slice. The times are simulated.
32 devices in a mesh: groups: 2 (over x), rows: 16 (over z, y, core).
Axes of the slice: x: 2, y: 2, z: 4, core: 2. Of those that a mesh axis runs over, the one named last changes fastest.
Arguments:
- tracer: float32 [128, 16384], P('groups', 'rows'), parts along dimension 0, may hold values from -6 to 6
- source: float32 [128, 16384], P('groups', 'rows'), parts along dimension 0, may hold values from -6 to 6
- exp_month_a: bfloat16 [128, 8, 128, 128], P('rows'), may hold values from -0.1875 to 0.1875
- exp_month_b: bfloat16 [128, 8, 128, 128], P('rows'), may hold values from -0.1875 to 0.1875
- imp_month_a: bfloat16 [128, 8, 128, 128], P('rows'), may hold values from -0.1875 to 0.1875
- imp_month_b: bfloat16 [128, 8, 128, 128], P('rows'), may hold values from -0.1875 to 0.1875
- col_index: int32 [128, 8], P('rows'), may hold values from 0 to 11, as said below
- block_count: int32 [128], P('rows'), may hold values from 2 to 8
- send_list: int32 [16, 4, 1], P('rows'), may hold values from 0 to 7, as said below
- wet_rows: int32 [128], P('rows'), may hold values from 32 to 128
- month_day: int32 [2], replicated, may hold values from 0 to 30
Outputs:
- tracer_out: float32 [128, 16384], P('groups', 'rows'), parts along dimension 0
There are 2 independent parts, one for each index of `groups`. A program takes and returns all parts, laid end to end along the dimension named above; an argument that names none is the same for every part. Nothing has to cross between parts.
Inputs may be any that keep to these rules, and one draw needn't show every extreme that they name: `col_index`: slot 0 of row block r is its own local block r % 8; no slot names a device outside the curve. `send_list`: the 1 entries of one device and direction are distinct.
All inputs are finite; a program needn't handle non-finite values.
Results may differ from a plain program's by a relative error of at most 0.0047.
Values may be sent and summed in bfloat16 or wider, within the bound.
No kernel may reach another device: no remote copies, remote signals or barrier semaphores. Data moves between devices by JAX's collectives and lax.ppermute only.
A program may use at most 64 MiB of HBM per device.

v0:
```python
import jax
import jax.numpy as jnp
from jax import lax
from jax.sharding import PartitionSpec as P

STEPS = 2
DAYS = 30
STRIDE = 4


def from_behind(value, axis, steps):
    count = lax.axis_size(axis)
    first, last = (max(0, -steps), min(count, count - steps))
    return lax.ppermute(value, axis, [(source, source + steps) for source in range(first, last)])


def blend_months(month_first, month_second, month_now):
    late_weight = month_now.astype(jnp.float32)
    early_weight = (DAYS - month_now).astype(jnp.float32)
    mixed = early_weight * month_first.astype(jnp.float32) + late_weight * month_second.astype(
        jnp.float32
    )
    return (mixed / DAYS).astype(jnp.bfloat16)


def fetch_halo(outgoing, phase_index):
    offsets = (1, -1, STRIDE, -STRIDE)
    pieces = []
    for direction in range(4):
        if phase_index == 0:
            incoming = from_behind(outgoing[:, direction], "rows", offsets[direction])
        else:
            incoming = from_behind(outgoing[:, direction], "rows", offsets[direction])
        pieces.append(incoming)
    return jnp.stack(pieces, 1)


def apply_blocks(rounded, matrix, col_index, slot_mask, send_rows, halo_count, phase_index):
    tracer_count, row_blocks, block_size = rounded.shape
    outgoing = rounded[:, send_rows, :].reshape(tracer_count, 4, halo_count, block_size)
    incoming = fetch_halo(outgoing, phase_index)
    extended = jnp.concatenate(
        [rounded, incoming.reshape(tracer_count, 4 * halo_count, block_size)], 1
    )
    picked = extended[:, col_index, :] * slot_mask[None, :, :, None]
    return jnp.einsum("trkj,rkij->tri", picked, matrix, preferred_element_type=jnp.float32)


def on_device(
    tracer,
    source,
    exp_month_a,
    exp_month_b,
    imp_month_a,
    imp_month_b,
    col_index,
    block_count,
    send_list,
    wet_rows,
    month_day,
):
    tracer_count = tracer.shape[0]
    row_blocks, slot_count = col_index.shape
    block_size = exp_month_a.shape[2]
    halo_count = send_list.shape[2]
    wet_mask = (jnp.arange(block_size)[None, :] < wet_rows[:, None]).astype(jnp.float32)[None]
    slot_mask = (jnp.arange(slot_count)[None, :] < block_count[:, None]).astype(jnp.bfloat16)
    send_rows = send_list[0].reshape(-1)
    tracer_state = tracer.reshape(tracer_count, row_blocks, block_size) * wet_mask
    forcing = source.reshape(tracer_count, row_blocks, block_size)
    for step_index in range(STEPS):
        month_now = month_day[step_index]
        explicit = blend_months(exp_month_a, exp_month_b, month_now)
        implicit = blend_months(imp_month_a, imp_month_b, month_now)
        rounded = tracer_state.astype(jnp.bfloat16)
        product = apply_blocks(rounded, explicit, col_index, slot_mask, send_rows, halo_count, 0)
        moved = ((product + forcing) * wet_mask).astype(jnp.bfloat16)
        tracer_state = (
            apply_blocks(moved, implicit, col_index, slot_mask, send_rows, halo_count, 1) * wet_mask
        )
    return tracer_state.reshape(tracer_count, row_blocks * block_size)


def solution(mesh):
    return jax.shard_map(
        on_device,
        mesh=mesh,
        in_specs=(
            P("groups", "rows"),
            P("groups", "rows"),
            P("rows", None, None, None),
            P("rows", None, None, None),
            P("rows", None, None, None),
            P("rows", None, None, None),
            P("rows", None),
            P("rows"),
            P("rows", None, None),
            P("rows"),
            P(),
        ),
        out_specs=P("groups", "rows"),
        check_vma=False,
    )
```

profile of v0, /device:TPU:1, one launch (start us, length us, event | category | flops | bytes accessed | tf_op | source)
XLA Modules:
  0.0 80.3 jit_solution(7827430003563745382)
XLA Ops:
  0.0 0.0 copy-start
  0.0 0.7 fusion.80
  0.7 0.7 fusion.78
  1.4 1.0 %fusion.77 = bf16[64,8,128]{2,0,1:T(8,128)(2,1)S(1)} fusion(f32[8,128]{1,0:T(8,128)S(1)} %fusion.78, f32[64,1024]{1,0:T(8,128)} %param.11), kind=kLoop, calls=%fused_computation.61 | loop fusion | flops 131072 | bytes 397312 | tf_op jit(solution)/shard_map/convert_element_type | solution.py:75
  2.4 0.6 gather_fusion
  3.0 4.5 %collective-permute-start = (bf16[64,1,128]{2,0,1:T(8,128)(2,1)S(1)}, bf16[64,1,128]{2,0,1:T(8,128)(2,1)S(1)}, u32[]{:S(2)}, u32[]{:S(2)}) collective-permute-start(bf16[64,1,128]{2,0,1:T(8,128)(2,1)S(1)} %get-tuple-element.17), channel_id=1, source_target_pairs={{0,1},{1,2},{2,3},{3,4},{4,5},{5,6},{6,7},{7,8},{8,9},{9,10},{10,1... | collective-permute-start | bytes 49160 | tf_op jit(solution)/shard_map/ppermute | solution.py:14
  7.5 1.3 %collective-permute-start.3 = (bf16[64,1,128]{2,0,1:T(8,128)(2,1)S(1)}, bf16[64,1,128]{2,0,1:T(8,128)(2,1)S(1)}, u32[]{:S(2)}, u32[]{:S(2)}) collective-permute-start(bf16[64,1,128]{2,0,1:T(8,128)(2,1)S(1)} %get-tuple-element.18), channel_id=1, source_target_pairs={{4,0},{5,1},{6,2},{7,3},{8,4},{9,5},{10,6},{11,7},{12,8},{13,9},{1... | collective-permute-start | bytes 49160 | tf_op jit(solution)/shard_map/ppermute | solution.py:14
  8.8 4.0 %collective-permute-start.2 = (bf16[64,1,128]{2,0,1:T(8,128)(2,1)S(1)}, bf16[64,1,128]{2,0,1:T(8,128)(2,1)S(1)}, u32[]{:S(2)}, u32[]{:S(2)}) collective-permute-start(bf16[64,1,128]{2,0,1:T(8,128)(2,1)S(1)} %get-tuple-element.19), channel_id=1, source_target_pairs={{0,4},{1,5},{2,6},{3,7},{4,8},{5,9},{6,10},{7,11},{8,12},{9,13},{1... | collective-permute-start | bytes 49160 | tf_op jit(solution)/shard_map/ppermute | solution.py:14
  12.8 1.9 %collective-permute-start.1 = (bf16[64,1,128]{2,0,1:T(8,128)(2,1)S(1)}, bf16[64,1,128]{2,0,1:T(8,128)(2,1)S(1)}, u32[]{:S(2)}, u32[]{:S(2)}) collective-permute-start(bf16[64,1,128]{2,0,1:T(8,128)(2,1)S(1)} %get-tuple-element.20), channel_id=1, source_target_pairs={{1,0},{2,1},{3,2},{4,3},{5,4},{6,5},{7,6},{8,7},{9,8},{10,9},{11,1... | collective-permute-start | bytes 49160 | tf_op jit(solution)/shard_map/ppermute | solution.py:14
  14.8 1.3 %fusion.85 = (s32[1]{0:T(128)}, s32[1]{0:T(128)}) fusion(s32[2]{0:T(128)} %param.21), kind=kLoop, calls=%fused_computation.99 | loop fusion | bytes 16 | tf_op jit(solution)/shard_map/slice | solution.py:72
  16.1 0.7 fusion.79
  16.8 0.7 compare_select_fusion
  17.5 0.1 reshape.131
  18.9 0.0 collective-permute-done
  18.9 0.0 collective-permute-done.3
  18.9 0.0 collective-permute-done.2
  18.9 0.0 collective-permute-done.1
  19.0 0.7 gather_fusion.1
  19.7 0.0 copy-done
  19.8 3.5 %fusion.59 = bf16[64,8,128]{2,0,1:T(8,128)(2,1)S(1)} fusion(bf16[8,8,128,128]{3,2,1,0:T(8,128)(2,1)} %param.13, bf16[8,8,128,128]{3,2,1,0:T(8,128)(2,1)} %param.14, f32[]{:T(128)} %bitcast.3, f32[]{:T(128)} %bitcast.2, bf16[8,8,64,128]{3,2,1,0:T(8,128)(2,1)S(1)} %bitcast.179, bf16[8,8]{1,0:T(8,128)(2,1)S(1)} %fusion.79, f32[8,128]{1,0:T(8,128)S(1)} %fusion.78, ...), kind=kOutput, calls=%fused_computation.45 | convolution fusion | flops 142278656 | bytes 5640328 | tf_op jit(solution)/shard_map/trkj,rkij->tri/dot_general | solution.py:46
  23.3 0.6 gather_fusion.2
  23.8 3.6 %collective-permute-start.4 = (bf16[64,1,128]{2,0,1:T(8,128)(2,1)S(1)}, bf16[64,1,128]{2,0,1:T(8,128)(2,1)S(1)}, u32[]{:S(2)}, u32[]{:S(2)}) collective-permute-start(bf16[64,1,128]{2,0,1:T(8,128)(2,1)S(1)} %get-tuple-element.13), channel_id=1, source_target_pairs={{0,1},{1,2},{2,3},{3,4},{4,5},{5,6},{6,7},{7,8},{8,9},{9,10},{10,1... | collective-permute-start | bytes 49160 | tf_op jit(solution)/shard_map/ppermute | solution.py:14
  27.5 1.3 %collective-permute-start.7 = (bf16[64,1,128]{2,0,1:T(8,128)(2,1)S(1)}, bf16[64,1,128]{2,0,1:T(8,128)(2,1)S(1)}, u32[]{:S(2)}, u32[]{:S(2)}) collective-permute-start(bf16[64,1,128]{2,0,1:T(8,128)(2,1)S(1)} %get-tuple-element.14), channel_id=1, source_target_pairs={{4,0},{5,1},{6,2},{7,3},{8,4},{9,5},{10,6},{11,7},{12,8},{13,9},{1... | collective-permute-start | bytes 49160 | tf_op jit(solution)/shard_map/ppermute | solution.py:14
  28.8 4.0 %collective-permute-start.6 = (bf16[64,1,128]{2,0,1:T(8,128)(2,1)S(1)}, bf16[64,1,128]{2,0,1:T(8,128)(2,1)S(1)}, u32[]{:S(2)}, u32[]{:S(2)}) collective-permute-start(bf16[64,1,128]{2,0,1:T(8,128)(2,1)S(1)} %get-tuple-element.15), channel_id=1, source_target_pairs={{0,4},{1,5},{2,6},{3,7},{4,8},{5,9},{6,10},{7,11},{8,12},{9,13},{1... | collective-permute-start | bytes 49160 | tf_op jit(solution)/shard_map/ppermute | solution.py:14
  32.8 1.9 %collective-permute-start.5 = (bf16[64,1,128]{2,0,1:T(8,128)(2,1)S(1)}, bf16[64,1,128]{2,0,1:T(8,128)(2,1)S(1)}, u32[]{:S(2)}, u32[]{:S(2)}) collective-permute-start(bf16[64,1,128]{2,0,1:T(8,128)(2,1)S(1)} %get-tuple-element.16), channel_id=1, source_target_pairs={{1,0},{2,1},{3,2},{4,3},{5,4},{6,5},{7,6},{8,7},{9,8},{10,9},{11,1... | collective-permute-start | bytes 49160 | tf_op jit(solution)/shard_map/ppermute | solution.py:14
  34.7 0.0 collective-permute-done.4
  34.7 0.0 collective-permute-done.7
  34.7 0.0 collective-permute-done.6
  34.8 3.1 %collective-permute-done.5 = bf16[64,1,128]{2,0,1:T(8,128)(2,1)S(1)} collective-permute-done((bf16[64,1,128]{2,0,1:T(8,128)(2,1)S(1)}, bf16[64,1,128]{2,0,1:T(8,128)(2,1)S(1)}, u32[]{:S(2)}, u32[]{:S(2)}) %collective-permute-start.5) | collective-permute-done | bytes 16416 | tf_op jit(solution)/shard_map/ppermute | solution.py:14
  37.9 0.7 gather_fusion.3
  38.7 3.5 %fusion.62 = bf16[64,8,128]{2,0,1:T(8,128)(2,1)S(1)} fusion(bf16[8,8,128,128]{3,2,1,0:T(8,128)(2,1)} %param.15, bf16[8,8,128,128]{3,2,1,0:T(8,128)(2,1)} %param.16, f32[]{:T(128)} %bitcast.3, f32[]{:T(128)} %bitcast.2, bf16[8,8,64,128]{3,2,1,0:T(8,128)(2,1)S(1)} %bitcast.178, bf16[8,8]{1,0:T(8,128)(2,1)S(1)} %fusion.79, f32[8,128]{1,0:T(8,128)S(1)} %fusion.78), kind=kOutput, calls=%fused_computation.46 | convolution fusion | flops 142213120 | bytes 5378184 | tf_op jit(solution)/shard_map/trkj,rkij->tri/dot_general | solution.py:46
  42.1 0.6 gather_fusion.4
  42.7 2.0 %collective-permute-start.8 = (bf16[64,1,128]{2,0,1:T(8,128)(2,1)S(1)}, bf16[64,1,128]{2,0,1:T(8,128)(2,1)S(1)}, u32[]{:S(2)}, u32[]{:S(2)}) collective-permute-start(bf16[64,1,128]{2,0,1:T(8,128)(2,1)S(1)} %get-tuple-element.9), channel_id=1, source_target_pairs={{0,1},{1,2},{2,3},{3,4},{4,5},{5,6},{6,7},{7,8},{8,9},{9,10},{10,1... | collective-permute-start | bytes 49160 | tf_op jit(solution)/shard_map/ppermute | solution.py:14
  44.7 1.3 %collective-permute-start.11 = (bf16[64,1,128]{2,0,1:T(8,128)(2,1)S(1)}, bf16[64,1,128]{2,0,1:T(8,128)(2,1)S(1)}, u32[]{:S(2)}, u32[]{:S(2)}) collective-permute-start(bf16[64,1,128]{2,0,1:T(8,128)(2,1)S(1)} %get-tuple-element.10), channel_id=1, source_target_pairs={{4,0},{5,1},{6,2},{7,3},{8,4},{9,5},{10,6},{11,7},{12,8},{13,9},{1... | collective-permute-start | bytes 49160 | tf_op jit(solution)/shard_map/ppermute | solution.py:14
  46.0 4.0 %collective-permute-start.10 = (bf16[64,1,128]{2,0,1:T(8,128)(2,1)S(1)}, bf16[64,1,128]{2,0,1:T(8,128)(2,1)S(1)}, u32[]{:S(2)}, u32[]{:S(2)}) collective-permute-start(bf16[64,1,128]{2,0,1:T(8,128)(2,1)S(1)} %get-tuple-element.11), channel_id=1, source_target_pairs={{0,4},{1,5},{2,6},{3,7},{4,8},{5,9},{6,10},{7,11},{8,12},{9,13},{1... | collective-permute-start | bytes 49160 | tf_op jit(solution)/shard_map/ppermute | solution.py:14
  50.0 2.9 %collective-permute-start.9 = (bf16[64,1,128]{2,0,1:T(8,128)(2,1)S(1)}, bf16[64,1,128]{2,0,1:T(8,128)(2,1)S(1)}, u32[]{:S(2)}, u32[]{:S(2)}) collective-permute-start(bf16[64,1,128]{2,0,1:T(8,128)(2,1)S(1)} %get-tuple-element.12), channel_id=1, source_target_pairs={{1,0},{2,1},{3,2},{4,3},{5,4},{6,5},{7,6},{8,7},{9,8},{10,9},{11,1... | collective-permute-start | bytes 49160 | tf_op jit(solution)/shard_map/ppermute | solution.py:14
  54.1 0.0 collective-permute-done.8
  54.1 0.0 collective-permute-done.11
  54.2 0.0 collective-permute-done.10
  54.2 3.1 %collective-permute-done.9 = bf16[64,1,128]{2,0,1:T(8,128)(2,1)S(1)} collective-permute-done((bf16[64,1,128]{2,0,1:T(8,128)(2,1)S(1)}, bf16[64,1,128]{2,0,1:T(8,128)(2,1)S(1)}, u32[]{:S(2)}, u32[]{:S(2)}) %collective-permute-start.9) | collective-permute-done | bytes 16416 | tf_op jit(solution)/shard_map/ppermute | solution.py:14
  57.3 0.7 gather_fusion.5
  58.0 3.5 %fusion.56 = bf16[64,8,128]{2,0,1:T(8,128)(2,1)S(1)} fusion(bf16[8,8,128,128]{3,2,1,0:T(8,128)(2,1)} %param.13, bf16[8,8,128,128]{3,2,1,0:T(8,128)(2,1)} %param.14, f32[]{:T(128)} %bitcast.1, f32[]{:T(128)} %bitcast, bf16[8,8,64,128]{3,2,1,0:T(8,128)(2,1)S(1)} %bitcast.180, bf16[8,8]{1,0:T(8,128)(2,1)S(1)} %fusion.79, f32[8,128]{1,0:T(8,128)S(1)} %fusion.78, ...), kind=kOutput, calls=%fused_computation.44 | convolution fusion | flops 142278656 | bytes 5640328 | tf_op jit(solution)/shard_map/trkj,rkij->tri/dot_general | solution.py:46
  61.5 0.6 gather_fusion.6
  62.1 1.9 %collective-permute-start.12 = (bf16[64,1,128]{2,0,1:T(8,128)(2,1)S(1)}, bf16[64,1,128]{2,0,1:T(8,128)(2,1)S(1)}, u32[]{:S(2)}, u32[]{:S(2)}) collective-permute-start(bf16[64,1,128]{2,0,1:T(8,128)(2,1)S(1)} %get-tuple-element.5), channel_id=1, source_target_pairs={{0,1},{1,2},{2,3},{3,4},{4,5},{5,6},{6,7},{7,8},{8,9},{9,10},{10,1... | collective-permute-start | bytes 49160 | tf_op jit(solution)/shard_map/ppermute | solution.py:14
  64.1 1.3 %collective-permute-start.15 = (bf16[64,1,128]{2,0,1:T(8,128)(2,1)S(1)}, bf16[64,1,128]{2,0,1:T(8,128)(2,1)S(1)}, u32[]{:S(2)}, u32[]{:S(2)}) collective-permute-start(bf16[64,1,128]{2,0,1:T(8,128)(2,1)S(1)} %get-tuple-element.6), channel_id=1, source_target_pairs={{4,0},{5,1},{6,2},{7,3},{8,4},{9,5},{10,6},{11,7},{12,8},{13,9},{1... | collective-permute-start | bytes 49160 | tf_op jit(solution)/shard_map/ppermute | solution.py:14
  65.4 4.0 %collective-permute-start.14 = (bf16[64,1,128]{2,0,1:T(8,128)(2,1)S(1)}, bf16[64,1,128]{2,0,1:T(8,128)(2,1)S(1)}, u32[]{:S(2)}, u32[]{:S(2)}) collective-permute-start(bf16[64,1,128]{2,0,1:T(8,128)(2,1)S(1)} %get-tuple-element.7), channel_id=1, source_target_pairs={{0,4},{1,5},{2,6},{3,7},{4,8},{5,9},{6,10},{7,11},{8,12},{9,13},{1... | collective-permute-start | bytes 49160 | tf_op jit(solution)/shard_map/ppermute | solution.py:14
  69.4 2.9 %collective-permute-start.13 = (bf16[64,1,128]{2,0,1:T(8,128)(2,1)S(1)}, bf16[64,1,128]{2,0,1:T(8,128)(2,1)S(1)}, u32[]{:S(2)}, u32[]{:S(2)}) collective-permute-start(bf16[64,1,128]{2,0,1:T(8,128)(2,1)S(1)} %get-tuple-element.8), channel_id=1, source_target_pairs={{1,0},{2,1},{3,2},{4,3},{5,4},{6,5},{7,6},{8,7},{9,8},{10,9},{11,1... | collective-permute-start | bytes 49160 | tf_op jit(solution)/shard_map/ppermute | solution.py:14
  72.3 0.0 collective-permute-done.12
  72.3 0.0 collective-permute-done.15
  72.3 0.0 collective-permute-done.14
  72.3 3.0 %collective-permute-done.13 = bf16[64,1,128]{2,0,1:T(8,128)(2,1)S(1)} collective-permute-done((bf16[64,1,128]{2,0,1:T(8,128)(2,1)S(1)}, bf16[64,1,128]{2,0,1:T(8,128)(2,1)S(1)}, u32[]{:S(2)}, u32[]{:S(2)}) %collective-permute-start.13) | collective-permute-done | bytes 16416 | tf_op jit(solution)/shard_map/ppermute | solution.py:14
  75.4 0.7 gather_fusion.7
  76.1 3.4 %fusion.50 = f32[8,8,8,128]{3,2,1,0:T(8,128)S(1)} fusion(bf16[8,8,128,128]{3,2,1,0:T(8,128)(2,1)} %param.15, bf16[8,8,128,128]{3,2,1,0:T(8,128)(2,1)} %param.16, f32[]{:T(128)} %bitcast.1, f32[]{:T(128)} %bitcast, bf16[8,8,64,128]{3,2,1,0:T(8,128)(2,1)S(1)} %bitcast.177, bf16[8,8]{1,0:T(8,128)(2,1)S(1)} %fusion.79, f32[8,128]{1,0:T(8,128)S(1)} %fusion.78), kind=kOutput, calls=%fused_computation.42 | convolution fusion | flops 142147584 | bytes 5509256 | tf_op jit(solution)/shard_map/trkj,rkij->tri/dot_general | solution.py:46
  79.6 0.7 copy.51
  (14 shorter events, 0.2 us)
Async XLA Ops:
  0.0 19.8 %copy-start = (f32[64,1024]{1,0:T(8,128)S(1)}, f32[64,1024]{1,0:T(8,128)}, u32[]{:S(2)}) copy-start(f32[64,1024]{1,0:T(8,128)} %param.12) | copy-start | bytes 786436
  3.0 15.9 %collective-permute-start = (bf16[64,1,128]{2,0,1:T(8,128)(2,1)S(1)}, bf16[64,1,128]{2,0,1:T(8,128)(2,1)S(1)}, u32[]{:S(2)}, u32[]{:S(2)}) collective-permute-start(bf16[64,1,128]{2,0,1:T(8,128)(2,1)S(1)} %get-tuple-element.17), channel_id=1, source_target_pairs={{0,1},{1,2},{2,3},{3,4},{4,5},{5,6},{6,7},{7,8},{8,9},{9,10},{10,1... | collective-permute-start | bytes 49160 | tf_op jit(solution)/shard_map/ppermute | solution.py:14
  7.5 11.4 %collective-permute-start.3 = (bf16[64,1,128]{2,0,1:T(8,128)(2,1)S(1)}, bf16[64,1,128]{2,0,1:T(8,128)(2,1)S(1)}, u32[]{:S(2)}, u32[]{:S(2)}) collective-permute-start(bf16[64,1,128]{2,0,1:T(8,128)(2,1)S(1)} %get-tuple-element.18), channel_id=1, source_target_pairs={{4,0},{5,1},{6,2},{7,3},{8,4},{9,5},{10,6},{11,7},{12,8},{13,9},{1... | collective-permute-start | bytes 49160 | tf_op jit(solution)/shard_map/ppermute | solution.py:14
  8.8 10.1 %collective-permute-start.2 = (bf16[64,1,128]{2,0,1:T(8,128)(2,1)S(1)}, bf16[64,1,128]{2,0,1:T(8,128)(2,1)S(1)}, u32[]{:S(2)}, u32[]{:S(2)}) collective-permute-start(bf16[64,1,128]{2,0,1:T(8,128)(2,1)S(1)} %get-tuple-element.19), channel_id=1, source_target_pairs={{0,4},{1,5},{2,6},{3,7},{4,8},{5,9},{6,10},{7,11},{8,12},{9,13},{1... | collective-permute-start | bytes 49160 | tf_op jit(solution)/shard_map/ppermute | solution.py:14
  12.8 6.1 %collective-permute-start.1 = (bf16[64,1,128]{2,0,1:T(8,128)(2,1)S(1)}, bf16[64,1,128]{2,0,1:T(8,128)(2,1)S(1)}, u32[]{:S(2)}, u32[]{:S(2)}) collective-permute-start(bf16[64,1,128]{2,0,1:T(8,128)(2,1)S(1)} %get-tuple-element.20), channel_id=1, source_target_pairs={{1,0},{2,1},{3,2},{4,3},{5,4},{6,5},{7,6},{8,7},{9,8},{10,9},{11,1... | collective-permute-start | bytes 49160 | tf_op jit(solution)/shard_map/ppermute | solution.py:14
  23.8 10.9 %collective-permute-start.4 = (bf16[64,1,128]{2,0,1:T(8,128)(2,1)S(1)}, bf16[64,1,128]{2,0,1:T(8,128)(2,1)S(1)}, u32[]{:S(2)}, u32[]{:S(2)}) collective-permute-start(bf16[64,1,128]{2,0,1:T(8,128)(2,1)S(1)} %get-tuple-element.13), channel_id=1, source_target_pairs={{0,1},{1,2},{2,3},{3,4},{4,5},{5,6},{6,7},{7,8},{8,9},{9,10},{10,1... | collective-permute-start | bytes 49160 | tf_op jit(solution)/shard_map/ppermute | solution.py:14
  27.5 7.2 %collective-permute-start.7 = (bf16[64,1,128]{2,0,1:T(8,128)(2,1)S(1)}, bf16[64,1,128]{2,0,1:T(8,128)(2,1)S(1)}, u32[]{:S(2)}, u32[]{:S(2)}) collective-permute-start(bf16[64,1,128]{2,0,1:T(8,128)(2,1)S(1)} %get-tuple-element.14), channel_id=1, source_target_pairs={{4,0},{5,1},{6,2},{7,3},{8,4},{9,5},{10,6},{11,7},{12,8},{13,9},{1... | collective-permute-start | bytes 49160 | tf_op jit(solution)/shard_map/ppermute | solution.py:14
  28.8 5.9 %collective-permute-start.6 = (bf16[64,1,128]{2,0,1:T(8,128)(2,1)S(1)}, bf16[64,1,128]{2,0,1:T(8,128)(2,1)S(1)}, u32[]{:S(2)}, u32[]{:S(2)}) collective-permute-start(bf16[64,1,128]{2,0,1:T(8,128)(2,1)S(1)} %get-tuple-element.15), channel_id=1, source_target_pairs={{0,4},{1,5},{2,6},{3,7},{4,8},{5,9},{6,10},{7,11},{8,12},{9,13},{1... | collective-permute-start | bytes 49160 | tf_op jit(solution)/shard_map/ppermute | solution.py:14
  32.8 5.1 %collective-permute-start.5 = (bf16[64,1,128]{2,0,1:T(8,128)(2,1)S(1)}, bf16[64,1,128]{2,0,1:T(8,128)(2,1)S(1)}, u32[]{:S(2)}, u32[]{:S(2)}) collective-permute-start(bf16[64,1,128]{2,0,1:T(8,128)(2,1)S(1)} %get-tuple-element.16), channel_id=1, source_target_pairs={{1,0},{2,1},{3,2},{4,3},{5,4},{6,5},{7,6},{8,7},{9,8},{10,9},{11,1... | collective-permute-start | bytes 49160 | tf_op jit(solution)/shard_map/ppermute | solution.py:14
  42.7 11.4 %collective-permute-start.8 = (bf16[64,1,128]{2,0,1:T(8,128)(2,1)S(1)}, bf16[64,1,128]{2,0,1:T(8,128)(2,1)S(1)}, u32[]{:S(2)}, u32[]{:S(2)}) collective-permute-start(bf16[64,1,128]{2,0,1:T(8,128)(2,1)S(1)} %get-tuple-element.9), channel_id=1, source_target_pairs={{0,1},{1,2},{2,3},{3,4},{4,5},{5,6},{6,7},{7,8},{8,9},{9,10},{10,1... | collective-permute-start | bytes 49160 | tf_op jit(solution)/shard_map/ppermute | solution.py:14
  44.7 9.5 %collective-permute-start.11 = (bf16[64,1,128]{2,0,1:T(8,128)(2,1)S(1)}, bf16[64,1,128]{2,0,1:T(8,128)(2,1)S(1)}, u32[]{:S(2)}, u32[]{:S(2)}) collective-permute-start(bf16[64,1,128]{2,0,1:T(8,128)(2,1)S(1)} %get-tuple-element.10), channel_id=1, source_target_pairs={{4,0},{5,1},{6,2},{7,3},{8,4},{9,5},{10,6},{11,7},{12,8},{13,9},{1... | collective-permute-start | bytes 49160 | tf_op jit(solution)/shard_map/ppermute | solution.py:14
  46.0 8.2 %collective-permute-start.10 = (bf16[64,1,128]{2,0,1:T(8,128)(2,1)S(1)}, bf16[64,1,128]{2,0,1:T(8,128)(2,1)S(1)}, u32[]{:S(2)}, u32[]{:S(2)}) collective-permute-start(bf16[64,1,128]{2,0,1:T(8,128)(2,1)S(1)} %get-tuple-element.11), channel_id=1, source_target_pairs={{0,4},{1,5},{2,6},{3,7},{4,8},{5,9},{6,10},{7,11},{8,12},{9,13},{1... | collective-permute-start | bytes 49160 | tf_op jit(solution)/shard_map/ppermute | solution.py:14
  50.0 7.3 %collective-permute-start.9 = (bf16[64,1,128]{2,0,1:T(8,128)(2,1)S(1)}, bf16[64,1,128]{2,0,1:T(8,128)(2,1)S(1)}, u32[]{:S(2)}, u32[]{:S(2)}) collective-permute-start(bf16[64,1,128]{2,0,1:T(8,128)(2,1)S(1)} %get-tuple-element.12), channel_id=1, source_target_pairs={{1,0},{2,1},{3,2},{4,3},{5,4},{6,5},{7,6},{8,7},{9,8},{10,9},{11,1... | collective-permute-start | bytes 49160 | tf_op jit(solution)/shard_map/ppermute | solution.py:14
  62.1 10.2 %collective-permute-start.12 = (bf16[64,1,128]{2,0,1:T(8,128)(2,1)S(1)}, bf16[64,1,128]{2,0,1:T(8,128)(2,1)S(1)}, u32[]{:S(2)}, u32[]{:S(2)}) collective-permute-start(bf16[64,1,128]{2,0,1:T(8,128)(2,1)S(1)} %get-tuple-element.5), channel_id=1, source_target_pairs={{0,1},{1,2},{2,3},{3,4},{4,5},{5,6},{6,7},{7,8},{8,9},{9,10},{10,1... | collective-permute-start | bytes 49160 | tf_op jit(solution)/shard_map/ppermute | solution.py:14
  64.1 8.3 %collective-permute-start.15 = (bf16[64,1,128]{2,0,1:T(8,128)(2,1)S(1)}, bf16[64,1,128]{2,0,1:T(8,128)(2,1)S(1)}, u32[]{:S(2)}, u32[]{:S(2)}) collective-permute-start(bf16[64,1,128]{2,0,1:T(8,128)(2,1)S(1)} %get-tuple-element.6), channel_id=1, source_target_pairs={{4,0},{5,1},{6,2},{7,3},{8,4},{9,5},{10,6},{11,7},{12,8},{13,9},{1... | collective-permute-start | bytes 49160 | tf_op jit(solution)/shard_map/ppermute | solution.py:14
  65.4 7.0 %collective-permute-start.14 = (bf16[64,1,128]{2,0,1:T(8,128)(2,1)S(1)}, bf16[64,1,128]{2,0,1:T(8,128)(2,1)S(1)}, u32[]{:S(2)}, u32[]{:S(2)}) collective-permute-start(bf16[64,1,128]{2,0,1:T(8,128)(2,1)S(1)} %get-tuple-element.7), channel_id=1, source_target_pairs={{0,4},{1,5},{2,6},{3,7},{4,8},{5,9},{6,10},{7,11},{8,12},{9,13},{1... | collective-permute-start | bytes 49160 | tf_op jit(solution)/shard_map/ppermute | solution.py:14
  69.4 6.0 %collective-permute-start.13 = (bf16[64,1,128]{2,0,1:T(8,128)(2,1)S(1)}, bf16[64,1,128]{2,0,1:T(8,128)(2,1)S(1)}, u32[]{:S(2)}, u32[]{:S(2)}) collective-permute-start(bf16[64,1,128]{2,0,1:T(8,128)(2,1)S(1)} %get-tuple-element.8), channel_id=1, source_target_pairs={{1,0},{2,1},{3,2},{4,3},{5,4},{6,5},{7,6},{8,7},{9,8},{10,9},{11,1... | collective-permute-start | bytes 49160 | tf_op jit(solution)/shard_map/ppermute | solution.py:14
where the time goes:
time: 80.9 us; the launch traced here: 80.3 us
  starting transfers between devices  42.9 us (53%)
  matrix products  13.9 us (17%)
  waiting for transfers between devices  9.15 us (11%)
  local copies, waits for them, and re-layouts  7.42 us (9%)
  other arithmetic  3.96 us (5%)
  between operations  2.94 us (4%)
    ppermute x16, starting transfers between devices, from_behind(): lax.ppermute(value, axis, [(source, source + steps) for source in range(f...  42.9 us
    dot_general x4, matrix products, apply_blocks(): jnp.einsum('trkj,rkij->tri', picked, matrix, preferred_element_type=jnp.f...  13.9 us
    ppermute x16, waiting for transfers between devices, from_behind(): lax.ppermute(value, axis, [(source, source + steps) for source in range(f...  9.15 us
    gather x4, local copies, waits for them, and re-layouts, apply_blocks(): picked = extended[:, col_index, :] * slot_mask[None, :, :, None]  3 us
    gather x4, local copies, waits for them, and re-layouts, apply_blocks(): rounded[:, send_rows, :].reshape(tracer_count, 4, halo_count, block_size)  2.26 us
  transfers between devices with their start and end apart: 16, of which 3 were waited for; matrix products, arithmetic and copies ran while one was open for 4% of the time, Pallas kernels for 0%

commit v1 on v0

v1 whole, which is shorter than its diff:
```python
import functools

import jax
import jax.numpy as jnp
from jax import lax
from jax.experimental import pallas as pl
from jax.experimental.pallas import tpu as pltpu
from jax.sharding import PartitionSpec as P

STEPS = 2
DAYS = 30
STRIDE = 4
DIRECTIONS = 4


def swap_pairs(count, groups, stride, parity):
    partner = {}
    for i in range(count - stride):
        if (i // stride) % 2 == parity:
            partner[i], partner[i + stride] = i + stride, i
    idle = [i for i in range(count) if i not in partner]
    for i in idle:
        if i ^ 1 in idle:
            partner[i] = i ^ 1
    pairs = []
    for g in range(groups):
        for i in range(count):
            if i in partner:
                pairs.append((g * count + i, g * count + partner[i]))
            else:
                other = g ^ 1 if g ^ 1 < groups else g
                pairs.append((g * count + i, other * count + i))
    return pairs


def my_flips():
    place = lax.axis_index("rows")
    return 1 - place % 2, 1 - (place // STRIDE) % 2


def direction_of(swap, flips):
    if swap < 2:
        return swap ^ 1 ^ flips[0]
    return 2 + ((swap - 2) ^ 1 ^ flips[1])


def first_kernel(tracer_ref, send_ref, wet_ref, c_ref, o_ref, z_ref, y_ref, buf, sems):
    flips = my_flips()
    block = buf.shape[2]
    rows = [send_ref[0, direction_of(n, flips), 0] for n in range(DIRECTIONS)]
    copies = []
    for n in range(DIRECTIONS):
        start = pl.multiple_of(rows[n] * block, block)
        copy = pltpu.make_async_copy(tracer_ref.at[:, pl.ds(start, block)], buf.at[n], sems.at[n])
        copy.start()
        copies.append(copy)
    lane = lax.broadcasted_iota(jnp.int32, buf.shape[1:], 1)
    for n, out in enumerate((c_ref, o_ref, z_ref, y_ref)):
        copies[n].wait()
        out[...] = jnp.where(lane < wet_ref[rows[n]], buf[n], 0.0).astype(out.dtype)


def blend_kernel(step, a_ref, b_ref, day_ref, out_ref):
    day = day_ref[step]
    late = day.astype(jnp.float32) / DAYS
    early = (DAYS - day).astype(jnp.float32) / DAYS
    row_blocks, slots, block, _ = a_ref.shape

    def one(r, carry):
        for k in range(slots):
            mixed = early * a_ref[r, k].astype(jnp.float32) + late * b_ref[r, k].astype(jnp.float32)
            out_ref[r, :, pl.ds(k * block, block)] = mixed.astype(out_ref.dtype)
        return carry

    lax.fori_loop(0, row_blocks, one, 0)


def apply_kernel(first, explicit, last, *refs):
    refs = list(refs)
    col_ref, count_ref, send_ref, wet_ref, field_ref, matrix_ref = refs[:6]
    halos = refs[6:10]
    refs = refs[10:]
    source_ref = refs.pop(0) if explicit else None
    out_ref = refs.pop(0)
    outgoing = [] if last else refs[:4]
    ext, picked = refs[-2:]
    flips = my_flips()
    row_blocks, slots = col_ref.shape
    block = matrix_ref.shape[1]
    lane = lax.broadcasted_iota(jnp.int32, ext.shape[1:], 1)
    for r in range(row_blocks):
        if first:
            own = field_ref[:, pl.ds(r * block, block)]
            ext[r] = jnp.where(lane < wet_ref[r], own, 0.0).astype(ext.dtype)
        else:
            ext[r] = field_ref[r]
    for n in range(DIRECTIONS):
        ext[row_blocks + n] = halos[n][...]
    nothing = row_blocks + DIRECTIONS
    ext[nothing] = jnp.zeros(ext.shape[1:], ext.dtype)
    for r in range(row_blocks):
        for k in range(slots):
            slot = col_ref[r, k]
            j = slot - row_blocks
            moved = row_blocks + (j ^ jnp.where(j < 2, flips[0], flips[1]))
            place = jnp.where(slot < row_blocks, slot, moved)
            place = jnp.where(k < count_ref[r], place, nothing)
            picked[r, :, pl.ds(k * block, block)] = ext[place]
    for r in range(row_blocks):
        total = lax.dot_general(
            picked[r], matrix_ref[r], (((1,), (1,)), ((), ())), preferred_element_type=jnp.float32
        )
        if explicit:
            total = total + source_ref[:, pl.ds(r * block, block)]
        total = jnp.where(lane < wet_ref[r], total, 0.0)
        if last:
            out_ref[:, pl.ds(r * block, block)] = total
        else:
            out_ref[r] = total.astype(out_ref.dtype)
    for n, out in enumerate(outgoing):
        out[...] = out_ref[send_ref[0, direction_of(n, flips), 0]]


def on_device(swaps, tracer, source, exp_a, exp_b, imp_a, imp_b, col_index, block_count, send_list, wet_rows, month_day):
    tracers, points = tracer.shape
    row_blocks, slots = col_index.shape
    block = points // row_blocks
    half = jnp.bfloat16
    smem = pl.BlockSpec(memory_space=pltpu.SMEM)
    vmem = pl.BlockSpec(memory_space=pltpu.VMEM)
    piece = jax.ShapeDtypeStruct((tracers, block), half)
    params = pltpu.CompilerParams(vmem_limit_bytes=40 * 1024 * 1024)

    outgoing = pl.pallas_call(
        first_kernel,
        out_shape=[piece] * DIRECTIONS,
        in_specs=[pl.BlockSpec(memory_space=pl.ANY), smem, smem],
        out_specs=[vmem] * DIRECTIONS,
        scratch_shapes=[
            pltpu.VMEM((DIRECTIONS, tracers, block), jnp.float32),
            pltpu.SemaphoreType.DMA((DIRECTIONS,)),
        ],
        compiler_params=params,
        name="first_outgoing",
    )(tracer, send_list, wet_rows)

    def blend(a, b, step):
        return pl.pallas_call(
            functools.partial(blend_kernel, step),
            out_shape=jax.ShapeDtypeStruct((row_blocks, block, slots * block), half),
            in_specs=[vmem, vmem, smem],
            out_specs=vmem,
            compiler_params=params,
            name="blend",
        )(a, b, month_day)

    def apply(field, halos, matrix, first, explicit, last):
        operands = [col_index, block_count, send_list, wet_rows, field, matrix, *halos]
        specs = [smem] * 4 + [vmem] * (2 + DIRECTIONS)
        if explicit:
            operands.append(source)
            specs.append(vmem)
        if last:
            shapes = [jax.ShapeDtypeStruct((tracers, points), jnp.float32)]
        else:
            shapes = [jax.ShapeDtypeStruct((row_blocks, tracers, block), half)] + [piece] * DIRECTIONS
        return pl.pallas_call(
            functools.partial(apply_kernel, first, explicit, last),
            out_shape=shapes,
            in_specs=specs,
            out_specs=[vmem] * len(shapes),
            scratch_shapes=[
                pltpu.VMEM((row_blocks + DIRECTIONS + 1, tracers, block), half),
                pltpu.VMEM((row_blocks, tracers, slots * block), half),
            ],
            compiler_params=params,
            name="apply",
        )(*operands)

    def exchange(pieces):
        return [lax.ppermute(p, ("groups", "rows"), s) for p, s in zip(pieces, swaps)]

    field = tracer
    for step in range(STEPS):
        for explicit in (True, False):
            matrix = blend(exp_a, exp_b, step) if explicit else blend(imp_a, imp_b, step)
            last = step == STEPS - 1 and not explicit
            halos = exchange(outgoing)
            field, *outgoing = apply(field, halos, matrix, step == 0 and explicit, explicit, last)
    return field


def solution(mesh):
    count, groups = mesh.shape["rows"], mesh.shape["groups"]
    swaps = [swap_pairs(count, groups, stride, parity) for stride in (1, STRIDE) for parity in (0, 1)]
    wide = P("groups", "rows")
    rows = P("rows")
    return jax.shard_map(
        functools.partial(on_device, swaps),
        mesh=mesh,
        in_specs=(wide, wide, rows, rows, rows, rows, rows, rows, rows, rows, P()),
        out_specs=wide,
        check_vma=False,
    )
```

time: 80.9 us -> 36.8 us (0.45)
  the two profiles are of different devices: /device:TPU:1 before, /device:TPU:0 now
where the time goes in v1:
time: 36.8 us; the launch traced here: 36.6 us
  starting transfers between devices  15.2 us (41%)
  Pallas kernels  12.7 us (35%)
  local copies, waits for them, and re-layouts  6.22 us (17%)
  waiting for transfers between devices  2.15 us (6%)
    ppermute x16, starting transfers between devices, exchange(): lax.ppermute(p, ('groups', 'rows'), s)  15.2 us
    pallas_call x4, Pallas kernels, apply(): pl.pallas_call(functools.partial(apply_kernel, first, explicit, last), ou...  6.49 us
    unnamed x29, local copies, waits for them, and re-layouts  6.22 us
    pallas_call x4, Pallas kernels, blend(): pl.pallas_call(functools.partial(blend_kernel, step), out_shape=jax.Shape...  5.57 us
    ppermute x16, waiting for transfers between devices, exchange(): lax.ppermute(p, ('groups', 'rows'), s)  2.15 us
  transfers between devices with their start and end apart: 16, of which 3 were waited for; matrix products, arithmetic and copies ran while one was open for 0% of the time, Pallas kernels for 15%

profile of v1, /device:TPU:0, one launch (start us, length us, event | category | flops | bytes accessed | tf_op | source)
XLA Modules:
  0.0 36.6 jit_solution(202585285143390526)
XLA Ops:
  0.0 0.7 %copy.16.send_ref.refs_2_ = s32[1,4,1]{2,1,0:T(4,128)S(1)} copy(s32[1,4,1]{1,2,0:T(1,128)} %param.19) | data formatting | bytes 32 | tf_op args[8]
  0.7 0.0 copy-start.6
  0.7 0.9 %copy-done.6 = f32[64,1024]{1,0:T(8,128)S(1)} copy-done((f32[64,1024]{1,0:T(8,128)S(1)}, f32[64,1024]{1,0:T(8,128)}, u32[]{:S(2)}) %copy-start.6) | copy-done | bytes 262168
  1.7 0.7 %copy-done.10 = s32[8]{0:T(128)S(1)} copy-done((s32[8]{0:T(128)S(1)}, s32[8]{0:T(128)}, u32[]{:S(2)}) %copy-start.10) | copy-done | bytes 56
  2.3 0.7 %first_outgoing.1 = (bf16[64,128]{1,0:T(8,128)(2,1)S(1)}, bf16[64,128]{1,0:T(8,128)(2,1)S(1)}, bf16[64,128]{1,0:T(8,128)(2,1)S(1)}, bf16[64,128]{1,0:T(8,128)(2,1)S(1)}) custom-call(f32[64,1024]{1,0:T(8,128)S(1)} %copy-done.6, s32[1,4,1]{2,1,0:T(4,128)S(1)} %copy.16.send_ref.refs_2_, s32[8]{0:T(128)S(1)} %copy-done.10), custom_call_target="tpu_custom_call" | custom-call | tf_op jit(solution)/shard_map/first_outgoing/pallas_call | solution.py:134
  3.0 0.5 %collective-permute-start = (bf16[64,128]{1,0:T(8,128)(2,1)S(1)}, bf16[64,128]{1,0:T(8,128)(2,1)S(1)}, u32[]{:S(2)}, u32[]{:S(2)}) collective-permute-start(bf16[64,128]{1,0:T(8,128)(2,1)S(1)} %get-tuple-element.24), channel_id=1, source_target_pairs={{0,1},{1,0},{2,3},{3,2},{4,5},{5,4},{6,7},{7,6},{8,9},{9,8},{10,11... | collective-permute-start | bytes 49160 | tf_op jit(solution)/shard_map/ppermute | solution.py:181
  3.6 2.6 %collective-permute-start.1 = (bf16[64,128]{1,0:T(8,128)(2,1)S(1)}, bf16[64,128]{1,0:T(8,128)(2,1)S(1)}, u32[]{:S(2)}, u32[]{:S(2)}) collective-permute-start(bf16[64,128]{1,0:T(8,128)(2,1)S(1)} %get-tuple-element.25), channel_id=1, source_target_pairs={{0,16},{1,2},{2,1},{3,4},{4,3},{5,6},{6,5},{7,8},{8,7},{9,10},{10,... | collective-permute-start | bytes 49160 | tf_op jit(solution)/shard_map/ppermute | solution.py:181
  6.1 1.5 %collective-permute-start.2 = (bf16[64,128]{1,0:T(8,128)(2,1)S(1)}, bf16[64,128]{1,0:T(8,128)(2,1)S(1)}, u32[]{:S(2)}, u32[]{:S(2)}) collective-permute-start(bf16[64,128]{1,0:T(8,128)(2,1)S(1)} %get-tuple-element.26), channel_id=1, source_target_pairs={{0,4},{1,5},{2,6},{3,7},{4,0},{5,1},{6,2},{7,3},{8,12},{9,13},{10,... | collective-permute-start | bytes 49160 | tf_op jit(solution)/shard_map/ppermute | solution.py:181
  7.7 0.0 collective-permute-start.3
  7.7 0.0 copy-start
  7.7 1.6 %copy-done = bf16[8,8,128,128]{3,2,1,0:T(8,128)(2,1)S(1)} copy-done((bf16[8,8,128,128]{3,2,1,0:T(8,128)(2,1)S(1)}, bf16[8,8,128,128]{3,2,1,0:T(8,128)(2,1)}, u32[]{:S(2)}) %copy-start) | copy-done | bytes 2097176
  9.2 0.0 copy-start.2
  9.2 1.6 %copy-done.2 = bf16[8,8,128,128]{3,2,1,0:T(8,128)(2,1)S(1)} copy-done((bf16[8,8,128,128]{3,2,1,0:T(8,128)(2,1)S(1)}, bf16[8,8,128,128]{3,2,1,0:T(8,128)(2,1)}, u32[]{:S(2)}) %copy-start.2) | copy-done | bytes 2097176
  10.8 0.0 copy-start.12
  10.8 0.7 %copy-done.12 = s32[2]{0:T(128)S(1)} copy-done((s32[2]{0:T(128)S(1)}, s32[2]{0:T(128)}, u32[]{:S(2)}) %copy-start.12) | copy-done | bytes 32
  11.5 0.0 copy-start.13
  11.5 0.0 copy-start.5
  11.5 1.4 %blend.4.refs_5_ = bf16[8,128,1024]{2,1,0:T(8,128)(2,1)S(1)} custom-call(bf16[8,8,128,128]{3,2,1,0:T(8,128)(2,1)S(1)} %copy-done, bf16[8,8,128,128]{3,2,1,0:T(8,128)(2,1)S(1)} %copy-done.2, s32[2]{0:T(128)S(1)} %copy-done.12), custom_call_target="tpu_custom_call" | custom-call | tf_op jit(solution)/shard_map/blend/pallas_call | solution.py:148
  12.9 0.0 copy-start.4
  12.9 0.0 collective-permute-done.refs_6_
  13.0 0.0 collective-permute-done.1.refs_7_
  13.0 0.0 collective-permute-done.2.refs_8_
  13.0 0.0 collective-permute-done.3.refs_9_
  13.0 0.0 copy-done.7
  13.0 0.0 copy-done.8
  13.0 0.0 copy-done.9
  13.0 0.0 copy-done.11
  13.0 0.0 copy-done.13
  13.0 1.4 %apply.4 = (bf16[8,64,128]{2,1,0:T(8,128)(2,1)S(1)}, bf16[64,128]{1,0:T(8,128)(2,1)S(1)}, bf16[64,128]{1,0:T(8,128)(2,1)S(1)}, bf16[64,128]{1,0:T(8,128)(2,1)S(1)}, bf16[64,128]{1,0:T(8,128)(2,1)S(1)}) custom-call(s32[8,8]{1,0:T(8,128)S(1)} %copy-done.9, s32[8]{0:T(128)S(1)} %copy-done.13, s32[1,4,1]{2,1,0:T(4,128)S(1)} %copy.16.send_ref.refs_2_, ...), custom_call_target="tpu_custom_call" | custom-call | tf_op jit(solution)/shard_map/apply/pallas_call | solution.py:167
  14.5 0.6 %collective-permute-start.4 = (bf16[64,128]{1,0:T(8,128)(2,1)S(1)}, bf16[64,128]{1,0:T(8,128)(2,1)S(1)}, u32[]{:S(2)}, u32[]{:S(2)}) collective-permute-start(bf16[64,128]{1,0:T(8,128)(2,1)S(1)} %get-tuple-element.29), channel_id=1, source_target_pairs={{0,1},{1,0},{2,3},{3,2},{4,5},{5,4},{6,7},{7,6},{8,9},{9,8},{10,11... | collective-permute-start | bytes 49160 | tf_op jit(solution)/shard_map/ppermute | solution.py:181
  15.0 1.5 %collective-permute-start.5 = (bf16[64,128]{1,0:T(8,128)(2,1)S(1)}, bf16[64,128]{1,0:T(8,128)(2,1)S(1)}, u32[]{:S(2)}, u32[]{:S(2)}) collective-permute-start(bf16[64,128]{1,0:T(8,128)(2,1)S(1)} %get-tuple-element.30), channel_id=1, source_target_pairs={{0,16},{1,2},{2,1},{3,4},{4,3},{5,6},{6,5},{7,8},{8,7},{9,10},{10,... | collective-permute-start | bytes 49160 | tf_op jit(solution)/shard_map/ppermute | solution.py:181
  16.5 1.3 %collective-permute-start.6 = (bf16[64,128]{1,0:T(8,128)(2,1)S(1)}, bf16[64,128]{1,0:T(8,128)(2,1)S(1)}, u32[]{:S(2)}, u32[]{:S(2)}) collective-permute-start(bf16[64,128]{1,0:T(8,128)(2,1)S(1)} %get-tuple-element.31), channel_id=1, source_target_pairs={{0,4},{1,5},{2,6},{3,7},{4,0},{5,1},{6,2},{7,3},{8,12},{9,13},{10,... | collective-permute-start | bytes 49160 | tf_op jit(solution)/shard_map/ppermute | solution.py:181
  17.8 0.8 %collective-permute-start.7 = (bf16[64,128]{1,0:T(8,128)(2,1)S(1)}, bf16[64,128]{1,0:T(8,128)(2,1)S(1)}, u32[]{:S(2)}, u32[]{:S(2)}) collective-permute-start(bf16[64,128]{1,0:T(8,128)(2,1)S(1)} %get-tuple-element.32), channel_id=1, source_target_pairs={{0,1},{1,0},{2,3},{3,2},{4,8},{5,9},{6,10},{7,11},{8,4},{9,5},{10,... | collective-permute-start | bytes 49160 | tf_op jit(solution)/shard_map/ppermute | solution.py:181
  18.7 0.0 copy-done.5
  18.7 0.0 copy-done.4
  18.7 1.4 %blend.5.refs_5_ = bf16[8,128,1024]{2,1,0:T(8,128)(2,1)S(1)} custom-call(bf16[8,8,128,128]{3,2,1,0:T(8,128)(2,1)S(1)} %copy-done.4, bf16[8,8,128,128]{3,2,1,0:T(8,128)(2,1)S(1)} %copy-done.5, s32[2]{0:T(128)S(1)} %copy-done.12), custom_call_target="tpu_custom_call" | custom-call | tf_op jit(solution)/shard_map/blend/pallas_call | solution.py:148
  20.1 0.0 copy-start.1
  20.1 0.0 collective-permute-done.4.refs_6_
  20.1 0.0 collective-permute-done.5.refs_7_
  20.1 0.2 collective-permute-done.6.refs_8_
  20.3 0.0 collective-permute-done.7.refs_9_
  20.3 1.5 %apply.5 = (bf16[8,64,128]{2,1,0:T(8,128)(2,1)S(1)}, bf16[64,128]{1,0:T(8,128)(2,1)S(1)}, bf16[64,128]{1,0:T(8,128)(2,1)S(1)}, bf16[64,128]{1,0:T(8,128)(2,1)S(1)}, bf16[64,128]{1,0:T(8,128)(2,1)S(1)}) custom-call(s32[8,8]{1,0:T(8,128)S(1)} %copy-done.9, s32[8]{0:T(128)S(1)} %copy-done.13, s32[1,4,1]{2,1,0:T(4,128)S(1)} %copy.16.send_ref.refs_2_, ...), custom_call_target="tpu_custom_call" | custom-call | tf_op jit(solution)/shard_map/apply/pallas_call | solution.py:167
  21.7 2.1 %collective-permute-start.10 = (bf16[64,128]{1,0:T(8,128)(2,1)S(1)}, bf16[64,128]{1,0:T(8,128)(2,1)S(1)}, u32[]{:S(2)}, u32[]{:S(2)}) collective-permute-start(bf16[64,128]{1,0:T(8,128)(2,1)S(1)} %get-tuple-element.36), channel_id=1, source_target_pairs={{0,4},{1,5},{2,6},{3,7},{4,0},{5,1},{6,2},{7,3},{8,12},{9,13},{10,... | collective-permute-start | bytes 49160 | tf_op jit(solution)/shard_map/ppermute | solution.py:181
  23.8 0.0 collective-permute-start.11
  23.8 0.5 %collective-permute-start.8 = (bf16[64,128]{1,0:T(8,128)(2,1)S(1)}, bf16[64,128]{1,0:T(8,128)(2,1)S(1)}, u32[]{:S(2)}, u32[]{:S(2)}) collective-permute-start(bf16[64,128]{1,0:T(8,128)(2,1)S(1)} %get-tuple-element.34), channel_id=1, source_target_pairs={{0,1},{1,0},{2,3},{3,2},{4,5},{5,4},{6,7},{7,6},{8,9},{9,8},{10,11... | collective-permute-start | bytes 49160 | tf_op jit(solution)/shard_map/ppermute | solution.py:181
  24.3 1.0 %collective-permute-start.9 = (bf16[64,128]{1,0:T(8,128)(2,1)S(1)}, bf16[64,128]{1,0:T(8,128)(2,1)S(1)}, u32[]{:S(2)}, u32[]{:S(2)}) collective-permute-start(bf16[64,128]{1,0:T(8,128)(2,1)S(1)} %get-tuple-element.35), channel_id=1, source_target_pairs={{0,16},{1,2},{2,1},{3,4},{4,3},{5,6},{6,5},{7,8},{8,7},{9,10},{10,... | collective-permute-start | bytes 49160 | tf_op jit(solution)/shard_map/ppermute | solution.py:181
  25.4 0.0 copy-done.3
  25.4 0.0 copy-done.1
  25.4 1.4 %blend.6.refs_5_ = bf16[8,128,1024]{2,1,0:T(8,128)(2,1)S(1)} custom-call(bf16[8,8,128,128]{3,2,1,0:T(8,128)(2,1)S(1)} %copy-done.1, bf16[8,8,128,128]{3,2,1,0:T(8,128)(2,1)S(1)} %copy-done.3, s32[2]{0:T(128)S(1)} %copy-done.12), custom_call_target="tpu_custom_call" | custom-call | tf_op jit(solution)/shard_map/blend/pallas_call | solution.py:148
  26.8 0.0 collective-permute-done.10.refs_8_
  26.8 0.0 collective-permute-done.11.refs_9_
  26.8 0.0 collective-permute-done.8.refs_6_
  26.8 1.3 %collective-permute-done.9.refs_7_ = bf16[64,128]{1,0:T(8,128)(2,1)S(1)} collective-permute-done((bf16[64,128]{1,0:T(8,128)(2,1)S(1)}, bf16[64,128]{1,0:T(8,128)(2,1)S(1)}, u32[]{:S(2)}, u32[]{:S(2)}) %collective-permute-start.9) | collective-permute-done | bytes 16416 | tf_op jit(solution)/shard_map/ppermute | solution.py:181
  28.1 1.5 %apply.6 = (bf16[8,64,128]{2,1,0:T(8,128)(2,1)S(1)}, bf16[64,128]{1,0:T(8,128)(2,1)S(1)}, bf16[64,128]{1,0:T(8,128)(2,1)S(1)}, bf16[64,128]{1,0:T(8,128)(2,1)S(1)}, bf16[64,128]{1,0:T(8,128)(2,1)S(1)}) custom-call(s32[8,8]{1,0:T(8,128)S(1)} %copy-done.9, s32[8]{0:T(128)S(1)} %copy-done.13, s32[1,4,1]{2,1,0:T(4,128)S(1)} %copy.16.send_ref.refs_2_, ...), custom_call_target="tpu_custom_call" | custom-call | tf_op jit(solution)/shard_map/apply/pallas_call | solution.py:167
  29.6 0.1 collective-permute-start.12
  29.6 1.1 %collective-permute-start.13 = (bf16[64,128]{1,0:T(8,128)(2,1)S(1)}, bf16[64,128]{1,0:T(8,128)(2,1)S(1)}, u32[]{:S(2)}, u32[]{:S(2)}) collective-permute-start(bf16[64,128]{1,0:T(8,128)(2,1)S(1)} %get-tuple-element.40), channel_id=1, source_target_pairs={{0,16},{1,2},{2,1},{3,4},{4,3},{5,6},{6,5},{7,8},{8,7},{9,10},{10,... | collective-permute-start | bytes 49160 | tf_op jit(solution)/shard_map/ppermute | solution.py:181
  30.7 1.6 %collective-permute-start.14 = (bf16[64,128]{1,0:T(8,128)(2,1)S(1)}, bf16[64,128]{1,0:T(8,128)(2,1)S(1)}, u32[]{:S(2)}, u32[]{:S(2)}) collective-permute-start(bf16[64,128]{1,0:T(8,128)(2,1)S(1)} %get-tuple-element.41), channel_id=1, source_target_pairs={{0,4},{1,5},{2,6},{3,7},{4,0},{5,1},{6,2},{7,3},{8,12},{9,13},{10,... | collective-permute-start | bytes 49160 | tf_op jit(solution)/shard_map/ppermute | solution.py:181
  32.4 0.0 collective-permute-start.15
  32.4 1.4 %blend.7.refs_5_ = bf16[8,128,1024]{2,1,0:T(8,128)(2,1)S(1)} custom-call(bf16[8,8,128,128]{3,2,1,0:T(8,128)(2,1)S(1)} %copy-done.4, bf16[8,8,128,128]{3,2,1,0:T(8,128)(2,1)S(1)} %copy-done.5, s32[2]{0:T(128)S(1)} %copy-done.12), custom_call_target="tpu_custom_call" | custom-call | tf_op jit(solution)/shard_map/blend/pallas_call | solution.py:148
  33.8 0.0 collective-permute-done.12.refs_6_
  33.8 0.0 collective-permute-done.13.refs_7_
  33.8 0.7 %collective-permute-done.14.refs_8_ = bf16[64,128]{1,0:T(8,128)(2,1)S(1)} collective-permute-done((bf16[64,128]{1,0:T(8,128)(2,1)S(1)}, bf16[64,128]{1,0:T(8,128)(2,1)S(1)}, u32[]{:S(2)}, u32[]{:S(2)}) %collective-permute-start.14) | collective-permute-done | bytes 16416 | tf_op jit(solution)/shard_map/ppermute | solution.py:181
  34.5 0.0 collective-permute-done.15.refs_9_
  34.5 2.1 %apply.7 = f32[64,1024]{1,0:T(8,128)} custom-call(s32[8,8]{1,0:T(8,128)S(1)} %copy-done.9, s32[8]{0:T(128)S(1)} %copy-done.13, s32[1,4,1]{2,1,0:T(4,128)S(1)} %copy.16.send_ref.refs_2_, s32[8]{0:T(128)S(1)} %copy-done.11, bf16[8,64,128]{2,1,0:T(8,128)(2,1)S(1)} %get-tuple-element.38.refs_4_, bf16[8,128,1024]{2,1,0:T(8,128)(2,1)S(1)} %blend.7.refs_5_, ...), custom_call_target="tpu_custom_call" | custom-call | tf_op jit(solution)/shard_map/apply/pallas_call | solution.py:167
  (6 shorter events, 0.0 us)
Async XLA Ops:
  0.7 0.9 %copy-start.6 = (f32[64,1024]{1,0:T(8,128)S(1)}, f32[64,1024]{1,0:T(8,128)}, u32[]{:S(2)}) copy-start(f32[64,1024]{1,0:T(8,128)} %refs_4_.1) | copy-start | bytes 786436
  1.7 0.7 %copy-start.10 = (s32[8]{0:T(128)S(1)}, s32[8]{0:T(128)}, u32[]{:S(2)}) copy-start(s32[8]{0:T(128)} %refs_3_.7) | copy-start | bytes 100
  3.0 9.9 %collective-permute-start = (bf16[64,128]{1,0:T(8,128)(2,1)S(1)}, bf16[64,128]{1,0:T(8,128)(2,1)S(1)}, u32[]{:S(2)}, u32[]{:S(2)}) collective-permute-start(bf16[64,128]{1,0:T(8,128)(2,1)S(1)} %get-tuple-element.24), channel_id=1, source_target_pairs={{0,1},{1,0},{2,3},{3,2},{4,5},{5,4},{6,7},{7,6},{8,9},{9,8},{10,11... | collective-permute-start | bytes 49160 | tf_op jit(solution)/shard_map/ppermute | solution.py:181
  3.6 9.4 %collective-permute-start.1 = (bf16[64,128]{1,0:T(8,128)(2,1)S(1)}, bf16[64,128]{1,0:T(8,128)(2,1)S(1)}, u32[]{:S(2)}, u32[]{:S(2)}) collective-permute-start(bf16[64,128]{1,0:T(8,128)(2,1)S(1)} %get-tuple-element.25), channel_id=1, source_target_pairs={{0,16},{1,2},{2,1},{3,4},{4,3},{5,6},{6,5},{7,8},{8,7},{9,10},{10,... | collective-permute-start | bytes 49160 | tf_op jit(solution)/shard_map/ppermute | solution.py:181
  6.1 6.8 %collective-permute-start.2 = (bf16[64,128]{1,0:T(8,128)(2,1)S(1)}, bf16[64,128]{1,0:T(8,128)(2,1)S(1)}, u32[]{:S(2)}, u32[]{:S(2)}) collective-permute-start(bf16[64,128]{1,0:T(8,128)(2,1)S(1)} %get-tuple-element.26), channel_id=1, source_target_pairs={{0,4},{1,5},{2,6},{3,7},{4,0},{5,1},{6,2},{7,3},{8,12},{9,13},{10,... | collective-permute-start | bytes 49160 | tf_op jit(solution)/shard_map/ppermute | solution.py:181
  7.7 5.3 %collective-permute-start.3 = (bf16[64,128]{1,0:T(8,128)(2,1)S(1)}, bf16[64,128]{1,0:T(8,128)(2,1)S(1)}, u32[]{:S(2)}, u32[]{:S(2)}) collective-permute-start(bf16[64,128]{1,0:T(8,128)(2,1)S(1)} %get-tuple-element.27), channel_id=1, source_target_pairs={{0,1},{1,0},{2,3},{3,2},{4,8},{5,9},{6,10},{7,11},{8,4},{9,5},{10,... | collective-permute-start | bytes 49160 | tf_op jit(solution)/shard_map/ppermute | solution.py:181
  7.7 1.6 %copy-start = (bf16[8,8,128,128]{3,2,1,0:T(8,128)(2,1)S(1)}, bf16[8,8,128,128]{3,2,1,0:T(8,128)(2,1)}, u32[]{:S(2)}) copy-start(bf16[8,8,128,128]{3,2,1,0:T(8,128)(2,1)} %a_ref.6) | copy-start | bytes 6291460
  9.2 1.6 %copy-start.2 = (bf16[8,8,128,128]{3,2,1,0:T(8,128)(2,1)S(1)}, bf16[8,8,128,128]{3,2,1,0:T(8,128)(2,1)}, u32[]{:S(2)}) copy-start(bf16[8,8,128,128]{3,2,1,0:T(8,128)(2,1)} %b_ref.6) | copy-start | bytes 6291460
  10.8 0.7 %copy-start.12 = (s32[2]{0:T(128)S(1)}, s32[2]{0:T(128)}, u32[]{:S(2)}) copy-start(s32[2]{0:T(128)} %day_ref.7) | copy-start | bytes 28
  11.5 1.5 %copy-start.7 = (f32[64,1024]{1,0:T(8,128)S(1)}, f32[64,1024]{1,0:T(8,128)}, u32[]{:S(2)}) copy-start(f32[64,1024]{1,0:T(8,128)} %refs_4_.1) | copy-start | bytes 786436
  11.5 1.5 %copy-start.8 = (f32[64,1024]{1,0:T(8,128)S(1)}, f32[64,1024]{1,0:T(8,128)}, u32[]{:S(2)}) copy-start(f32[64,1024]{1,0:T(8,128)} %refs_10_.3) | copy-start | bytes 786436
  11.5 1.5 %copy-start.9 = (s32[8,8]{1,0:T(8,128)S(1)}, s32[8,8]{1,0:T(8,128)}, u32[]{:S(2)}) copy-start(s32[8,8]{1,0:T(8,128)} %refs_0_.7) | copy-start | bytes 772
  11.5 1.5 %copy-start.11 = (s32[8]{0:T(128)S(1)}, s32[8]{0:T(128)}, u32[]{:S(2)}) copy-start(s32[8]{0:T(128)} %refs_3_.7) | copy-start | bytes 100
  11.5 1.5 %copy-start.13 = (s32[8]{0:T(128)S(1)}, s32[8]{0:T(128)}, u32[]{:S(2)}) copy-start(s32[8]{0:T(128)} %refs_1_.7) | copy-start | bytes 100
  11.5 7.2 %copy-start.5 = (bf16[8,8,128,128]{3,2,1,0:T(8,128)(2,1)S(1)}, bf16[8,8,128,128]{3,2,1,0:T(8,128)(2,1)}, u32[]{:S(2)}) copy-start(bf16[8,8,128,128]{3,2,1,0:T(8,128)(2,1)} %b_ref.7) | copy-start | bytes 6291460
  12.9 5.8 %copy-start.4 = (bf16[8,8,128,128]{3,2,1,0:T(8,128)(2,1)S(1)}, bf16[8,8,128,128]{3,2,1,0:T(8,128)(2,1)}, u32[]{:S(2)}) copy-start(bf16[8,8,128,128]{3,2,1,0:T(8,128)(2,1)} %a_ref.7) | copy-start | bytes 6291460
  14.5 5.6 %collective-permute-start.4 = (bf16[64,128]{1,0:T(8,128)(2,1)S(1)}, bf16[64,128]{1,0:T(8,128)(2,1)S(1)}, u32[]{:S(2)}, u32[]{:S(2)}) collective-permute-start(bf16[64,128]{1,0:T(8,128)(2,1)S(1)} %get-tuple-element.29), channel_id=1, source_target_pairs={{0,1},{1,0},{2,3},{3,2},{4,5},{5,4},{6,7},{7,6},{8,9},{9,8},{10,11... | collective-permute-start | bytes 49160 | tf_op jit(solution)/shard_map/ppermute | solution.py:181
  15.0 5.1 %collective-permute-start.5 = (bf16[64,128]{1,0:T(8,128)(2,1)S(1)}, bf16[64,128]{1,0:T(8,128)(2,1)S(1)}, u32[]{:S(2)}, u32[]{:S(2)}) collective-permute-start(bf16[64,128]{1,0:T(8,128)(2,1)S(1)} %get-tuple-element.30), channel_id=1, source_target_pairs={{0,16},{1,2},{2,1},{3,4},{4,3},{5,6},{6,5},{7,8},{8,7},{9,10},{10,... | collective-permute-start | bytes 49160 | tf_op jit(solution)/shard_map/ppermute | solution.py:181
  16.5 3.7 %collective-permute-start.6 = (bf16[64,128]{1,0:T(8,128)(2,1)S(1)}, bf16[64,128]{1,0:T(8,128)(2,1)S(1)}, u32[]{:S(2)}, u32[]{:S(2)}) collective-permute-start(bf16[64,128]{1,0:T(8,128)(2,1)S(1)} %get-tuple-element.31), channel_id=1, source_target_pairs={{0,4},{1,5},{2,6},{3,7},{4,0},{5,1},{6,2},{7,3},{8,12},{9,13},{10,... | collective-permute-start | bytes 49160 | tf_op jit(solution)/shard_map/ppermute | solution.py:181
  17.8 2.4 %collective-permute-start.7 = (bf16[64,128]{1,0:T(8,128)(2,1)S(1)}, bf16[64,128]{1,0:T(8,128)(2,1)S(1)}, u32[]{:S(2)}, u32[]{:S(2)}) collective-permute-start(bf16[64,128]{1,0:T(8,128)(2,1)S(1)} %get-tuple-element.32), channel_id=1, source_target_pairs={{0,1},{1,0},{2,3},{3,2},{4,8},{5,9},{6,10},{7,11},{8,4},{9,5},{10,... | collective-permute-start | bytes 49160 | tf_op jit(solution)/shard_map/ppermute | solution.py:181
  18.7 6.7 %copy-start.3 = (bf16[8,8,128,128]{3,2,1,0:T(8,128)(2,1)S(1)}, bf16[8,8,128,128]{3,2,1,0:T(8,128)(2,1)}, u32[]{:S(2)}) copy-start(bf16[8,8,128,128]{3,2,1,0:T(8,128)(2,1)} %b_ref.6) | copy-start | bytes 6291460
  20.1 5.3 %copy-start.1 = (bf16[8,8,128,128]{3,2,1,0:T(8,128)(2,1)S(1)}, bf16[8,8,128,128]{3,2,1,0:T(8,128)(2,1)}, u32[]{:S(2)}) copy-start(bf16[8,8,128,128]{3,2,1,0:T(8,128)(2,1)} %a_ref.6) | copy-start | bytes 6291460
  21.7 5.0 %collective-permute-start.10 = (bf16[64,128]{1,0:T(8,128)(2,1)S(1)}, bf16[64,128]{1,0:T(8,128)(2,1)S(1)}, u32[]{:S(2)}, u32[]{:S(2)}) collective-permute-start(bf16[64,128]{1,0:T(8,128)(2,1)S(1)} %get-tuple-element.36), channel_id=1, source_target_pairs={{0,4},{1,5},{2,6},{3,7},{4,0},{5,1},{6,2},{7,3},{8,12},{9,13},{10,... | collective-permute-start | bytes 49160 | tf_op jit(solution)/shard_map/ppermute | solution.py:181
  23.8 3.0 %collective-permute-start.11 = (bf16[64,128]{1,0:T(8,128)(2,1)S(1)}, bf16[64,128]{1,0:T(8,128)(2,1)S(1)}, u32[]{:S(2)}, u32[]{:S(2)}) collective-permute-start(bf16[64,128]{1,0:T(8,128)(2,1)S(1)} %get-tuple-element.37), channel_id=1, source_target_pairs={{0,1},{1,0},{2,3},{3,2},{4,8},{5,9},{6,10},{7,11},{8,4},{9,5},{10,... | collective-permute-start | bytes 49160 | tf_op jit(solution)/shard_map/ppermute | solution.py:181
  23.8 3.0 %collective-permute-start.8 = (bf16[64,128]{1,0:T(8,128)(2,1)S(1)}, bf16[64,128]{1,0:T(8,128)(2,1)S(1)}, u32[]{:S(2)}, u32[]{:S(2)}) collective-permute-start(bf16[64,128]{1,0:T(8,128)(2,1)S(1)} %get-tuple-element.34), channel_id=1, source_target_pairs={{0,1},{1,0},{2,3},{3,2},{4,5},{5,4},{6,7},{7,6},{8,9},{9,8},{10,11... | collective-permute-start | bytes 49160 | tf_op jit(solution)/shard_map/ppermute | solution.py:181
  24.3 3.7 %collective-permute-start.9 = (bf16[64,128]{1,0:T(8,128)(2,1)S(1)}, bf16[64,128]{1,0:T(8,128)(2,1)S(1)}, u32[]{:S(2)}, u32[]{:S(2)}) collective-permute-start(bf16[64,128]{1,0:T(8,128)(2,1)S(1)} %get-tuple-element.35), channel_id=1, source_target_pairs={{0,16},{1,2},{2,1},{3,4},{4,3},{5,6},{6,5},{7,8},{8,7},{9,10},{10,... | collective-permute-start | bytes 49160 | tf_op jit(solution)/shard_map/ppermute | solution.py:181
  29.6 4.2 %collective-permute-start.12 = (bf16[64,128]{1,0:T(8,128)(2,1)S(1)}, bf16[64,128]{1,0:T(8,128)(2,1)S(1)}, u32[]{:S(2)}, u32[]{:S(2)}) collective-permute-start(bf16[64,128]{1,0:T(8,128)(2,1)S(1)} %get-tuple-element.39), channel_id=1, source_target_pairs={{0,1},{1,0},{2,3},{3,2},{4,5},{5,4},{6,7},{7,6},{8,9},{9,8},{10,11... | collective-permute-start | bytes 49160 | tf_op jit(solution)/shard_map/ppermute | solution.py:181
  29.6 4.1 %collective-permute-start.13 = (bf16[64,128]{1,0:T(8,128)(2,1)S(1)}, bf16[64,128]{1,0:T(8,128)(2,1)S(1)}, u32[]{:S(2)}, u32[]{:S(2)}) collective-permute-start(bf16[64,128]{1,0:T(8,128)(2,1)S(1)} %get-tuple-element.40), channel_id=1, source_target_pairs={{0,16},{1,2},{2,1},{3,4},{4,3},{5,6},{6,5},{7,8},{8,7},{9,10},{10,... | collective-permute-start | bytes 49160 | tf_op jit(solution)/shard_map/ppermute | solution.py:181
  30.7 3.7 %collective-permute-start.14 = (bf16[64,128]{1,0:T(8,128)(2,1)S(1)}, bf16[64,128]{1,0:T(8,128)(2,1)S(1)}, u32[]{:S(2)}, u32[]{:S(2)}) collective-permute-start(bf16[64,128]{1,0:T(8,128)(2,1)S(1)} %get-tuple-element.41), channel_id=1, source_target_pairs={{0,4},{1,5},{2,6},{3,7},{4,0},{5,1},{6,2},{7,3},{8,12},{9,13},{10,... | collective-permute-start | bytes 49160 | tf_op jit(solution)/shard_map/ppermute | solution.py:181
  32.4 2.1 %collective-permute-start.15 = (bf16[64,128]{1,0:T(8,128)(2,1)S(1)}, bf16[64,128]{1,0:T(8,128)(2,1)S(1)}, u32[]{:S(2)}, u32[]{:S(2)}) collective-permute-start(bf16[64,128]{1,0:T(8,128)(2,1)S(1)} %get-tuple-element.42), channel_id=1, source_target_pairs={{0,1},{1,0},{2,3},{3,2},{4,8},{5,9},{6,10},{7,11},{8,4},{9,5},{10,... | collective-permute-start | bytes 49160 | tf_op jit(solution)/shard_map/ppermute | solution.py:181

commit v2 on v1

v2 whole, which is shorter than its diff:
```python
import functools

import jax
import jax.numpy as jnp
from jax import lax
from jax.experimental import pallas as pl
from jax.experimental.pallas import tpu as pltpu
from jax.sharding import PartitionSpec as P

STEPS = 2
DAYS = 30
STRIDE = 4
DIRECTIONS = 4


def swap_pairs(count, groups, stride, parity):
    partner = {}
    for i in range(count - stride):
        if (i // stride) % 2 == parity:
            partner[i], partner[i + stride] = i + stride, i
    idle = [i for i in range(count) if i not in partner]
    for i in idle:
        if i ^ 1 in idle:
            partner[i] = i ^ 1
    pairs = []
    for g in range(groups):
        for i in range(count):
            if i in partner:
                pairs.append((g * count + i, g * count + partner[i]))
            else:
                other = g ^ 1 if g ^ 1 < groups else g
                pairs.append((g * count + i, other * count + i))
    return pairs


def my_flips():
    place = lax.axis_index("rows")
    return 1 - place % 2, 1 - (place // STRIDE) % 2


def direction_of(swap, flips):
    if swap < 2:
        return swap ^ 1 ^ flips[0]
    return 2 + ((swap - 2) ^ 1 ^ flips[1])


def place_of(slot, row_blocks, flips):
    j = slot - row_blocks
    return jnp.where(slot < row_blocks, slot, row_blocks + (j ^ jnp.where(j < 2, flips[0], flips[1])))


def start_all(copies):
    for copy in copies:
        copy.start()
    return copies


def prologue_kernel(tracer, wet, send, c_out, o_out, z_out, y_out, field, wet_mask, send_pick, raw, wet_s, send_s, sems):
    copies = start_all(
        [
            pltpu.make_async_copy(tracer, raw, sems.at[0]),
            pltpu.make_async_copy(wet, wet_s, sems.at[1]),
            pltpu.make_async_copy(send, send_s, sems.at[2]),
        ]
    )
    flips = my_flips()
    row_blocks = wet.shape[0]
    tracers, points = raw.shape
    block = points // row_blocks
    for copy in copies[::-1]:
        copy.wait()
    rows = [send_s[direction_of(n, flips)] for n in range(DIRECTIONS)]
    lane = lax.broadcasted_iota(jnp.int32, (tracers, block), 1)
    lane8 = lax.broadcasted_iota(jnp.int32, (wet_mask.shape[0], block), 1)
    for r in range(row_blocks):
        columns = pl.ds(r * block, block)
        field[:, columns] = jnp.where(lane < wet_s[r], raw[:, columns], 0.0).astype(field.dtype)
    for n, out in enumerate((c_out, o_out, z_out, y_out)):
        out[...] = field[:, pl.ds(pl.multiple_of(rows[n] * block, block), block)]
    for r in range(row_blocks):
        wet_mask[:, pl.ds(r * block, block)] = jnp.where(lane8 < wet_s[r], 1.0, 0.0)
    for n in range(DIRECTIONS):
        send_pick[n] = jnp.full(send_pick.shape[1:], rows[n], jnp.int32).astype(send_pick.dtype)


def blended(a, b, early, late):
    mixed = early * a.astype(jnp.float32) + late * b.astype(jnp.float32)
    return mixed.astype(a.dtype).T


def add_repeats(table, dense, pairs, block):
    def one(e, carry):
        row = table[pairs + 1 + e]
        columns = pl.ds(pl.multiple_of(row * block, block), block)
        source = pl.ds(pl.multiple_of(table[2 * pairs + 1 + e] * block, block), block)
        target = pl.ds(pl.multiple_of(table[3 * pairs + 1 + e] * block, block), block)
        dense[target, columns] = dense[target, columns] + dense[source, columns]
        return carry

    lax.fori_loop(0, table[pairs], one, 0)


def local_part(field, dense, source, partial):
    total = jnp.dot(field[...], dense[pl.ds(0, field.shape[1]), :], preferred_element_type=jnp.float32)
    partial[...] = total if source is None else total + source[...]


def ready_first_kernel(
    col, count, day, field, source, a, b,
    dense, partial, table_out, weights,
    a_v, b_v, source_v, col_s, count_s, day_s, table, sems,
):
    row_blocks, slots, block, _ = a.shape
    pairs = row_blocks * slots
    index_copies = start_all(
        [
            pltpu.make_async_copy(col, col_s, sems.at[0]),
            pltpu.make_async_copy(count, count_s, sems.at[1]),
            pltpu.make_async_copy(day, day_s, sems.at[2]),
        ]
    )
    month_copies = []
    for r in range(row_blocks):
        month_copies.append(
            start_all(
                [
                    pltpu.make_async_copy(a.at[r], a_v.at[r], sems.at[5 + r]),
                    pltpu.make_async_copy(b.at[r], b_v.at[r], sems.at[5 + row_blocks + r]),
                ]
            )
        )
    source_copy = start_all([pltpu.make_async_copy(source, source_v, sems.at[3])])[0]
    flips = my_flips()
    dense[...] = jnp.zeros(dense.shape, dense.dtype)
    for copy in index_copies:
        copy.wait()
    for step in range(STEPS):
        now = day_s[step]
        for n, days in enumerate((DAYS - now, now)):
            weights[2 * step + n] = jnp.full(weights.shape[1:], days.astype(jnp.float32) * (1.0 / DAYS), jnp.float32)
    unused = row_blocks + DIRECTIONS
    repeats = jnp.int32(0)
    places = {}
    for r in range(row_blocks):
        for k in range(slots):
            slot = col_s[r, k]
            used = k < count_s[r]
            again = jnp.bool_(False)
            for earlier in range(k):
                again = again | (col_s[r, earlier] == slot)
            again = again & used
            target = place_of(slot, row_blocks, flips)
            aside = unused + 1 + k
            place = jnp.where(used, jnp.where(again, aside, target), unused)
            places[r, k] = place
            table[r * slots + k] = place
            table[pairs + 1 + repeats] = jnp.int32(r)
            table[2 * pairs + 1 + repeats] = jnp.int32(aside)
            table[3 * pairs + 1 + repeats] = target
            repeats = repeats + again.astype(jnp.int32)
    table[pairs] = repeats
    table_copy = start_all([pltpu.make_async_copy(table, table_out, sems.at[4])])[0]
    early, late = weights[0, :1], weights[1, :1]
    for r in range(row_blocks):
        for copy in month_copies[r]:
            copy.wait()
        for k in range(slots):
            rows = pl.ds(pl.multiple_of(places[r, k] * block, block), block)
            dense[rows, pl.ds(r * block, block)] = blended(a_v[r, k], b_v[r, k], early, late)
    add_repeats(table, dense, pairs, block)
    source_copy.wait()
    local_part(field, dense, source_v, partial)
    table_copy.wait()


def ready_kernel(step, explicit, *refs):
    refs = list(refs)
    table_in, weights, field, a, b, _ = refs[:6]
    refs = refs[6:]
    source = refs.pop(0) if explicit else None
    dense, partial, stage, table, sem = refs
    row_blocks, slots, block, _ = a.shape
    pairs = row_blocks * slots
    table_copy = pltpu.make_async_copy(table_in, table, sem)
    table_copy.start()
    early, late = weights[2 * step, :1], weights[2 * step + 1, :1]
    staged = stage.shape[0]

    def rows_of(r, k):
        return pl.ds(pl.multiple_of(table[r * slots + k] * block, block), block)

    for r in range(staged):
        for k in range(slots):
            stage[r, k] = blended(a[r, k], b[r, k], early, late)
    table_copy.wait()
    for r in range(row_blocks):
        for k in range(slots):
            value = stage[r, k] if r < staged else blended(a[r, k], b[r, k], early, late)
            dense[rows_of(r, k), pl.ds(r * block, block)] = value
    add_repeats(table, dense, pairs, block)
    local_part(field, dense, source, partial)


def finish_kernel(last, partial, dense, wet_mask, send_pick, c_in, o_in, z_in, y_in, out, *refs):
    tracers, points = partial.shape
    block = c_in.shape[1]
    row_blocks = points // block
    halo = jnp.concatenate([h[...] for h in (c_in, o_in, z_in, y_in)], 1)
    total = partial[...] + jnp.dot(
        halo, dense[pl.ds(points, DIRECTIONS * block), :], preferred_element_type=jnp.float32
    )
    tall = wet_mask.shape[0]
    total = total.reshape(tracers // tall, tall, points) * wet_mask[...][None]
    total = total.reshape(tracers, points)
    if last:
        stage, sem = refs
        stage[...] = total
        copy = pltpu.make_async_copy(stage, out, sem)
        copy.start()
        copy.wait()
        return
    total = total.astype(out.dtype)
    out[...] = total
    tall = send_pick.shape[1]
    blocks = [
        total[:, r * block : (r + 1) * block].reshape(tracers // tall, tall, block) for r in range(row_blocks)
    ]
    for n, outgoing in enumerate(refs):
        wanted = send_pick[n]
        chosen = blocks[0]
        for r in range(1, row_blocks):
            chosen = jnp.where((wanted == r)[None], blocks[r], chosen)
        outgoing[...] = chosen.reshape(tracers, block)


def on_device(swaps, tracer, source, exp_a, exp_b, imp_a, imp_b, col_index, block_count, send_list, wet_rows, month_day):
    tracers, points = tracer.shape
    row_blocks, slots = col_index.shape
    block = points // row_blocks
    pairs = row_blocks * slots
    half, full = jnp.bfloat16, jnp.float32
    hbm = pl.BlockSpec(memory_space=pltpu.HBM)
    vmem = pl.BlockSpec(memory_space=pltpu.VMEM)
    params = pltpu.CompilerParams(vmem_limit_bytes=32 * 1024 * 1024)
    shape = jax.ShapeDtypeStruct
    piece = shape((tracers, block), half)
    field_shape = shape((tracers, points), half)
    partial_shape = shape((tracers, points), full)
    dense_shape = shape(((row_blocks + DIRECTIONS + 1 + slots) * block, points), half)
    table_size = 4 * pairs + 1
    dma = pltpu.SemaphoreType.DMA

    def stay(*arrays):
        return [pltpu.with_memory_space_constraint(x, pltpu.HBM) for x in arrays]

    *outgoing, field, wet_mask, send_pick = pl.pallas_call(
        prologue_kernel,
        out_shape=[piece] * DIRECTIONS
        + [field_shape, shape((8, points), full), shape((DIRECTIONS, 16, block), half)],
        in_specs=[hbm] * 3,
        out_specs=[vmem] * (DIRECTIONS + 3),
        scratch_shapes=[
            pltpu.VMEM((tracers, points), full),
            pltpu.SMEM((row_blocks,), jnp.int32),
            pltpu.SMEM((DIRECTIONS,), jnp.int32),
            dma((3,)),
        ],
        compiler_params=params,
        name="prologue",
    )(*stay(tracer, wet_rows, send_list.reshape(DIRECTIONS)))

    def ready_first(field):
        return pl.pallas_call(
            ready_first_kernel,
            out_shape=[dense_shape, partial_shape, shape((table_size,), jnp.int32), shape((2 * STEPS, 8, block), full)],
            in_specs=[hbm] * 3 + [vmem] + [hbm] * 3,
            out_specs=[vmem] * 4,
            scratch_shapes=[
                pltpu.VMEM(exp_a.shape, half),
                pltpu.VMEM(exp_b.shape, half),
                pltpu.VMEM((tracers, points), full),
                pltpu.SMEM((row_blocks, slots), jnp.int32),
                pltpu.SMEM((row_blocks,), jnp.int32),
                pltpu.SMEM((STEPS,), jnp.int32),
                pltpu.SMEM((table_size,), jnp.int32),
                dma((5 + 2 * row_blocks,)),
            ],
            compiler_params=params,
            name="ready_first",
        )(*stay(col_index, block_count, month_day), field, *stay(source, exp_a, exp_b))

    def ready(step, explicit, table, weights, field, dense):
        a, b = (exp_a, exp_b) if explicit else (imp_a, imp_b)
        operands = [table, weights, field, a, b, dense] + ([source] if explicit else [])
        return pl.pallas_call(
            functools.partial(ready_kernel, step, explicit),
            out_shape=[dense_shape, partial_shape],
            in_specs=[vmem] * len(operands),
            out_specs=[vmem] * 2,
            input_output_aliases={5: 0},
            scratch_shapes=[
                pltpu.VMEM((row_blocks // 2, slots, block, block), half),
                pltpu.SMEM((table_size,), jnp.int32),
                dma(()),
            ],
            compiler_params=params,
            name="ready",
        )(*operands)

    def finish(last, partial, dense, halos):
        return pl.pallas_call(
            functools.partial(finish_kernel, last),
            out_shape=[partial_shape] if last else [field_shape] + [piece] * DIRECTIONS,
            in_specs=[vmem] * (4 + DIRECTIONS),
            out_specs=[hbm] if last else [vmem] * (1 + DIRECTIONS),
            scratch_shapes=[pltpu.VMEM((tracers, points), full), dma(())] if last else [],
            compiler_params=params,
            name="finish",
        )(partial, dense, wet_mask, send_pick, *halos)

    for step in range(STEPS):
        for explicit in (True, False):
            halos = [lax.ppermute(p, ("groups", "rows"), s) for p, s in zip(outgoing, swaps)]
            if step == 0 and explicit:
                dense, partial, table, weights = ready_first(field)
            else:
                dense, partial = ready(step, explicit, table, weights, field, dense)
            last = step == STEPS - 1 and not explicit
            field, *outgoing = finish(last, partial, dense, halos)
    return field


def solution(mesh):
    count, groups = mesh.shape["rows"], mesh.shape["groups"]
    swaps = [swap_pairs(count, groups, stride, parity) for stride in (1, STRIDE) for parity in (0, 1)]
    wide = P("groups", "rows")
    rows = P("rows")
    return jax.shard_map(
        functools.partial(on_device, swaps),
        mesh=mesh,
        in_specs=(wide, wide, rows, rows, rows, rows, rows, rows, rows, rows, P()),
        out_specs=wide,
        check_vma=False,
    )
```

time: 36.8 us -> 28.8 us (0.78)
  local copies, waits for them, and re-layouts: 6.22 us -> 0.02 us
  waiting for transfers between devices: 2.15 us -> 0.42 us
  Pallas kernels: 12.7 us -> 13.1 us
    unnamed x29 -> x10, local copies, waits for them, and re-layouts: 6.22 us -> 0.02 us
    ppermute x16, waiting for transfers between devices: 2.15 us -> 0.42 us  [on_device(): lax.ppermute(p, ('groups', 'rows'), s)]
  transfers between devices with their start and end apart: 16 -> 16, of which waited for: 3 -> 1; matrix products, arithmetic and copies ran while one was open for 0% -> 0% of each run, Pallas kernels for 15% -> 35%
where the time goes in v2:
time: 28.8 us; the launch traced here: 28.7 us
  starting transfers between devices  15 us (52%)
  Pallas kernels  13.1 us (45%)
  waiting for transfers between devices  0.42 us (1%)
    ppermute x16, starting transfers between devices, on_device(): lax.ppermute(p, ('groups', 'rows'), s)  15 us
    pallas_call x3, Pallas kernels, ready(): pl.pallas_call(functools.partial(ready_kernel, step, explicit), out_shape...  6.23 us
    pallas_call x1, Pallas kernels, ready_first(): pl.pallas_call(ready_first_kernel, out_shape=[dense_shape, partial_shape,...  3.7 us
    pallas_call x4, Pallas kernels, finish(): pl.pallas_call(functools.partial(finish_kernel, last), out_shape=[partial...  1.98 us
    pallas_call x1, Pallas kernels, on_device(): pl.pallas_call(prologue_kernel, out_shape=[piece] * DIRECTIONS + [field_s...  1.17 us
  transfers between devices with their start and end apart: 16, of which 1 were waited for; matrix products, arithmetic and copies ran while one was open for 0% of the time, Pallas kernels for 35%

profile of v2, /device:TPU:0, one launch (start us, length us, event | category | flops | bytes accessed | tf_op | source)
XLA Modules:
  0.0 28.7 jit_solution(14365694552311538205)
XLA Ops:
  0.0 0.0 copy-start.3
  0.0 0.0 copy-start.2
  0.0 1.2 %prologue.1 = (bf16[64,128]{1,0:T(8,128)(2,1)S(1)}, bf16[64,128]{1,0:T(8,128)(2,1)S(1)}, bf16[64,128]{1,0:T(8,128)(2,1)S(1)}, bf16[64,128]{1,0:T(8,128)(2,1)S(1)...) custom-call(f32[64,1024]{1,0:T(8,128)} %tracer.1, s32[8]{0:T(128)} %wet.1, ...), custom_call_target="tpu_custom_call" | custom-call | tf_op jit(solution)/shard_map/prologue/pallas_call | solution.py:256
  1.2 0.5 %collective-permute-start = (bf16[64,128]{1,0:T(8,128)(2,1)S(1)}, bf16[64,128]{1,0:T(8,128)(2,1)S(1)}, u32[]{:S(2)}, u32[]{:S(2)}) collective-permute-start(bf16[64,128]{1,0:T(8,128)(2,1)S(1)} %get-tuple-element.44), channel_id=1, source_target_pairs={{0,1},{1,0},{2,3},{3,2},{4,5},{5,4},{6,7},{7,6},{8,9},{9,8},{10,11... | collective-permute-start | bytes 49160 | tf_op jit(solution)/shard_map/ppermute | solution.py:323
  1.7 2.6 %collective-permute-start.1 = (bf16[64,128]{1,0:T(8,128)(2,1)S(1)}, bf16[64,128]{1,0:T(8,128)(2,1)S(1)}, u32[]{:S(2)}, u32[]{:S(2)}) collective-permute-start(bf16[64,128]{1,0:T(8,128)(2,1)S(1)} %get-tuple-element.45), channel_id=1, source_target_pairs={{0,16},{1,2},{2,1},{3,4},{4,3},{5,6},{6,5},{7,8},{8,7},{9,10},{10,... | collective-permute-start | bytes 49160 | tf_op jit(solution)/shard_map/ppermute | solution.py:323
  4.3 1.5 %collective-permute-start.2 = (bf16[64,128]{1,0:T(8,128)(2,1)S(1)}, bf16[64,128]{1,0:T(8,128)(2,1)S(1)}, u32[]{:S(2)}, u32[]{:S(2)}) collective-permute-start(bf16[64,128]{1,0:T(8,128)(2,1)S(1)} %get-tuple-element.46), channel_id=1, source_target_pairs={{0,4},{1,5},{2,6},{3,7},{4,0},{5,1},{6,2},{7,3},{8,12},{9,13},{10,... | collective-permute-start | bytes 49160 | tf_op jit(solution)/shard_map/ppermute | solution.py:323
  5.8 0.0 collective-permute-start.3
  5.8 3.7 %ready_first.1 = (bf16[2688,1024]{1,0:T(8,128)(2,1)S(1)}, f32[64,1024]{1,0:T(8,128)S(1)}, s32[257]{0:T(512)S(1)}, f32[4,8,128]{2,1,0:T(8,128)S(1)}) custom-call(s32[8,8]{1,0:T(8,128)} %col.1, s32[8]{0:T(128)} %count.1, s32[2]{0:T(128)} %day.1, bf16[64,1024]{1,0:T(8,128)(2,1)S(1)} %get-tuple-element.37.field, f32[64,1024]{1,0:T(8,128)} %refs_6_.1, ...), custom_call_target="tpu_custom_call" | custom-call | tf_op jit(solution)/shard_map/ready_first/pallas_call | solution.py:273
  9.5 0.0 collective-permute-done.c_in
  9.5 0.0 collective-permute-done.1.o_in
  9.5 0.0 collective-permute-done.2.z_in
  9.5 0.0 collective-permute-done.3.y_in
  9.5 0.3 %finish.4 = (bf16[64,1024]{1,0:T(8,128)(2,1)S(1)}, bf16[64,128]{1,0:T(8,128)(2,1)S(1)}, bf16[64,128]{1,0:T(8,128)(2,1)S(1)}, bf16[64,128]{1,0:T(8,128)(2,1)S(1)}, bf16[64,128]{1,0:T(8,128)(2,1)S(1)}) custom-call(f32[64,1024]{1,0:T(8,128)S(1)} %get-tuple-element.40.partial, bf16[2688,1024]{1,0:T(8,128)(2,1)S(1)} %get-tuple-element.41.dense.refs_5_, ...), custom_call_target="tpu_custom_call" | custom-call | tf_op jit(solution)/shard_map/finish/pallas_call | solution.py:311
  9.9 0.5 %collective-permute-start.4 = (bf16[64,128]{1,0:T(8,128)(2,1)S(1)}, bf16[64,128]{1,0:T(8,128)(2,1)S(1)}, u32[]{:S(2)}, u32[]{:S(2)}) collective-permute-start(bf16[64,128]{1,0:T(8,128)(2,1)S(1)} %get-tuple-element.51), channel_id=1, source_target_pairs={{0,1},{1,0},{2,3},{3,2},{4,5},{5,4},{6,7},{7,6},{8,9},{9,8},{10,11... | collective-permute-start | bytes 49160 | tf_op jit(solution)/shard_map/ppermute | solution.py:323
  10.4 1.5 %collective-permute-start.5 = (bf16[64,128]{1,0:T(8,128)(2,1)S(1)}, bf16[64,128]{1,0:T(8,128)(2,1)S(1)}, u32[]{:S(2)}, u32[]{:S(2)}) collective-permute-start(bf16[64,128]{1,0:T(8,128)(2,1)S(1)} %get-tuple-element.52), channel_id=1, source_target_pairs={{0,16},{1,2},{2,1},{3,4},{4,3},{5,6},{6,5},{7,8},{8,7},{9,10},{10,... | collective-permute-start | bytes 49160 | tf_op jit(solution)/shard_map/ppermute | solution.py:323
  11.9 1.3 %collective-permute-start.6 = (bf16[64,128]{1,0:T(8,128)(2,1)S(1)}, bf16[64,128]{1,0:T(8,128)(2,1)S(1)}, u32[]{:S(2)}, u32[]{:S(2)}) collective-permute-start(bf16[64,128]{1,0:T(8,128)(2,1)S(1)} %get-tuple-element.53), channel_id=1, source_target_pairs={{0,4},{1,5},{2,6},{3,7},{4,0},{5,1},{6,2},{7,3},{8,12},{9,13},{10,... | collective-permute-start | bytes 49160 | tf_op jit(solution)/shard_map/ppermute | solution.py:323
  13.2 0.8 %collective-permute-start.7 = (bf16[64,128]{1,0:T(8,128)(2,1)S(1)}, bf16[64,128]{1,0:T(8,128)(2,1)S(1)}, u32[]{:S(2)}, u32[]{:S(2)}) collective-permute-start(bf16[64,128]{1,0:T(8,128)(2,1)S(1)} %get-tuple-element.54), channel_id=1, source_target_pairs={{0,1},{1,0},{2,3},{3,2},{4,8},{5,9},{6,10},{7,11},{8,4},{9,5},{10,... | collective-permute-start | bytes 49160 | tf_op jit(solution)/shard_map/ppermute | solution.py:323
  14.0 0.0 copy-done.3
  14.0 0.0 copy-done.2
  14.0 0.0 copy-start
  14.0 0.0 copy-start.1
  14.0 0.0 copy-start.4
  14.0 2.1 %ready.3 = (bf16[2688,1024]{1,0:T(8,128)(2,1)S(1)}, f32[64,1024]{1,0:T(8,128)S(1)}) custom-call(s32[257]{0:T(512)S(1)} %get-tuple-element.38.refs_0_, f32[4,8,128]{2,1,0:T(8,128)S(1)} %get-tuple-element.39.refs_1_, bf16[64,1024]{1,0:T(8,128)(2,1)S(1)} %get-tuple-element.48.refs_2_, ...), custom_call_target="tpu_custom_call", output_to_operand_aliasing={{0}: (5, {})} | custom-call | tf_op jit(solution)/shard_map/ready/pallas_call | solution.py:295
  16.1 0.0 collective-permute-done.4.c_in
  16.1 0.0 collective-permute-done.5.o_in
  16.1 0.0 collective-permute-done.6.z_in
  16.1 0.0 collective-permute-done.7.y_in
  16.1 0.3 %finish.5 = (bf16[64,1024]{1,0:T(8,128)(2,1)S(1)}, bf16[64,128]{1,0:T(8,128)(2,1)S(1)}, bf16[64,128]{1,0:T(8,128)(2,1)S(1)}, bf16[64,128]{1,0:T(8,128)(2,1)S(1)}, bf16[64,128]{1,0:T(8,128)(2,1)S(1)}) custom-call(f32[64,1024]{1,0:T(8,128)S(1)} %get-tuple-element.49.partial, bf16[2688,1024]{1,0:T(8,128)(2,1)S(1)} %get-tuple-element.50.dense.refs_5_, ...), custom_call_target="tpu_custom_call" | custom-call | tf_op jit(solution)/shard_map/finish/pallas_call | solution.py:311
  16.5 0.1 collective-permute-start.8
  16.5 1.2 %collective-permute-start.9 = (bf16[64,128]{1,0:T(8,128)(2,1)S(1)}, bf16[64,128]{1,0:T(8,128)(2,1)S(1)}, u32[]{:S(2)}, u32[]{:S(2)}) collective-permute-start(bf16[64,128]{1,0:T(8,128)(2,1)S(1)} %get-tuple-element.59), channel_id=1, source_target_pairs={{0,16},{1,2},{2,1},{3,4},{4,3},{5,6},{6,5},{7,8},{8,7},{9,10},{10,... | collective-permute-start | bytes 49160 | tf_op jit(solution)/shard_map/ppermute | solution.py:323
  17.8 1.7 %collective-permute-start.10 = (bf16[64,128]{1,0:T(8,128)(2,1)S(1)}, bf16[64,128]{1,0:T(8,128)(2,1)S(1)}, u32[]{:S(2)}, u32[]{:S(2)}) collective-permute-start(bf16[64,128]{1,0:T(8,128)(2,1)S(1)} %get-tuple-element.60), channel_id=1, source_target_pairs={{0,4},{1,5},{2,6},{3,7},{4,0},{5,1},{6,2},{7,3},{8,12},{9,13},{10,... | collective-permute-start | bytes 49160 | tf_op jit(solution)/shard_map/ppermute | solution.py:323
  19.5 0.0 collective-permute-start.11
  19.5 0.0 copy-done
  19.5 0.0 copy-done.1
  19.5 0.0 copy-done.4
  19.5 2.1 %ready.4 = (bf16[2688,1024]{1,0:T(8,128)(2,1)S(1)}, f32[64,1024]{1,0:T(8,128)S(1)}) custom-call(s32[257]{0:T(512)S(1)} %get-tuple-element.38.refs_0_, f32[4,8,128]{2,1,0:T(8,128)S(1)} %get-tuple-element.39.refs_1_, bf16[64,1024]{1,0:T(8,128)(2,1)S(1)} %get-tuple-element.55.refs_2_, ...), custom_call_target="tpu_custom_call", output_to_operand_aliasing={{0}: (5, {})} | custom-call | tf_op jit(solution)/shard_map/ready/pallas_call | solution.py:295
  21.6 0.0 collective-permute-done.8.c_in
  21.6 0.0 collective-permute-done.9.o_in
  21.6 0.0 collective-permute-done.10.z_in
  21.6 0.0 collective-permute-done.11.y_in
  21.6 0.3 %finish.6 = (bf16[64,1024]{1,0:T(8,128)(2,1)S(1)}, bf16[64,128]{1,0:T(8,128)(2,1)S(1)}, bf16[64,128]{1,0:T(8,128)(2,1)S(1)}, bf16[64,128]{1,0:T(8,128)(2,1)S(1)}, bf16[64,128]{1,0:T(8,128)(2,1)S(1)}) custom-call(f32[64,1024]{1,0:T(8,128)S(1)} %get-tuple-element.56.partial, bf16[2688,1024]{1,0:T(8,128)(2,1)S(1)} %get-tuple-element.57.dense.refs_5_, ...), custom_call_target="tpu_custom_call" | custom-call | tf_op jit(solution)/shard_map/finish/pallas_call | solution.py:311
  21.9 0.5 %collective-permute-start.12 = (bf16[64,128]{1,0:T(8,128)(2,1)S(1)}, bf16[64,128]{1,0:T(8,128)(2,1)S(1)}, u32[]{:S(2)}, u32[]{:S(2)}) collective-permute-start(bf16[64,128]{1,0:T(8,128)(2,1)S(1)} %get-tuple-element.65), channel_id=1, source_target_pairs={{0,1},{1,0},{2,3},{3,2},{4,5},{5,4},{6,7},{7,6},{8,9},{9,8},{10,11... | collective-permute-start | bytes 49160 | tf_op jit(solution)/shard_map/ppermute | solution.py:323
  22.5 1.5 %collective-permute-start.13 = (bf16[64,128]{1,0:T(8,128)(2,1)S(1)}, bf16[64,128]{1,0:T(8,128)(2,1)S(1)}, u32[]{:S(2)}, u32[]{:S(2)}) collective-permute-start(bf16[64,128]{1,0:T(8,128)(2,1)S(1)} %get-tuple-element.66), channel_id=1, source_target_pairs={{0,16},{1,2},{2,1},{3,4},{4,3},{5,6},{6,5},{7,8},{8,7},{9,10},{10,... | collective-permute-start | bytes 49160 | tf_op jit(solution)/shard_map/ppermute | solution.py:323
  23.9 1.2 %collective-permute-start.14 = (bf16[64,128]{1,0:T(8,128)(2,1)S(1)}, bf16[64,128]{1,0:T(8,128)(2,1)S(1)}, u32[]{:S(2)}, u32[]{:S(2)}) collective-permute-start(bf16[64,128]{1,0:T(8,128)(2,1)S(1)} %get-tuple-element.67), channel_id=1, source_target_pairs={{0,4},{1,5},{2,6},{3,7},{4,0},{5,1},{6,2},{7,3},{8,12},{9,13},{10,... | collective-permute-start | bytes 49160 | tf_op jit(solution)/shard_map/ppermute | solution.py:323
  25.2 0.0 collective-permute-start.15
  25.2 2.1 %ready.5 = (bf16[2688,1024]{1,0:T(8,128)(2,1)S(1)}, f32[64,1024]{1,0:T(8,128)S(1)}) custom-call(s32[257]{0:T(512)S(1)} %get-tuple-element.38.refs_0_, f32[4,8,128]{2,1,0:T(8,128)S(1)} %get-tuple-element.39.refs_1_, bf16[64,1024]{1,0:T(8,128)(2,1)S(1)} %get-tuple-element.62.refs_2_, ...), custom_call_target="tpu_custom_call", output_to_operand_aliasing={{0}: (5, {})} | custom-call | tf_op jit(solution)/shard_map/ready/pallas_call | solution.py:295
  27.3 0.0 collective-permute-done.12.c_in
  27.3 0.0 collective-permute-done.13.o_in
  27.3 0.4 %collective-permute-done.14.z_in = bf16[64,128]{1,0:T(8,128)(2,1)S(1)} collective-permute-done((bf16[64,128]{1,0:T(8,128)(2,1)S(1)}, bf16[64,128]{1,0:T(8,128)(2,1)S(1)}, u32[]{:S(2)}, u32[]{:S(2)}) %collective-permute-start.14) | collective-permute-done | bytes 16416 | tf_op jit(solution)/shard_map/ppermute | solution.py:323
  27.7 0.0 collective-permute-done.15.y_in
  27.7 1.0 %finish.7 = f32[64,1024]{1,0:T(8,128)} custom-call(f32[64,1024]{1,0:T(8,128)S(1)} %get-tuple-element.63.partial, bf16[2688,1024]{1,0:T(8,128)(2,1)S(1)} %get-tuple-element.64.dense, f32[8,1024]{1,0:T(8,128)S(1)} %get-tuple-element.42.wet_mask, bf16[4,16,128]{2,1,0:T(8,128)(2,1)S(1)} %get-tuple-element.43.send_pick, ...), custom_call_target="tpu_custom_call" | custom-call | tf_op jit(solution)/shard_map/finish/pallas_call | solution.py:311
Async XLA Ops:
  0.0 14.0 %copy-start.3 = (bf16[8,8,128,128]{3,2,1,0:T(8,128)(2,1)S(1)}, bf16[8,8,128,128]{3,2,1,0:T(8,128)(2,1)}, u32[]{:S(2)}) copy-start(bf16[8,8,128,128]{3,2,1,0:T(8,128)(2,1)} %refs_4_.5) | copy-start | bytes 6291460
  0.0 14.0 %copy-start.2 = (bf16[8,8,128,128]{3,2,1,0:T(8,128)(2,1)S(1)}, bf16[8,8,128,128]{3,2,1,0:T(8,128)(2,1)}, u32[]{:S(2)}) copy-start(bf16[8,8,128,128]{3,2,1,0:T(8,128)(2,1)} %refs_3_.5) | copy-start | bytes 6291460
  1.2 8.3 %collective-permute-start = (bf16[64,128]{1,0:T(8,128)(2,1)S(1)}, bf16[64,128]{1,0:T(8,128)(2,1)S(1)}, u32[]{:S(2)}, u32[]{:S(2)}) collective-permute-start(bf16[64,128]{1,0:T(8,128)(2,1)S(1)} %get-tuple-element.44), channel_id=1, source_target_pairs={{0,1},{1,0},{2,3},{3,2},{4,5},{5,4},{6,7},{7,6},{8,9},{9,8},{10,11... | collective-permute-start | bytes 49160 | tf_op jit(solution)/shard_map/ppermute | solution.py:323
  1.7 7.8 %collective-permute-start.1 = (bf16[64,128]{1,0:T(8,128)(2,1)S(1)}, bf16[64,128]{1,0:T(8,128)(2,1)S(1)}, u32[]{:S(2)}, u32[]{:S(2)}) collective-permute-start(bf16[64,128]{1,0:T(8,128)(2,1)S(1)} %get-tuple-element.45), channel_id=1, source_target_pairs={{0,16},{1,2},{2,1},{3,4},{4,3},{5,6},{6,5},{7,8},{8,7},{9,10},{10,... | collective-permute-start | bytes 49160 | tf_op jit(solution)/shard_map/ppermute | solution.py:323
  4.3 5.3 %collective-permute-start.2 = (bf16[64,128]{1,0:T(8,128)(2,1)S(1)}, bf16[64,128]{1,0:T(8,128)(2,1)S(1)}, u32[]{:S(2)}, u32[]{:S(2)}) collective-permute-start(bf16[64,128]{1,0:T(8,128)(2,1)S(1)} %get-tuple-element.46), channel_id=1, source_target_pairs={{0,4},{1,5},{2,6},{3,7},{4,0},{5,1},{6,2},{7,3},{8,12},{9,13},{10,... | collective-permute-start | bytes 49160 | tf_op jit(solution)/shard_map/ppermute | solution.py:323
  5.8 3.7 %collective-permute-start.3 = (bf16[64,128]{1,0:T(8,128)(2,1)S(1)}, bf16[64,128]{1,0:T(8,128)(2,1)S(1)}, u32[]{:S(2)}, u32[]{:S(2)}) collective-permute-start(bf16[64,128]{1,0:T(8,128)(2,1)S(1)} %get-tuple-element.47), channel_id=1, source_target_pairs={{0,1},{1,0},{2,3},{3,2},{4,8},{5,9},{6,10},{7,11},{8,4},{9,5},{10,... | collective-permute-start | bytes 49160 | tf_op jit(solution)/shard_map/ppermute | solution.py:323
  9.9 6.2 %collective-permute-start.4 = (bf16[64,128]{1,0:T(8,128)(2,1)S(1)}, bf16[64,128]{1,0:T(8,128)(2,1)S(1)}, u32[]{:S(2)}, u32[]{:S(2)}) collective-permute-start(bf16[64,128]{1,0:T(8,128)(2,1)S(1)} %get-tuple-element.51), channel_id=1, source_target_pairs={{0,1},{1,0},{2,3},{3,2},{4,5},{5,4},{6,7},{7,6},{8,9},{9,8},{10,11... | collective-permute-start | bytes 49160 | tf_op jit(solution)/shard_map/ppermute | solution.py:323
  10.4 5.7 %collective-permute-start.5 = (bf16[64,128]{1,0:T(8,128)(2,1)S(1)}, bf16[64,128]{1,0:T(8,128)(2,1)S(1)}, u32[]{:S(2)}, u32[]{:S(2)}) collective-permute-start(bf16[64,128]{1,0:T(8,128)(2,1)S(1)} %get-tuple-element.52), channel_id=1, source_target_pairs={{0,16},{1,2},{2,1},{3,4},{4,3},{5,6},{6,5},{7,8},{8,7},{9,10},{10,... | collective-permute-start | bytes 49160 | tf_op jit(solution)/shard_map/ppermute | solution.py:323
  11.9 4.2 %collective-permute-start.6 = (bf16[64,128]{1,0:T(8,128)(2,1)S(1)}, bf16[64,128]{1,0:T(8,128)(2,1)S(1)}, u32[]{:S(2)}, u32[]{:S(2)}) collective-permute-start(bf16[64,128]{1,0:T(8,128)(2,1)S(1)} %get-tuple-element.53), channel_id=1, source_target_pairs={{0,4},{1,5},{2,6},{3,7},{4,0},{5,1},{6,2},{7,3},{8,12},{9,13},{10,... | collective-permute-start | bytes 49160 | tf_op jit(solution)/shard_map/ppermute | solution.py:323
  13.2 2.9 %collective-permute-start.7 = (bf16[64,128]{1,0:T(8,128)(2,1)S(1)}, bf16[64,128]{1,0:T(8,128)(2,1)S(1)}, u32[]{:S(2)}, u32[]{:S(2)}) collective-permute-start(bf16[64,128]{1,0:T(8,128)(2,1)S(1)} %get-tuple-element.54), channel_id=1, source_target_pairs={{0,1},{1,0},{2,3},{3,2},{4,8},{5,9},{6,10},{7,11},{8,4},{9,5},{10,... | collective-permute-start | bytes 49160 | tf_op jit(solution)/shard_map/ppermute | solution.py:323
  14.0 5.5 %copy-start = (bf16[8,8,128,128]{3,2,1,0:T(8,128)(2,1)S(1)}, bf16[8,8,128,128]{3,2,1,0:T(8,128)(2,1)}, u32[]{:S(2)}) copy-start(bf16[8,8,128,128]{3,2,1,0:T(8,128)(2,1)} %refs_3_.4) | copy-start | bytes 6291460
  14.0 5.5 %copy-start.1 = (bf16[8,8,128,128]{3,2,1,0:T(8,128)(2,1)S(1)}, bf16[8,8,128,128]{3,2,1,0:T(8,128)(2,1)}, u32[]{:S(2)}) copy-start(bf16[8,8,128,128]{3,2,1,0:T(8,128)(2,1)} %refs_4_.4) | copy-start | bytes 6291460
  14.0 5.5 %copy-start.4 = (f32[64,1024]{1,0:T(8,128)S(1)}, f32[64,1024]{1,0:T(8,128)}, u32[]{:S(2)}) copy-start(f32[64,1024]{1,0:T(8,128)} %refs_6_.1) | copy-start | bytes 786436
  16.5 5.1 %collective-permute-start.8 = (bf16[64,128]{1,0:T(8,128)(2,1)S(1)}, bf16[64,128]{1,0:T(8,128)(2,1)S(1)}, u32[]{:S(2)}, u32[]{:S(2)}) collective-permute-start(bf16[64,128]{1,0:T(8,128)(2,1)S(1)} %get-tuple-element.58), channel_id=1, source_target_pairs={{0,1},{1,0},{2,3},{3,2},{4,5},{5,4},{6,7},{7,6},{8,9},{9,8},{10,11... | collective-permute-start | bytes 49160 | tf_op jit(solution)/shard_map/ppermute | solution.py:323
  16.5 5.1 %collective-permute-start.9 = (bf16[64,128]{1,0:T(8,128)(2,1)S(1)}, bf16[64,128]{1,0:T(8,128)(2,1)S(1)}, u32[]{:S(2)}, u32[]{:S(2)}) collective-permute-start(bf16[64,128]{1,0:T(8,128)(2,1)S(1)} %get-tuple-element.59), channel_id=1, source_target_pairs={{0,16},{1,2},{2,1},{3,4},{4,3},{5,6},{6,5},{7,8},{8,7},{9,10},{10,... | collective-permute-start | bytes 49160 | tf_op jit(solution)/shard_map/ppermute | solution.py:323
  17.8 3.8 %collective-permute-start.10 = (bf16[64,128]{1,0:T(8,128)(2,1)S(1)}, bf16[64,128]{1,0:T(8,128)(2,1)S(1)}, u32[]{:S(2)}, u32[]{:S(2)}) collective-permute-start(bf16[64,128]{1,0:T(8,128)(2,1)S(1)} %get-tuple-element.60), channel_id=1, source_target_pairs={{0,4},{1,5},{2,6},{3,7},{4,0},{5,1},{6,2},{7,3},{8,12},{9,13},{10,... | collective-permute-start | bytes 49160 | tf_op jit(solution)/shard_map/ppermute | solution.py:323
  19.5 2.1 %collective-permute-start.11 = (bf16[64,128]{1,0:T(8,128)(2,1)S(1)}, bf16[64,128]{1,0:T(8,128)(2,1)S(1)}, u32[]{:S(2)}, u32[]{:S(2)}) collective-permute-start(bf16[64,128]{1,0:T(8,128)(2,1)S(1)} %get-tuple-element.61), channel_id=1, source_target_pairs={{0,1},{1,0},{2,3},{3,2},{4,8},{5,9},{6,10},{7,11},{8,4},{9,5},{10,... | collective-permute-start | bytes 49160 | tf_op jit(solution)/shard_map/ppermute | solution.py:323
  21.9 5.3 %collective-permute-start.12 = (bf16[64,128]{1,0:T(8,128)(2,1)S(1)}, bf16[64,128]{1,0:T(8,128)(2,1)S(1)}, u32[]{:S(2)}, u32[]{:S(2)}) collective-permute-start(bf16[64,128]{1,0:T(8,128)(2,1)S(1)} %get-tuple-element.65), channel_id=1, source_target_pairs={{0,1},{1,0},{2,3},{3,2},{4,5},{5,4},{6,7},{7,6},{8,9},{9,8},{10,11... | collective-permute-start | bytes 49160 | tf_op jit(solution)/shard_map/ppermute | solution.py:323
  22.5 4.8 %collective-permute-start.13 = (bf16[64,128]{1,0:T(8,128)(2,1)S(1)}, bf16[64,128]{1,0:T(8,128)(2,1)S(1)}, u32[]{:S(2)}, u32[]{:S(2)}) collective-permute-start(bf16[64,128]{1,0:T(8,128)(2,1)S(1)} %get-tuple-element.66), channel_id=1, source_target_pairs={{0,16},{1,2},{2,1},{3,4},{4,3},{5,6},{6,5},{7,8},{8,7},{9,10},{10,... | collective-permute-start | bytes 49160 | tf_op jit(solution)/shard_map/ppermute | solution.py:323
  23.9 3.7 %collective-permute-start.14 = (bf16[64,128]{1,0:T(8,128)(2,1)S(1)}, bf16[64,128]{1,0:T(8,128)(2,1)S(1)}, u32[]{:S(2)}, u32[]{:S(2)}) collective-permute-start(bf16[64,128]{1,0:T(8,128)(2,1)S(1)} %get-tuple-element.67), channel_id=1, source_target_pairs={{0,4},{1,5},{2,6},{3,7},{4,0},{5,1},{6,2},{7,3},{8,12},{9,13},{10,... | collective-permute-start | bytes 49160 | tf_op jit(solution)/shard_map/ppermute | solution.py:323
  25.2 2.5 %collective-permute-start.15 = (bf16[64,128]{1,0:T(8,128)(2,1)S(1)}, bf16[64,128]{1,0:T(8,128)(2,1)S(1)}, u32[]{:S(2)}, u32[]{:S(2)}) collective-permute-start(bf16[64,128]{1,0:T(8,128)(2,1)S(1)} %get-tuple-element.68), channel_id=1, source_target_pairs={{0,1},{1,0},{2,3},{3,2},{4,8},{5,9},{6,10},{7,11},{8,4},{9,5},{10,... | collective-permute-start | bytes 49160 | tf_op jit(solution)/shard_map/ppermute | solution.py:323

commit v3 on v1

v3 whole, which is shorter than its diff:
```python
import functools

import jax
import jax.numpy as jnp
from jax import lax
from jax.experimental import pallas as pl
from jax.experimental.pallas import tpu as pltpu
from jax.sharding import PartitionSpec as P

STEPS = 2
DAYS = 30
STRIDE = 4
DIRECTIONS = 4


def swap_pairs(count, groups, stride, parity):
    partner = {}
    for i in range(count - stride):
        if (i // stride) % 2 == parity:
            partner[i], partner[i + stride] = i + stride, i
    idle = [i for i in range(count) if i not in partner]
    for i in idle:
        if i ^ 1 in idle:
            partner[i] = i ^ 1
    pairs = []
    for g in range(groups):
        for i in range(count):
            if i in partner:
                pairs.append((g * count + i, g * count + partner[i]))
            else:
                other = g ^ 1 if g ^ 1 < groups else g
                pairs.append((g * count + i, other * count + i))
    return pairs


def my_flips():
    place = lax.axis_index("rows")
    return 1 - place % 2, 1 - (place // STRIDE) % 2


def direction_of(swap, flips):
    if swap < 2:
        return swap ^ 1 ^ flips[0]
    return 2 + ((swap - 2) ^ 1 ^ flips[1])


def place_of(slot, row_blocks, flips):
    j = slot - row_blocks
    return jnp.where(slot < row_blocks, slot, row_blocks + (j ^ jnp.where(j < 2, flips[0], flips[1])))


def prologue_kernel(
    tracer, wet_in, send_in, col_in, count_in, day_in, source,
    c_out, o_out, z_out, y_out, field, dense, forcing, wet, send, col, count, day,
    raw, sems,
):
    tracers, points = raw.shape
    row_blocks = wet.shape[0]
    block = points // row_blocks
    pairs = ((tracer, raw), (wet_in, wet), (send_in, send), (col_in, col), (count_in, count), (day_in, day), (source, forcing))
    copies = [pltpu.make_async_copy(a, b, sems.at[n]) for n, (a, b) in enumerate(pairs)]
    for copy in copies:
        copy.start()
    used = (row_blocks + DIRECTIONS) * block
    dense[pl.ds(0, used), :] = jnp.zeros((used, points), dense.dtype)
    flips = my_flips()
    for copy in copies[:-1]:
        copy.wait()
    lane = lax.broadcasted_iota(jnp.int32, (tracers, block), 1)
    for n, out in enumerate((c_out, o_out, z_out, y_out)):
        row = send[direction_of(n, flips)]
        piece = raw[:, pl.ds(pl.multiple_of(row * block, block), block)]
        out[...] = jnp.where(lane < wet[row], piece, 0.0).astype(out.dtype)
    for r in range(row_blocks):
        columns = pl.ds(r * block, block)
        field[:, columns] = jnp.where(lane < wet[r], raw[:, columns], 0.0).astype(field.dtype)
    copies[-1].wait()


def blended(a, b, early, late):
    mixed = early * a.astype(jnp.float32) + late * b.astype(jnp.float32)
    return mixed.astype(a.dtype).T


def make_table(col, count, _a, _b, table):
    row_blocks, slots = col.shape
    pairs = row_blocks * slots
    flips = my_flips()
    unused = row_blocks + DIRECTIONS
    repeats = jnp.int32(0)
    for r in range(row_blocks):
        for k in range(slots):
            slot = col[r, k]
            used = k < count[r]
            again = jnp.bool_(False)
            for earlier in range(k):
                again = again | (col[r, earlier] == slot)
            again = again & used
            target = place_of(slot, row_blocks, flips)
            aside = unused + 1 + k
            table[r * slots + k] = jnp.where(used, jnp.where(again, aside, target), unused)
            table[pairs + 1 + repeats] = jnp.int32(r)
            table[2 * pairs + 1 + repeats] = jnp.int32(aside)
            table[3 * pairs + 1 + repeats] = target
            repeats = repeats + again.astype(jnp.int32)
    table[pairs] = repeats


def add_repeats(table, dense, pairs, block):
    def one(e, carry):
        row = table[pairs + 1 + e]
        columns = pl.ds(pl.multiple_of(row * block, block), block)
        source = pl.ds(pl.multiple_of(table[2 * pairs + 1 + e] * block, block), block)
        target = pl.ds(pl.multiple_of(table[3 * pairs + 1 + e] * block, block), block)
        dense[target, columns] = dense[target, columns] + dense[source, columns]
        return carry

    lax.fori_loop(0, table[pairs], one, 0)


def ready_kernel(step, explicit, *refs):
    refs = list(refs)
    day, table, field, a, b, _ = refs[:6]
    refs = refs[6:]
    source = refs.pop(0) if explicit else None
    dense, partial = refs
    row_blocks, slots, block, _ = a.shape
    now = day[step]
    early = (DAYS - now).astype(jnp.float32) * (1.0 / DAYS)
    late = now.astype(jnp.float32) * (1.0 / DAYS)
    for r in range(row_blocks):
        for k in range(slots):
            rows = pl.ds(pl.multiple_of(table[r * slots + k] * block, block), block)
            dense[rows, pl.ds(r * block, block)] = blended(a[r, k], b[r, k], early, late)
    add_repeats(table, dense, row_blocks * slots, block)
    total = jnp.dot(field[...], dense[pl.ds(0, field.shape[1]), :], preferred_element_type=jnp.float32)
    partial[...] = total + source[...] if explicit else total


def finish_kernel(last, wet, send, partial, dense, c_in, o_in, z_in, y_in, out, *refs):
    tracers, points = partial.shape
    block = c_in.shape[1]
    row_blocks = points // block
    halo = jnp.concatenate([h[...] for h in (c_in, o_in, z_in, y_in)], 1)
    total = partial[...] + jnp.dot(
        halo, dense[pl.ds(points, DIRECTIONS * block), :], preferred_element_type=jnp.float32
    )
    lane = lax.broadcasted_iota(jnp.int32, (tracers, block), 1)
    target = refs[0] if last else out
    for r in range(row_blocks):
        columns = slice(r * block, (r + 1) * block)
        target[:, columns] = jnp.where(lane < wet[r], total[:, columns], 0.0).astype(target.dtype)
    if last:
        copy = pltpu.make_async_copy(target, out, refs[1])
        copy.start()
        copy.wait()
        return
    flips = my_flips()
    for n, outgoing in enumerate(refs):
        row = send[direction_of(n, flips)]
        outgoing[...] = out[:, pl.ds(pl.multiple_of(row * block, block), block)]


def on_device(swaps, tracer, source, exp_a, exp_b, imp_a, imp_b, col_index, block_count, send_list, wet_rows, month_day):
    tracers, points = tracer.shape
    row_blocks, slots = col_index.shape
    block = points // row_blocks
    half, full, whole = jnp.bfloat16, jnp.float32, jnp.int32
    hbm = pl.BlockSpec(memory_space=pltpu.HBM)
    vmem = pl.BlockSpec(memory_space=pltpu.VMEM)
    smem = pl.BlockSpec(memory_space=pltpu.SMEM)
    params = pltpu.CompilerParams(vmem_limit_bytes=32 * 1024 * 1024)
    shape = jax.ShapeDtypeStruct
    piece = shape((tracers, block), half)
    field_shape = shape((tracers, points), half)
    partial_shape = shape((tracers, points), full)
    dense_shape = shape(((row_blocks + DIRECTIONS + 1 + slots) * block, points), half)
    dma = pltpu.SemaphoreType.DMA

    def stay(*arrays):
        return [pltpu.with_memory_space_constraint(x, pltpu.HBM) for x in arrays]

    indices = [wet_rows, send_list.reshape(DIRECTIONS), col_index, block_count, month_day]
    *outgoing, field, dense, forcing, wet, send, col, count, day = pl.pallas_call(
        prologue_kernel,
        out_shape=[piece] * DIRECTIONS
        + [field_shape, dense_shape, partial_shape]
        + [pltpu.SMEM(x.shape, whole) for x in indices],
        in_specs=[hbm] * 7,
        out_specs=[vmem] * (DIRECTIONS + 3) + [smem] * 5,
        scratch_shapes=[pltpu.VMEM((tracers, points), full), dma((7,))],
        compiler_params=params,
        name="prologue",
    )(*stay(tracer, *indices, source))

    table = pl.pallas_call(
        make_table,
        out_shape=pltpu.SMEM((4 * row_blocks * slots + 1,), whole),
        in_specs=[smem] * 2 + [hbm] * 2,
        out_specs=smem,
        compiler_params=params,
        name="make_table",
    )(col, count, *stay(exp_a, exp_b))

    def ready(step, explicit, field, dense):
        a, b = (exp_a, exp_b) if explicit else (imp_a, imp_b)
        operands = [day, table, field, a, b, dense] + ([forcing] if explicit else [])
        return pl.pallas_call(
            functools.partial(ready_kernel, step, explicit),
            out_shape=[dense_shape, partial_shape],
            in_specs=[smem] * 2 + [vmem] * (len(operands) - 2),
            out_specs=[vmem] * 2,
            input_output_aliases={5: 0},
            compiler_params=params,
            name="ready",
        )(*operands)

    def finish(last, partial, dense, halos):
        return pl.pallas_call(
            functools.partial(finish_kernel, last),
            out_shape=[partial_shape] if last else [field_shape] + [piece] * DIRECTIONS,
            in_specs=[smem] * 2 + [vmem] * (2 + DIRECTIONS),
            out_specs=[hbm] if last else [vmem] * (1 + DIRECTIONS),
            scratch_shapes=[pltpu.VMEM((tracers, points), full), dma(())] if last else [],
            compiler_params=params,
            name="finish",
        )(wet, send, partial, dense, *halos)

    for step in range(STEPS):
        for explicit in (True, False):
            halos = [lax.ppermute(p, ("groups", "rows"), s) for p, s in zip(outgoing, swaps)]
            dense, partial = ready(step, explicit, field, dense)
            last = step == STEPS - 1 and not explicit
            field, *outgoing = finish(last, partial, dense, halos)
    return field


def solution(mesh):
    count, groups = mesh.shape["rows"], mesh.shape["groups"]
    swaps = [swap_pairs(count, groups, stride, parity) for stride in (1, STRIDE) for parity in (0, 1)]
    wide = P("groups", "rows")
    rows = P("rows")
    return jax.shard_map(
        functools.partial(on_device, swaps),
        mesh=mesh,
        in_specs=(wide, wide, rows, rows, rows, rows, rows, rows, rows, rows, P()),
        out_specs=wide,
        check_vma=False,
    )
```

time: 36.8 us -> 27.7 us (0.75)
  local copies, waits for them, and re-layouts: 6.22 us -> 0.02 us
  Pallas kernels: 12.7 us -> 10 us
  waiting for transfers between devices: 2.15 us -> 0.81 us
  starting transfers between devices: 15.2 us -> 16.5 us
    unnamed x29 -> x8, local copies, waits for them, and re-layouts: 6.22 us -> 0.02 us
    pallas_call x9 -> x10, Pallas kernels: 12.7 us -> 10 us  [the longest x4 6.78 us: ready(): pl.pallas_call(functools.partial(ready_kernel, step, explicit), out_shape...]
    ppermute x16, waiting for transfers between devices: 2.15 us -> 0.81 us  [on_device(): lax.ppermute(p, ('groups', 'rows'), s)]
    ppermute x16, starting transfers between devices: 15.2 us -> 16.5 us  [on_device(): lax.ppermute(p, ('groups', 'rows'), s)]
  transfers between devices with their start and end apart: 16 -> 16, of which waited for: 3 -> 3; matrix products, arithmetic and copies ran while one was open for 0% -> 0% of each run, Pallas kernels for 15% -> 25%
where the time goes in v3:
time: 27.7 us; the launch traced here: 27.5 us
  starting transfers between devices  16.5 us (60%)
  Pallas kernels  10 us (36%)
  waiting for transfers between devices  0.81 us (3%)
    ppermute x16, starting transfers between devices, on_device(): lax.ppermute(p, ('groups', 'rows'), s)  16.5 us
    pallas_call x4, Pallas kernels, ready(): pl.pallas_call(functools.partial(ready_kernel, step, explicit), out_shape...  6.78 us
    pallas_call x4, Pallas kernels, finish(): pl.pallas_call(functools.partial(finish_kernel, last), out_shape=[partial...  1.98 us
    pallas_call x1, Pallas kernels, on_device(): pl.pallas_call(prologue_kernel, out_shape=[piece] * DIRECTIONS + [field_s...  1.26 us
    ppermute x16, waiting for transfers between devices, on_device(): lax.ppermute(p, ('groups', 'rows'), s)  0.81 us
  transfers between devices with their start and end apart: 16, of which 3 were waited for; matrix products, arithmetic and copies ran while one was open for 0% of the time, Pallas kernels for 25%

profile of v3, /device:TPU:0, one launch (start us, length us, event | category | flops | bytes accessed | tf_op | source)
XLA Modules:
  0.0 27.5 jit_solution(12914237908149198237)
XLA Ops:
  0.0 0.0 copy-start.1
  0.0 0.0 copy-start
  0.0 1.3 %prologue.1 = (bf16[64,128]{1,0:T(8,128)(2,1)S(1)}, bf16[64,128]{1,0:T(8,128)(2,1)S(1)}, bf16[64,128]{1,0:T(8,128)(2,1)S(1)}, bf16[64,128]{1,0:T(8,128)(2,1)S(1)...) custom-call(f32[64,1024]{1,0:T(8,128)} %tracer.1, ...), custom_call_target="tpu_custom_call" | custom-call | tf_op jit(solution)/shard_map/prologue/pallas_call | solution.py:184
  1.3 0.5 %collective-permute-start = (bf16[64,128]{1,0:T(8,128)(2,1)S(1)}, bf16[64,128]{1,0:T(8,128)(2,1)S(1)}, u32[]{:S(2)}, u32[]{:S(2)}) collective-permute-start(bf16[64,128]{1,0:T(8,128)(2,1)S(1)} %get-tuple-element.50), channel_id=1, source_target_pairs={{0,1},{1,0},{2,3},{3,2},{4,5},{5,4},{6,7},{7,6},{8,9},{9,8},{10,11... | collective-permute-start | bytes 49160 | tf_op jit(solution)/shard_map/ppermute | solution.py:231
  1.8 2.6 %collective-permute-start.1 = (bf16[64,128]{1,0:T(8,128)(2,1)S(1)}, bf16[64,128]{1,0:T(8,128)(2,1)S(1)}, u32[]{:S(2)}, u32[]{:S(2)}) collective-permute-start(bf16[64,128]{1,0:T(8,128)(2,1)S(1)} %get-tuple-element.51), channel_id=1, source_target_pairs={{0,16},{1,2},{2,1},{3,4},{4,3},{5,6},{6,5},{7,8},{8,7},{9,10},{10,... | collective-permute-start | bytes 49160 | tf_op jit(solution)/shard_map/ppermute | solution.py:231
  4.4 1.5 %collective-permute-start.2 = (bf16[64,128]{1,0:T(8,128)(2,1)S(1)}, bf16[64,128]{1,0:T(8,128)(2,1)S(1)}, u32[]{:S(2)}, u32[]{:S(2)}) collective-permute-start(bf16[64,128]{1,0:T(8,128)(2,1)S(1)} %get-tuple-element.52), channel_id=1, source_target_pairs={{0,4},{1,5},{2,6},{3,7},{4,0},{5,1},{6,2},{7,3},{8,12},{9,13},{10,... | collective-permute-start | bytes 49160 | tf_op jit(solution)/shard_map/ppermute | solution.py:231
  5.9 0.0 collective-permute-start.3
  5.9 0.0 copy-done.1
  5.9 0.0 copy-done
  5.9 0.0 copy-start.2
  5.9 0.0 copy-start.3
  5.9 1.7 %ready.4 = (bf16[2688,1024]{1,0:T(8,128)(2,1)S(1)}, f32[64,1024]{1,0:T(8,128)S(1)}) custom-call(s32[2]{0:T(128)S(4)} %get-tuple-element.42.refs_0_, s32[257]{0:T(512)S(4)} %make_table.1.refs_1_, bf16[64,1024]{1,0:T(8,128)(2,1)S(1)} %get-tuple-element.45.refs_2_, bf16[8,8,128,128]{3,2,1,0:T(8,128)(2,1)S(1)} %copy-done, ...), custom_call_target="tpu_custom_call", output_to_operand_aliasing={{0}: (5, {})} | custom-call | tf_op jit(solution)/shard_map/ready/pallas_call | solution.py:208
  7.6 0.0 collective-permute-done.c_in
  7.6 0.0 collective-permute-done.1.o_in
  7.6 0.4 %collective-permute-done.2.z_in = bf16[64,128]{1,0:T(8,128)(2,1)S(1)} collective-permute-done((bf16[64,128]{1,0:T(8,128)(2,1)S(1)}, bf16[64,128]{1,0:T(8,128)(2,1)S(1)}, u32[]{:S(2)}, u32[]{:S(2)}) %collective-permute-start.2) | collective-permute-done | bytes 16416 | tf_op jit(solution)/shard_map/ppermute | solution.py:231
  8.1 0.0 collective-permute-done.3.y_in
  8.1 0.3 %finish.4 = (bf16[64,1024]{1,0:T(8,128)(2,1)S(1)}, bf16[64,128]{1,0:T(8,128)(2,1)S(1)}, bf16[64,128]{1,0:T(8,128)(2,1)S(1)}, bf16[64,128]{1,0:T(8,128)(2,1)S(1)}, bf16[64,128]{1,0:T(8,128)(2,1)S(1)}) custom-call(s32[8]{0:T(128)S(4)} %get-tuple-element.40.wet, s32[4]{0:T(128)S(4)} %get-tuple-element.41.send, f32[64,1024]{1,0:T(8,128)S(1)} %get-tuple-element.48.partial, ...), custom_call_target="tpu_custom_call" | custom-call | tf_op jit(solution)/shard_map/finish/pallas_call | solution.py:219
  8.4 0.1 collective-permute-start.4
  8.6 1.5 %collective-permute-start.5 = (bf16[64,128]{1,0:T(8,128)(2,1)S(1)}, bf16[64,128]{1,0:T(8,128)(2,1)S(1)}, u32[]{:S(2)}, u32[]{:S(2)}) collective-permute-start(bf16[64,128]{1,0:T(8,128)(2,1)S(1)} %get-tuple-element.58), channel_id=1, source_target_pairs={{0,16},{1,2},{2,1},{3,4},{4,3},{5,6},{6,5},{7,8},{8,7},{9,10},{10,... | collective-permute-start | bytes 49160 | tf_op jit(solution)/shard_map/ppermute | solution.py:231
  10.0 1.3 %collective-permute-start.6 = (bf16[64,128]{1,0:T(8,128)(2,1)S(1)}, bf16[64,128]{1,0:T(8,128)(2,1)S(1)}, u32[]{:S(2)}, u32[]{:S(2)}) collective-permute-start(bf16[64,128]{1,0:T(8,128)(2,1)S(1)} %get-tuple-element.59), channel_id=1, source_target_pairs={{0,4},{1,5},{2,6},{3,7},{4,0},{5,1},{6,2},{7,3},{8,12},{9,13},{10,... | collective-permute-start | bytes 49160 | tf_op jit(solution)/shard_map/ppermute | solution.py:231
  11.3 0.9 %collective-permute-start.7 = (bf16[64,128]{1,0:T(8,128)(2,1)S(1)}, bf16[64,128]{1,0:T(8,128)(2,1)S(1)}, u32[]{:S(2)}, u32[]{:S(2)}) collective-permute-start(bf16[64,128]{1,0:T(8,128)(2,1)S(1)} %get-tuple-element.60), channel_id=1, source_target_pairs={{0,1},{1,0},{2,3},{3,2},{4,8},{5,9},{6,10},{7,11},{8,4},{9,5},{10,... | collective-permute-start | bytes 49160 | tf_op jit(solution)/shard_map/ppermute | solution.py:231
  12.2 0.0 copy-done.2
  12.2 0.0 copy-done.3
  12.2 1.7 %ready.5 = (bf16[2688,1024]{1,0:T(8,128)(2,1)S(1)}, f32[64,1024]{1,0:T(8,128)S(1)}) custom-call(s32[2]{0:T(128)S(4)} %get-tuple-element.42.refs_0_, s32[257]{0:T(512)S(4)} %make_table.1.refs_1_, bf16[64,1024]{1,0:T(8,128)(2,1)S(1)} %get-tuple-element.54.refs_2_, bf16[8,8,128,128]{3,2,1,0:T(8,128)(2,1)S(1)} %copy-done.2, ...), custom_call_target="tpu_custom_call", output_to_operand_aliasing={{0}: (5, {})} | custom-call | tf_op jit(solution)/shard_map/ready/pallas_call | solution.py:208
  13.9 0.0 collective-permute-done.4.c_in
  13.9 0.0 collective-permute-done.5.o_in
  13.9 0.0 collective-permute-done.6.z_in
  14.0 0.0 collective-permute-done.7.y_in
  14.0 0.3 %finish.5 = (bf16[64,1024]{1,0:T(8,128)(2,1)S(1)}, bf16[64,128]{1,0:T(8,128)(2,1)S(1)}, bf16[64,128]{1,0:T(8,128)(2,1)S(1)}, bf16[64,128]{1,0:T(8,128)(2,1)S(1)}, bf16[64,128]{1,0:T(8,128)(2,1)S(1)}) custom-call(s32[8]{0:T(128)S(4)} %get-tuple-element.40.wet, s32[4]{0:T(128)S(4)} %get-tuple-element.41.send, f32[64,1024]{1,0:T(8,128)S(1)} %get-tuple-element.55.partial, ...), custom_call_target="tpu_custom_call" | custom-call | tf_op jit(solution)/shard_map/finish/pallas_call | solution.py:219
  14.3 0.1 collective-permute-start.8
  14.4 1.1 %collective-permute-start.9 = (bf16[64,128]{1,0:T(8,128)(2,1)S(1)}, bf16[64,128]{1,0:T(8,128)(2,1)S(1)}, u32[]{:S(2)}, u32[]{:S(2)}) collective-permute-start(bf16[64,128]{1,0:T(8,128)(2,1)S(1)} %get-tuple-element.65), channel_id=1, source_target_pairs={{0,16},{1,2},{2,1},{3,4},{4,3},{5,6},{6,5},{7,8},{8,7},{9,10},{10,... | collective-permute-start | bytes 49160 | tf_op jit(solution)/shard_map/ppermute | solution.py:231
  15.5 2.7 %collective-permute-start.10 = (bf16[64,128]{1,0:T(8,128)(2,1)S(1)}, bf16[64,128]{1,0:T(8,128)(2,1)S(1)}, u32[]{:S(2)}, u32[]{:S(2)}) collective-permute-start(bf16[64,128]{1,0:T(8,128)(2,1)S(1)} %get-tuple-element.66), channel_id=1, source_target_pairs={{0,4},{1,5},{2,6},{3,7},{4,0},{5,1},{6,2},{7,3},{8,12},{9,13},{10,... | collective-permute-start | bytes 49160 | tf_op jit(solution)/shard_map/ppermute | solution.py:231
  18.2 0.0 collective-permute-start.11
  18.2 1.7 %ready.6 = (bf16[2688,1024]{1,0:T(8,128)(2,1)S(1)}, f32[64,1024]{1,0:T(8,128)S(1)}) custom-call(s32[2]{0:T(128)S(4)} %get-tuple-element.42.refs_0_, s32[257]{0:T(512)S(4)} %make_table.1.refs_1_, bf16[64,1024]{1,0:T(8,128)(2,1)S(1)} %get-tuple-element.61.refs_2_, bf16[8,8,128,128]{3,2,1,0:T(8,128)(2,1)S(1)} %copy-done, ...), custom_call_target="tpu_custom_call", output_to_operand_aliasing={{0}: (5, {})} | custom-call | tf_op jit(solution)/shard_map/ready/pallas_call | solution.py:208
  19.9 0.0 collective-permute-done.8.c_in
  19.9 0.0 collective-permute-done.9.o_in
  19.9 0.2 collective-permute-done.10.z_in
  20.1 0.0 collective-permute-done.11.y_in
  20.1 0.3 %finish.6 = (bf16[64,1024]{1,0:T(8,128)(2,1)S(1)}, bf16[64,128]{1,0:T(8,128)(2,1)S(1)}, bf16[64,128]{1,0:T(8,128)(2,1)S(1)}, bf16[64,128]{1,0:T(8,128)(2,1)S(1)}, bf16[64,128]{1,0:T(8,128)(2,1)S(1)}) custom-call(s32[8]{0:T(128)S(4)} %get-tuple-element.40.wet, s32[4]{0:T(128)S(4)} %get-tuple-element.41.send, f32[64,1024]{1,0:T(8,128)S(1)} %get-tuple-element.62.partial, ...), custom_call_target="tpu_custom_call" | custom-call | tf_op jit(solution)/shard_map/finish/pallas_call | solution.py:219
  20.4 0.4 %collective-permute-start.12 = (bf16[64,128]{1,0:T(8,128)(2,1)S(1)}, bf16[64,128]{1,0:T(8,128)(2,1)S(1)}, u32[]{:S(2)}, u32[]{:S(2)}) collective-permute-start(bf16[64,128]{1,0:T(8,128)(2,1)S(1)} %get-tuple-element.71), channel_id=1, source_target_pairs={{0,1},{1,0},{2,3},{3,2},{4,5},{5,4},{6,7},{7,6},{8,9},{9,8},{10,11... | collective-permute-start | bytes 49160 | tf_op jit(solution)/shard_map/ppermute | solution.py:231
  20.9 1.5 %collective-permute-start.13 = (bf16[64,128]{1,0:T(8,128)(2,1)S(1)}, bf16[64,128]{1,0:T(8,128)(2,1)S(1)}, u32[]{:S(2)}, u32[]{:S(2)}) collective-permute-start(bf16[64,128]{1,0:T(8,128)(2,1)S(1)} %get-tuple-element.72), channel_id=1, source_target_pairs={{0,16},{1,2},{2,1},{3,4},{4,3},{5,6},{6,5},{7,8},{8,7},{9,10},{10,... | collective-permute-start | bytes 49160 | tf_op jit(solution)/shard_map/ppermute | solution.py:231
  22.4 2.2 %collective-permute-start.14 = (bf16[64,128]{1,0:T(8,128)(2,1)S(1)}, bf16[64,128]{1,0:T(8,128)(2,1)S(1)}, u32[]{:S(2)}, u32[]{:S(2)}) collective-permute-start(bf16[64,128]{1,0:T(8,128)(2,1)S(1)} %get-tuple-element.73), channel_id=1, source_target_pairs={{0,4},{1,5},{2,6},{3,7},{4,0},{5,1},{6,2},{7,3},{8,12},{9,13},{10,... | collective-permute-start | bytes 49160 | tf_op jit(solution)/shard_map/ppermute | solution.py:231
  24.6 0.0 collective-permute-start.15
  24.6 1.7 %ready.7 = (bf16[2688,1024]{1,0:T(8,128)(2,1)S(1)}, f32[64,1024]{1,0:T(8,128)S(1)}) custom-call(s32[2]{0:T(128)S(4)} %get-tuple-element.42.refs_0_, s32[257]{0:T(512)S(4)} %make_table.1.refs_1_, bf16[64,1024]{1,0:T(8,128)(2,1)S(1)} %get-tuple-element.68.refs_2_, bf16[8,8,128,128]{3,2,1,0:T(8,128)(2,1)S(1)} %copy-done.2, ...), custom_call_target="tpu_custom_call", output_to_operand_aliasing={{0}: (5, {})} | custom-call | tf_op jit(solution)/shard_map/ready/pallas_call | solution.py:208
  26.3 0.0 collective-permute-done.12.c_in
  26.3 0.0 collective-permute-done.13.o_in
  26.3 0.2 collective-permute-done.14.z_in
  26.4 0.0 collective-permute-done.15.y_in
  26.5 1.0 %finish.7 = f32[64,1024]{1,0:T(8,128)} custom-call(s32[8]{0:T(128)S(4)} %get-tuple-element.40.wet, s32[4]{0:T(128)S(4)} %get-tuple-element.41.send, f32[64,1024]{1,0:T(8,128)S(1)} %get-tuple-element.69.partial, bf16[2688,1024]{1,0:T(8,128)(2,1)S(1)} %get-tuple-element.70.dense, bf16[64,128]{1,0:T(8,128)(2,1)S(1)} %collective-permute-done.12.c_in, ...), custom_call_target="tpu_custom_call" | custom-call | tf_op jit(solution)/shard_map/finish/pallas_call | solution.py:219
  (1 shorter events, 0.0 us)
Async XLA Ops:
  0.0 5.9 %copy-start.1 = (bf16[8,8,128,128]{3,2,1,0:T(8,128)(2,1)S(1)}, bf16[8,8,128,128]{3,2,1,0:T(8,128)(2,1)}, u32[]{:S(2)}) copy-start(bf16[8,8,128,128]{3,2,1,0:T(8,128)(2,1)} %refs_4_.6) | copy-start | bytes 6291460
  0.0 5.9 %copy-start = (bf16[8,8,128,128]{3,2,1,0:T(8,128)(2,1)S(1)}, bf16[8,8,128,128]{3,2,1,0:T(8,128)(2,1)}, u32[]{:S(2)}) copy-start(bf16[8,8,128,128]{3,2,1,0:T(8,128)(2,1)} %refs_3_.6) | copy-start | bytes 6291460
  1.3 6.4 %collective-permute-start = (bf16[64,128]{1,0:T(8,128)(2,1)S(1)}, bf16[64,128]{1,0:T(8,128)(2,1)S(1)}, u32[]{:S(2)}, u32[]{:S(2)}) collective-permute-start(bf16[64,128]{1,0:T(8,128)(2,1)S(1)} %get-tuple-element.50), channel_id=1, source_target_pairs={{0,1},{1,0},{2,3},{3,2},{4,5},{5,4},{6,7},{7,6},{8,9},{9,8},{10,11... | collective-permute-start | bytes 49160 | tf_op jit(solution)/shard_map/ppermute | solution.py:231
  1.8 5.8 %collective-permute-start.1 = (bf16[64,128]{1,0:T(8,128)(2,1)S(1)}, bf16[64,128]{1,0:T(8,128)(2,1)S(1)}, u32[]{:S(2)}, u32[]{:S(2)}) collective-permute-start(bf16[64,128]{1,0:T(8,128)(2,1)S(1)} %get-tuple-element.51), channel_id=1, source_target_pairs={{0,16},{1,2},{2,1},{3,4},{4,3},{5,6},{6,5},{7,8},{8,7},{9,10},{10,... | collective-permute-start | bytes 49160 | tf_op jit(solution)/shard_map/ppermute | solution.py:231
  4.4 3.7 %collective-permute-start.2 = (bf16[64,128]{1,0:T(8,128)(2,1)S(1)}, bf16[64,128]{1,0:T(8,128)(2,1)S(1)}, u32[]{:S(2)}, u32[]{:S(2)}) collective-permute-start(bf16[64,128]{1,0:T(8,128)(2,1)S(1)} %get-tuple-element.52), channel_id=1, source_target_pairs={{0,4},{1,5},{2,6},{3,7},{4,0},{5,1},{6,2},{7,3},{8,12},{9,13},{10,... | collective-permute-start | bytes 49160 | tf_op jit(solution)/shard_map/ppermute | solution.py:231
  5.9 2.2 %collective-permute-start.3 = (bf16[64,128]{1,0:T(8,128)(2,1)S(1)}, bf16[64,128]{1,0:T(8,128)(2,1)S(1)}, u32[]{:S(2)}, u32[]{:S(2)}) collective-permute-start(bf16[64,128]{1,0:T(8,128)(2,1)S(1)} %get-tuple-element.53), channel_id=1, source_target_pairs={{0,1},{1,0},{2,3},{3,2},{4,8},{5,9},{6,10},{7,11},{8,4},{9,5},{10,... | collective-permute-start | bytes 49160 | tf_op jit(solution)/shard_map/ppermute | solution.py:231
  5.9 6.3 %copy-start.2 = (bf16[8,8,128,128]{3,2,1,0:T(8,128)(2,1)S(1)}, bf16[8,8,128,128]{3,2,1,0:T(8,128)(2,1)}, u32[]{:S(2)}) copy-start(bf16[8,8,128,128]{3,2,1,0:T(8,128)(2,1)} %refs_3_.7) | copy-start | bytes 6291460
  5.9 6.3 %copy-start.3 = (bf16[8,8,128,128]{3,2,1,0:T(8,128)(2,1)S(1)}, bf16[8,8,128,128]{3,2,1,0:T(8,128)(2,1)}, u32[]{:S(2)}) copy-start(bf16[8,8,128,128]{3,2,1,0:T(8,128)(2,1)} %refs_4_.7) | copy-start | bytes 6291460
  8.4 5.5 %collective-permute-start.4 = (bf16[64,128]{1,0:T(8,128)(2,1)S(1)}, bf16[64,128]{1,0:T(8,128)(2,1)S(1)}, u32[]{:S(2)}, u32[]{:S(2)}) collective-permute-start(bf16[64,128]{1,0:T(8,128)(2,1)S(1)} %get-tuple-element.57), channel_id=1, source_target_pairs={{0,1},{1,0},{2,3},{3,2},{4,5},{5,4},{6,7},{7,6},{8,9},{9,8},{10,11... | collective-permute-start | bytes 49160 | tf_op jit(solution)/shard_map/ppermute | solution.py:231
  8.6 5.4 %collective-permute-start.5 = (bf16[64,128]{1,0:T(8,128)(2,1)S(1)}, bf16[64,128]{1,0:T(8,128)(2,1)S(1)}, u32[]{:S(2)}, u32[]{:S(2)}) collective-permute-start(bf16[64,128]{1,0:T(8,128)(2,1)S(1)} %get-tuple-element.58), channel_id=1, source_target_pairs={{0,16},{1,2},{2,1},{3,4},{4,3},{5,6},{6,5},{7,8},{8,7},{9,10},{10,... | collective-permute-start | bytes 49160 | tf_op jit(solution)/shard_map/ppermute | solution.py:231
  10.0 3.9 %collective-permute-start.6 = (bf16[64,128]{1,0:T(8,128)(2,1)S(1)}, bf16[64,128]{1,0:T(8,128)(2,1)S(1)}, u32[]{:S(2)}, u32[]{:S(2)}) collective-permute-start(bf16[64,128]{1,0:T(8,128)(2,1)S(1)} %get-tuple-element.59), channel_id=1, source_target_pairs={{0,4},{1,5},{2,6},{3,7},{4,0},{5,1},{6,2},{7,3},{8,12},{9,13},{10,... | collective-permute-start | bytes 49160 | tf_op jit(solution)/shard_map/ppermute | solution.py:231
  11.3 2.6 %collective-permute-start.7 = (bf16[64,128]{1,0:T(8,128)(2,1)S(1)}, bf16[64,128]{1,0:T(8,128)(2,1)S(1)}, u32[]{:S(2)}, u32[]{:S(2)}) collective-permute-start(bf16[64,128]{1,0:T(8,128)(2,1)S(1)} %get-tuple-element.60), channel_id=1, source_target_pairs={{0,1},{1,0},{2,3},{3,2},{4,8},{5,9},{6,10},{7,11},{8,4},{9,5},{10,... | collective-permute-start | bytes 49160 | tf_op jit(solution)/shard_map/ppermute | solution.py:231
  14.3 5.6 %collective-permute-start.8 = (bf16[64,128]{1,0:T(8,128)(2,1)S(1)}, bf16[64,128]{1,0:T(8,128)(2,1)S(1)}, u32[]{:S(2)}, u32[]{:S(2)}) collective-permute-start(bf16[64,128]{1,0:T(8,128)(2,1)S(1)} %get-tuple-element.64), channel_id=1, source_target_pairs={{0,1},{1,0},{2,3},{3,2},{4,5},{5,4},{6,7},{7,6},{8,9},{9,8},{10,11... | collective-permute-start | bytes 49160 | tf_op jit(solution)/shard_map/ppermute | solution.py:231
  14.4 5.6 %collective-permute-start.9 = (bf16[64,128]{1,0:T(8,128)(2,1)S(1)}, bf16[64,128]{1,0:T(8,128)(2,1)S(1)}, u32[]{:S(2)}, u32[]{:S(2)}) collective-permute-start(bf16[64,128]{1,0:T(8,128)(2,1)S(1)} %get-tuple-element.65), channel_id=1, source_target_pairs={{0,16},{1,2},{2,1},{3,4},{4,3},{5,6},{6,5},{7,8},{8,7},{9,10},{10,... | collective-permute-start | bytes 49160 | tf_op jit(solution)/shard_map/ppermute | solution.py:231
  15.5 4.6 %collective-permute-start.10 = (bf16[64,128]{1,0:T(8,128)(2,1)S(1)}, bf16[64,128]{1,0:T(8,128)(2,1)S(1)}, u32[]{:S(2)}, u32[]{:S(2)}) collective-permute-start(bf16[64,128]{1,0:T(8,128)(2,1)S(1)} %get-tuple-element.66), channel_id=1, source_target_pairs={{0,4},{1,5},{2,6},{3,7},{4,0},{5,1},{6,2},{7,3},{8,12},{9,13},{10,... | collective-permute-start | bytes 49160 | tf_op jit(solution)/shard_map/ppermute | solution.py:231
  18.2 1.9 %collective-permute-start.11 = (bf16[64,128]{1,0:T(8,128)(2,1)S(1)}, bf16[64,128]{1,0:T(8,128)(2,1)S(1)}, u32[]{:S(2)}, u32[]{:S(2)}) collective-permute-start(bf16[64,128]{1,0:T(8,128)(2,1)S(1)} %get-tuple-element.67), channel_id=1, source_target_pairs={{0,1},{1,0},{2,3},{3,2},{4,8},{5,9},{6,10},{7,11},{8,4},{9,5},{10,... | collective-permute-start | bytes 49160 | tf_op jit(solution)/shard_map/ppermute | solution.py:231
  20.4 5.8 %collective-permute-start.12 = (bf16[64,128]{1,0:T(8,128)(2,1)S(1)}, bf16[64,128]{1,0:T(8,128)(2,1)S(1)}, u32[]{:S(2)}, u32[]{:S(2)}) collective-permute-start(bf16[64,128]{1,0:T(8,128)(2,1)S(1)} %get-tuple-element.71), channel_id=1, source_target_pairs={{0,1},{1,0},{2,3},{3,2},{4,5},{5,4},{6,7},{7,6},{8,9},{9,8},{10,11... | collective-permute-start | bytes 49160 | tf_op jit(solution)/shard_map/ppermute | solution.py:231
  20.9 5.4 %collective-permute-start.13 = (bf16[64,128]{1,0:T(8,128)(2,1)S(1)}, bf16[64,128]{1,0:T(8,128)(2,1)S(1)}, u32[]{:S(2)}, u32[]{:S(2)}) collective-permute-start(bf16[64,128]{1,0:T(8,128)(2,1)S(1)} %get-tuple-element.72), channel_id=1, source_target_pairs={{0,16},{1,2},{2,1},{3,4},{4,3},{5,6},{6,5},{7,8},{8,7},{9,10},{10,... | collective-permute-start | bytes 49160 | tf_op jit(solution)/shard_map/ppermute | solution.py:231
  22.4 4.1 %collective-permute-start.14 = (bf16[64,128]{1,0:T(8,128)(2,1)S(1)}, bf16[64,128]{1,0:T(8,128)(2,1)S(1)}, u32[]{:S(2)}, u32[]{:S(2)}) collective-permute-start(bf16[64,128]{1,0:T(8,128)(2,1)S(1)} %get-tuple-element.73), channel_id=1, source_target_pairs={{0,4},{1,5},{2,6},{3,7},{4,0},{5,1},{6,2},{7,3},{8,12},{9,13},{10,... | collective-permute-start | bytes 49160 | tf_op jit(solution)/shard_map/ppermute | solution.py:231
  24.6 1.9 %collective-permute-start.15 = (bf16[64,128]{1,0:T(8,128)(2,1)S(1)}, bf16[64,128]{1,0:T(8,128)(2,1)S(1)}, u32[]{:S(2)}, u32[]{:S(2)}) collective-permute-start(bf16[64,128]{1,0:T(8,128)(2,1)S(1)} %get-tuple-element.74), channel_id=1, source_target_pairs={{0,1},{1,0},{2,3},{3,2},{4,8},{5,9},{6,10},{7,11},{8,4},{9,5},{10,... | collective-permute-start | bytes 49160 | tf_op jit(solution)/shard_map/ppermute | solution.py:231

commit v4 on v3

v4 whole, which is shorter than its diff:
```python
import functools

import jax
import jax.numpy as jnp
from jax import lax
from jax.experimental import pallas as pl
from jax.experimental.pallas import tpu as pltpu
from jax.sharding import PartitionSpec as P

STEPS = 2
DAYS = 30
STRIDE = 4
DIRECTIONS = 4
GROUP = 3
PARTS = 2
AHEAD = (0, 4, 4, 4, 0)
SWAPS = ((1, 1), (STRIDE, 0), (STRIDE, 1), (1, 0))


def swap_pairs(count, groups, stride, parity):
    partner = {}
    for i in range(count - stride):
        if (i // stride) % 2 == parity:
            partner[i], partner[i + stride] = i + stride, i
    idle = [i for i in range(count) if i not in partner]
    for i in idle:
        if i ^ 1 in idle:
            partner[i] = i ^ 1
    pairs = []
    for g in range(groups):
        for i in range(count):
            if i in partner:
                pairs.append((g * count + i, g * count + partner[i]))
            else:
                other = g ^ 1 if g ^ 1 < groups else g
                pairs.append((g * count + i, other * count + i))
    return pairs


def direction_of(swap):
    stride, parity = SWAPS[swap]
    up = (lax.axis_index("rows") // stride) % 2 == parity
    return jnp.where(up, 0, 1) + (0 if stride == 1 else 2)


def halo_places(row_blocks):
    places = []
    for direction in range(DIRECTIONS):
        stride = 1 if direction < 2 else STRIDE
        mine = (lax.axis_index("rows") // stride) % 2
        parity = mine if direction % 2 else 1 - mine
        even, odd = (row_blocks + SWAPS.index((stride, p)) for p in (0, 1))
        places.append(jnp.where(parity == 0, even, odd))
    return places


def place_of(slot, row_blocks, halos):
    place = slot
    for direction in range(DIRECTIONS):
        place = jnp.where(slot == row_blocks + direction, halos[direction], place)
    return place


def prologue_kernel(
    tracer, wet_in, send_in, col_in, count_in, day_in, source,
    out_0, out_1, out_2, out_3, field, dense, later, forcing, wet, send, col, count, day,
    raw, sems,
):
    tracers, points = raw.shape
    row_blocks = wet.shape[0]
    block = points // row_blocks
    pairs = ((tracer, raw), (wet_in, wet), (send_in, send), (col_in, col), (count_in, count), (day_in, day), (source, forcing))
    copies = [pltpu.make_async_copy(a, b, sems.at[n]) for n, (a, b) in enumerate(pairs)]
    for copy in copies:
        copy.start()
    used = (row_blocks + DIRECTIONS) * block
    for empty in (dense, later):
        empty[pl.ds(0, used), :] = jnp.zeros((used, points), empty.dtype)
    for copy in copies[:-1]:
        copy.wait()
    lane = lax.broadcasted_iota(jnp.int32, (tracers, block), 1)
    for n, out in enumerate((out_0, out_1, out_2, out_3)):
        row = send[direction_of(n)]
        piece = raw[:, pl.ds(pl.multiple_of(row * block, block), block)]
        out[...] = jnp.where(lane < wet[row], piece, 0.0).astype(out.dtype)
    for r in range(row_blocks):
        columns = pl.ds(r * block, block)
        field[:, columns] = jnp.where(lane < wet[r], raw[:, columns], 0.0).astype(field.dtype)
    copies[-1].wait()


def blended(a, b, early, late):
    mixed = early * a.astype(jnp.float32) + late * b.astype(jnp.float32)
    return mixed.astype(a.dtype).T


def make_table(col, count, _a, _b, _c, _d, table):
    row_blocks, slots = col.shape
    pairs = row_blocks * slots
    halos = halo_places(row_blocks)
    unused = row_blocks + DIRECTIONS
    seconds, others = jnp.int32(0), jnp.int32(0)

    def append(length, first, entry):
        for n, value in enumerate(entry):
            table[(first + n) * pairs + 2 + length] = value

    for r in range(row_blocks):
        known = []
        for k in range(slots):
            slot = col[r, k]
            used = k < count[r]
            aside = unused + 1 + k
            again, rest, later = jnp.bool_(False), jnp.int32(aside), jnp.bool_(False)
            for slot_before, again_before, rest_before in known:
                same = slot_before == slot
                again = again | same
                later = later | (same & again_before)
                rest = jnp.where(same & again_before, rest_before, rest)
            again, later = again & used, later & used
            known.append((slot, again, rest))
            target = place_of(slot, row_blocks, halos)
            table[r * slots + k] = jnp.where(used, jnp.where(again, aside, target), unused)
            entry = (jnp.int32(r), jnp.int32(aside), target)
            append(seconds, 1, entry)
            append(others, 4, (*entry, rest))
            seconds = seconds + (again & ~later).astype(jnp.int32)
            others = others + later.astype(jnp.int32)
    table[pairs] = seconds
    table[pairs + 1] = others
    for n in range(GROUP - 1):
        append(seconds + n, 1, (jnp.int32(0), jnp.int32(unused), jnp.int32(unused)))


def add_repeats(table, dense, pairs, block):
    size = block // PARTS
    parts = range(0, block, size)

    def entry(first, length, e):
        row, *places = [table[(first + n) * pairs + 2 + e] for n in range(length)]
        columns = pl.ds(pl.multiple_of(row * block, block), block)
        return [[(pl.ds(pl.multiple_of(p * block + part, size), size), columns) for p in places] for part in parts]

    def added(*places):
        total = dense[places[0]].astype(jnp.float32)
        for place in places[1:]:
            total = total + dense[place].astype(jnp.float32)
        rounded = total.astype(dense.dtype)
        return rounded, (total - rounded.astype(jnp.float32)).astype(dense.dtype)

    def group(g, carry):
        for entries in zip(*[entry(1, 3, g * GROUP + n) for n in range(GROUP)]):
            sums = [added(target, aside) for aside, target in entries]
            for (aside, target), (rounded, rest) in zip(entries, sums):
                dense[target] = rounded
                dense[aside] = rest
        return carry

    def one(e, carry):
        for aside, target, kept in entry(4, 4, e):
            rounded, rest = added(target, aside, kept)
            dense[target] = rounded
            dense[kept] = rest
        return carry

    lax.fori_loop(0, (table[pairs] + GROUP - 1) // GROUP, group, 0)
    lax.fori_loop(0, table[pairs + 1], one, 0)


def month_weights(day, step):
    now = day[step]
    return (DAYS - now).astype(jnp.float32) * (1.0 / DAYS), now.astype(jnp.float32) * (1.0 / DAYS)


def lay_out(a, b, weights, table, dense, rows):
    slots, block = a.shape[1:3]
    for r in rows:
        for k in range(slots):
            place = pl.ds(pl.multiple_of(table[r * slots + k] * block, block), block)
            dense[place, pl.ds(r * block, block)] = blended(a[r, k], b[r, k], *weights)


def ready_kernel(apply, *refs):
    refs = list(refs)
    explicit, more = apply % 2 == 0, apply + 1 < 2 * STEPS
    day, table, field, a, b, dense = [refs.pop(0) for _ in range(6)]
    next_a, next_b, _ = [refs.pop(0) for _ in range(3)] if more else (None, None, None)
    forcing = refs.pop(0) if explicit else None
    dense, partial = refs[:2]
    row_blocks, slots, block, _ = a.shape
    done, ahead = [row_blocks * share // 8 for share in (AHEAD[apply], AHEAD[apply + 1])]
    lay_out(a, b, month_weights(day, apply // 2), table, dense, range(done, row_blocks))
    add_repeats(table, dense, row_blocks * slots, block)
    total = jnp.dot(field[...], dense[pl.ds(0, field.shape[1]), :], preferred_element_type=jnp.float32)
    partial[...] = total + forcing[...] if explicit else total
    if more:
        lay_out(next_a, next_b, month_weights(day, (apply + 1) // 2), table, refs[2], range(ahead))


def finish_kernel(last, wet, send, partial, dense, in_0, in_1, in_2, in_3, out, *refs):
    tracers, points = partial.shape
    block = in_0.shape[1]
    row_blocks = points // block
    halo = jnp.concatenate([h[...] for h in (in_0, in_1, in_2, in_3)], 1)
    total = partial[...] + jnp.dot(
        halo, dense[pl.ds(points, DIRECTIONS * block), :], preferred_element_type=jnp.float32
    )
    lane = lax.broadcasted_iota(jnp.int32, (tracers, block), 1)
    target = refs[0] if last else out
    for r in range(row_blocks):
        columns = slice(r * block, (r + 1) * block)
        target[:, columns] = jnp.where(lane < wet[r], total[:, columns], 0.0).astype(target.dtype)
    if last:
        copy = pltpu.make_async_copy(target, out, refs[1])
        copy.start()
        copy.wait()
        return
    for n, outgoing in enumerate(refs):
        row = send[direction_of(n)]
        outgoing[...] = out[:, pl.ds(pl.multiple_of(row * block, block), block)]


def on_device(swaps, tracer, source, exp_a, exp_b, imp_a, imp_b, col_index, block_count, send_list, wet_rows, month_day):
    tracers, points = tracer.shape
    row_blocks, slots = col_index.shape
    block = points // row_blocks
    half, full, whole = jnp.bfloat16, jnp.float32, jnp.int32
    hbm = pl.BlockSpec(memory_space=pltpu.HBM)
    vmem = pl.BlockSpec(memory_space=pltpu.VMEM)
    smem = pl.BlockSpec(memory_space=pltpu.SMEM)
    params = pltpu.CompilerParams(vmem_limit_bytes=32 * 1024 * 1024)
    shape = jax.ShapeDtypeStruct
    piece = shape((tracers, block), half)
    field_shape = shape((tracers, points), half)
    partial_shape = shape((tracers, points), full)
    dense_shape = shape(((row_blocks + DIRECTIONS + 1 + slots) * block, points), half)
    dma = pltpu.SemaphoreType.DMA

    def stay(*arrays):
        return [pltpu.with_memory_space_constraint(x, pltpu.HBM) for x in arrays]

    indices = [wet_rows, send_list.reshape(DIRECTIONS), col_index, block_count, month_day]
    *outgoing, field, dense, later, forcing, wet, send, col, count, day = pl.pallas_call(
        prologue_kernel,
        out_shape=[piece] * DIRECTIONS
        + [field_shape, dense_shape, dense_shape, partial_shape]
        + [pltpu.SMEM(x.shape, whole) for x in indices],
        in_specs=[hbm] * 7,
        out_specs=[vmem] * (DIRECTIONS + 4) + [smem] * 5,
        scratch_shapes=[pltpu.VMEM((tracers, points), full), dma((7,))],
        compiler_params=params,
        name="prologue",
    )(*stay(tracer, *indices, source))

    table = pl.pallas_call(
        make_table,
        out_shape=pltpu.SMEM((8 * row_blocks * slots + 2,), whole),
        in_specs=[smem] * 2 + [hbm] * 4,
        out_specs=smem,
        compiler_params=params,
        name="make_table",
    )(col, count, *stay(exp_a, exp_b, imp_a, imp_b))

    def ready(apply, field, dense, later):
        explicit, more = apply % 2 == 0, apply + 1 < 2 * STEPS
        mine, other = ((exp_a, exp_b), (imp_a, imp_b))[:: 1 if explicit else -1]
        operands = [day, table, field, *mine, dense]
        aliases = {5: 0}
        if more:
            operands += [*other, later]
            aliases[8] = 2
        if explicit:
            operands.append(forcing)
        return pl.pallas_call(
            functools.partial(ready_kernel, apply),
            out_shape=[dense_shape, partial_shape] + [dense_shape] * more,
            in_specs=[smem] * 2 + [vmem] * (len(operands) - 2),
            out_specs=[vmem] * (2 + more),
            input_output_aliases=aliases,
            compiler_params=params,
            name="ready",
        )(*operands)

    def finish(last, partial, dense, halos):
        return pl.pallas_call(
            functools.partial(finish_kernel, last),
            out_shape=[partial_shape] if last else [field_shape] + [piece] * DIRECTIONS,
            in_specs=[smem] * 2 + [vmem] * (2 + DIRECTIONS),
            out_specs=[hbm] if last else [vmem] * (1 + DIRECTIONS),
            scratch_shapes=[pltpu.VMEM((tracers, points), full), dma(())] if last else [],
            compiler_params=params,
            name="finish",
        )(wet, send, partial, dense, *halos)

    for apply in range(2 * STEPS):
        halos = [lax.ppermute(p, ("groups", "rows"), s) for p, s in zip(outgoing, swaps)]
        dense, partial, *begun = ready(apply, field, dense, later)
        field, *outgoing = finish(apply + 1 == 2 * STEPS, partial, dense, halos)
        dense, later = begun[0] if begun else None, dense
    return field


def solution(mesh):
    count, groups = mesh.shape["rows"], mesh.shape["groups"]
    swaps = [swap_pairs(count, groups, stride, parity) for stride, parity in SWAPS]
    wide = P("groups", "rows")
    rows = P("rows")
    return jax.shard_map(
        functools.partial(on_device, swaps),
        mesh=mesh,
        in_specs=(wide, wide, rows, rows, rows, rows, rows, rows, rows, rows, P()),
        out_specs=wide,
        check_vma=False,
    )
```

time: 27.7 us -> 26.6 us (0.960)
  waiting for transfers between devices: 0.81 us -> 0.31 us
  Pallas kernels: 10 us -> 9.57 us
  starting transfers between devices: 16.5 us -> 16.2 us
    ppermute x16, waiting for transfers between devices: 0.81 us -> 0.31 us  [on_device(): lax.ppermute(p, ('groups', 'rows'), s)]
    pallas_call x5, Pallas kernels: 6.78 us -> 6.34 us  [the longest x4 6.22 us: ready(): pl.pallas_call(functools.partial(ready_kernel, apply), out_shape=[dense_s...]
  transfers between devices with their start and end apart: 16 -> 16, of which waited for: 3 -> 2; matrix products, arithmetic and copies ran while one was open for 0% -> 0% of each run, Pallas kernels for 25% -> 24%
where the time goes in v4:
time: 26.6 us; the launch traced here: 26.3 us
  starting transfers between devices  16.2 us (61%)
  Pallas kernels  9.57 us (36%)
  waiting for transfers between devices  0.31 us (1%)
    ppermute x16, starting transfers between devices, on_device(): lax.ppermute(p, ('groups', 'rows'), s)  16.2 us
    pallas_call x4, Pallas kernels, ready(): pl.pallas_call(functools.partial(ready_kernel, apply), out_shape=[dense_s...  6.22 us
    pallas_call x4, Pallas kernels, finish(): pl.pallas_call(functools.partial(finish_kernel, last), out_shape=[partial...  1.98 us
    pallas_call x1, Pallas kernels, on_device(): pl.pallas_call(prologue_kernel, out_shape=[piece] * DIRECTIONS + [field_s...  1.26 us
  transfers between devices with their start and end apart: 16, of which 2 were waited for; matrix products, arithmetic and copies ran while one was open for 0% of the time, Pallas kernels for 24%

profile of v4, /device:TPU:0, one launch (start us, length us, event | category | flops | bytes accessed | tf_op | source)
XLA Modules:
  0.0 26.3 jit_solution(18284889535062242659)
XLA Ops:
  0.0 0.0 copy-start.1
  0.0 0.0 copy-start
  0.0 0.0 copy-start.3
  0.0 0.0 copy-start.2
  0.0 1.3 %prologue.1 = (bf16[64,128]{1,0:T(8,128)(2,1)S(1)}, bf16[64,128]{1,0:T(8,128)(2,1)S(1)}, bf16[64,128]{1,0:T(8,128)(2,1)S(1)}, bf16[64,128]{1,0:T(8,128)(2,1)S(1)...) custom-call(f32[64,1024]{1,0:T(8,128)} %tracer.1, ...), custom_call_target="tpu_custom_call" | custom-call | tf_op jit(solution)/shard_map/prologue/pallas_call | solution.py:243
  1.3 3.0 %collective-permute-start = (bf16[64,128]{1,0:T(8,128)(2,1)S(1)}, bf16[64,128]{1,0:T(8,128)(2,1)S(1)}, u32[]{:S(2)}, u32[]{:S(2)}) collective-permute-start(bf16[64,128]{1,0:T(8,128)(2,1)S(1)} %get-tuple-element.55), channel_id=1, source_target_pairs={{0,16},{1,2},{2,1},{3,4},{4,3},{5,6},{6,5},{7,8},{8,7},{9,10},{10,... | collective-permute-start | bytes 49160 | tf_op jit(solution)/shard_map/ppermute | solution.py:296
  4.3 0.9 %collective-permute-start.1 = (bf16[64,128]{1,0:T(8,128)(2,1)S(1)}, bf16[64,128]{1,0:T(8,128)(2,1)S(1)}, u32[]{:S(2)}, u32[]{:S(2)}) collective-permute-start(bf16[64,128]{1,0:T(8,128)(2,1)S(1)} %get-tuple-element.56), channel_id=1, source_target_pairs={{0,4},{1,5},{2,6},{3,7},{4,0},{5,1},{6,2},{7,3},{8,12},{9,13},{10,... | collective-permute-start | bytes 49160 | tf_op jit(solution)/shard_map/ppermute | solution.py:296
  5.2 0.5 %collective-permute-start.2 = (bf16[64,128]{1,0:T(8,128)(2,1)S(1)}, bf16[64,128]{1,0:T(8,128)(2,1)S(1)}, u32[]{:S(2)}, u32[]{:S(2)}) collective-permute-start(bf16[64,128]{1,0:T(8,128)(2,1)S(1)} %get-tuple-element.57), channel_id=1, source_target_pairs={{0,1},{1,0},{2,3},{3,2},{4,8},{5,9},{6,10},{7,11},{8,4},{9,5},{10,... | collective-permute-start | bytes 49160 | tf_op jit(solution)/shard_map/ppermute | solution.py:296
  5.7 0.0 collective-permute-start.3
  5.7 0.1 make_table.1.refs_1_
  5.9 0.0 copy-done.1
  5.9 0.0 copy-done
  5.9 0.0 copy-done.3
  5.9 0.0 copy-done.2
  5.9 2.0 %ready.4 = (bf16[2688,1024]{1,0:T(8,128)(2,1)S(1)}, f32[64,1024]{1,0:T(8,128)S(1)}, bf16[2688,1024]{1,0:T(8,128)(2,1)S(1)}) custom-call(s32[2]{0:T(128)S(4)} %get-tuple-element.46.refs_0_, s32[514]{0:T(1024)S(4)} %make_table.1.refs_1_, bf16[64,1024]{1,0:T(8,128)(2,1)S(1)} %get-tuple-element.49.refs_2_, ...), custom_call_target="tpu_custom_call", output_to_operand_aliasing={{0}: (5, {}), {2}: (8, {})} | custom-call | tf_op jit(solution)/shard_map/ready/pallas_call | solution.py:274
  7.9 0.0 collective-permute-done.in_0
  7.9 0.1 collective-permute-done.1.in_1
  8.0 0.0 collective-permute-done.2.in_2
  8.0 0.0 collective-permute-done.3.in_3
  8.0 0.3 %finish.4 = (bf16[64,1024]{1,0:T(8,128)(2,1)S(1)}, bf16[64,128]{1,0:T(8,128)(2,1)S(1)}, bf16[64,128]{1,0:T(8,128)(2,1)S(1)}, bf16[64,128]{1,0:T(8,128)(2,1)S(1)}, bf16[64,128]{1,0:T(8,128)(2,1)S(1)}) custom-call(s32[8]{0:T(128)S(4)} %get-tuple-element.44.wet, s32[4]{0:T(128)S(4)} %get-tuple-element.45.send, f32[64,1024]{1,0:T(8,128)S(1)} %get-tuple-element.53.partial, ...), custom_call_target="tpu_custom_call" | custom-call | tf_op jit(solution)/shard_map/finish/pallas_call | solution.py:285
  8.4 1.3 %collective-permute-start.4 = (bf16[64,128]{1,0:T(8,128)(2,1)S(1)}, bf16[64,128]{1,0:T(8,128)(2,1)S(1)}, u32[]{:S(2)}, u32[]{:S(2)}) collective-permute-start(bf16[64,128]{1,0:T(8,128)(2,1)S(1)} %get-tuple-element.63), channel_id=1, source_target_pairs={{0,16},{1,2},{2,1},{3,4},{4,3},{5,6},{6,5},{7,8},{8,7},{9,10},{10,... | collective-permute-start | bytes 49160 | tf_op jit(solution)/shard_map/ppermute | solution.py:296
  9.7 1.8 %collective-permute-start.5 = (bf16[64,128]{1,0:T(8,128)(2,1)S(1)}, bf16[64,128]{1,0:T(8,128)(2,1)S(1)}, u32[]{:S(2)}, u32[]{:S(2)}) collective-permute-start(bf16[64,128]{1,0:T(8,128)(2,1)S(1)} %get-tuple-element.64), channel_id=1, source_target_pairs={{0,4},{1,5},{2,6},{3,7},{4,0},{5,1},{6,2},{7,3},{8,12},{9,13},{10,... | collective-permute-start | bytes 49160 | tf_op jit(solution)/shard_map/ppermute | solution.py:296
  11.5 0.5 %collective-permute-start.6 = (bf16[64,128]{1,0:T(8,128)(2,1)S(1)}, bf16[64,128]{1,0:T(8,128)(2,1)S(1)}, u32[]{:S(2)}, u32[]{:S(2)}) collective-permute-start(bf16[64,128]{1,0:T(8,128)(2,1)S(1)} %get-tuple-element.65), channel_id=1, source_target_pairs={{0,1},{1,0},{2,3},{3,2},{4,8},{5,9},{6,10},{7,11},{8,4},{9,5},{10,... | collective-permute-start | bytes 49160 | tf_op jit(solution)/shard_map/ppermute | solution.py:296
  12.0 0.0 collective-permute-start.7
  12.0 1.5 %ready.5 = (bf16[2688,1024]{1,0:T(8,128)(2,1)S(1)}, f32[64,1024]{1,0:T(8,128)S(1)}, bf16[2688,1024]{1,0:T(8,128)(2,1)S(1)}) custom-call(s32[2]{0:T(128)S(4)} %get-tuple-element.46.refs_0_, s32[514]{0:T(1024)S(4)} %make_table.1.refs_1_, bf16[64,1024]{1,0:T(8,128)(2,1)S(1)} %get-tuple-element.59.refs_2_, ...), custom_call_target="tpu_custom_call", output_to_operand_aliasing={{0}: (5, {}), {2}: (8, {})} | custom-call | tf_op jit(solution)/shard_map/ready/pallas_call | solution.py:274
  13.5 0.0 collective-permute-done.4.in_0
  13.5 0.0 collective-permute-done.5.in_1
  13.5 0.0 collective-permute-done.6.in_2
  13.5 0.0 collective-permute-done.7.in_3
  13.5 0.3 %finish.5 = (bf16[64,1024]{1,0:T(8,128)(2,1)S(1)}, bf16[64,128]{1,0:T(8,128)(2,1)S(1)}, bf16[64,128]{1,0:T(8,128)(2,1)S(1)}, bf16[64,128]{1,0:T(8,128)(2,1)S(1)}, bf16[64,128]{1,0:T(8,128)(2,1)S(1)}) custom-call(s32[8]{0:T(128)S(4)} %get-tuple-element.44.wet, s32[4]{0:T(128)S(4)} %get-tuple-element.45.send, f32[64,1024]{1,0:T(8,128)S(1)} %get-tuple-element.61.partial, ...), custom_call_target="tpu_custom_call" | custom-call | tf_op jit(solution)/shard_map/finish/pallas_call | solution.py:285
  13.9 1.6 %collective-permute-start.8 = (bf16[64,128]{1,0:T(8,128)(2,1)S(1)}, bf16[64,128]{1,0:T(8,128)(2,1)S(1)}, u32[]{:S(2)}, u32[]{:S(2)}) collective-permute-start(bf16[64,128]{1,0:T(8,128)(2,1)S(1)} %get-tuple-element.71), channel_id=1, source_target_pairs={{0,16},{1,2},{2,1},{3,4},{4,3},{5,6},{6,5},{7,8},{8,7},{9,10},{10,... | collective-permute-start | bytes 49160 | tf_op jit(solution)/shard_map/ppermute | solution.py:296
  15.4 2.1 %collective-permute-start.9 = (bf16[64,128]{1,0:T(8,128)(2,1)S(1)}, bf16[64,128]{1,0:T(8,128)(2,1)S(1)}, u32[]{:S(2)}, u32[]{:S(2)}) collective-permute-start(bf16[64,128]{1,0:T(8,128)(2,1)S(1)} %get-tuple-element.72), channel_id=1, source_target_pairs={{0,4},{1,5},{2,6},{3,7},{4,0},{5,1},{6,2},{7,3},{8,12},{9,13},{10,... | collective-permute-start | bytes 49160 | tf_op jit(solution)/shard_map/ppermute | solution.py:296
  17.5 0.0 collective-permute-start.10
  17.5 0.5 %collective-permute-start.11 = (bf16[64,128]{1,0:T(8,128)(2,1)S(1)}, bf16[64,128]{1,0:T(8,128)(2,1)S(1)}, u32[]{:S(2)}, u32[]{:S(2)}) collective-permute-start(bf16[64,128]{1,0:T(8,128)(2,1)S(1)} %get-tuple-element.74), channel_id=1, source_target_pairs={{0,1},{1,0},{2,3},{3,2},{4,5},{5,4},{6,7},{7,6},{8,9},{9,8},{10,11... | collective-permute-start | bytes 49160 | tf_op jit(solution)/shard_map/ppermute | solution.py:296
  18.0 1.5 %ready.6 = (bf16[2688,1024]{1,0:T(8,128)(2,1)S(1)}, f32[64,1024]{1,0:T(8,128)S(1)}, bf16[2688,1024]{1,0:T(8,128)(2,1)S(1)}) custom-call(s32[2]{0:T(128)S(4)} %get-tuple-element.46.refs_0_, s32[514]{0:T(1024)S(4)} %make_table.1.refs_1_, bf16[64,1024]{1,0:T(8,128)(2,1)S(1)} %get-tuple-element.67.refs_2_, ...), custom_call_target="tpu_custom_call", output_to_operand_aliasing={{0}: (5, {}), {2}: (8, {})} | custom-call | tf_op jit(solution)/shard_map/ready/pallas_call | solution.py:274
  19.5 0.0 collective-permute-done.8.in_0
  19.5 0.0 collective-permute-done.9.in_1
  19.5 0.0 collective-permute-done.10.in_2
  19.6 0.0 collective-permute-done.11.in_3
  19.6 0.3 %finish.6 = (bf16[64,1024]{1,0:T(8,128)(2,1)S(1)}, bf16[64,128]{1,0:T(8,128)(2,1)S(1)}, bf16[64,128]{1,0:T(8,128)(2,1)S(1)}, bf16[64,128]{1,0:T(8,128)(2,1)S(1)}, bf16[64,128]{1,0:T(8,128)(2,1)S(1)}) custom-call(s32[8]{0:T(128)S(4)} %get-tuple-element.44.wet, s32[4]{0:T(128)S(4)} %get-tuple-element.45.send, f32[64,1024]{1,0:T(8,128)S(1)} %get-tuple-element.69.partial, ...), custom_call_target="tpu_custom_call" | custom-call | tf_op jit(solution)/shard_map/finish/pallas_call | solution.py:285
  19.9 1.6 %collective-permute-start.12 = (bf16[64,128]{1,0:T(8,128)(2,1)S(1)}, bf16[64,128]{1,0:T(8,128)(2,1)S(1)}, u32[]{:S(2)}, u32[]{:S(2)}) collective-permute-start(bf16[64,128]{1,0:T(8,128)(2,1)S(1)} %get-tuple-element.79), channel_id=1, source_target_pairs={{0,16},{1,2},{2,1},{3,4},{4,3},{5,6},{6,5},{7,8},{8,7},{9,10},{10,... | collective-permute-start | bytes 49160 | tf_op jit(solution)/shard_map/ppermute | solution.py:296
  21.4 1.9 %collective-permute-start.13 = (bf16[64,128]{1,0:T(8,128)(2,1)S(1)}, bf16[64,128]{1,0:T(8,128)(2,1)S(1)}, u32[]{:S(2)}, u32[]{:S(2)}) collective-permute-start(bf16[64,128]{1,0:T(8,128)(2,1)S(1)} %get-tuple-element.80), channel_id=1, source_target_pairs={{0,4},{1,5},{2,6},{3,7},{4,0},{5,1},{6,2},{7,3},{8,12},{9,13},{10,... | collective-permute-start | bytes 49160 | tf_op jit(solution)/shard_map/ppermute | solution.py:296
  23.4 0.0 collective-permute-start.14
  23.4 0.5 %collective-permute-start.15 = (bf16[64,128]{1,0:T(8,128)(2,1)S(1)}, bf16[64,128]{1,0:T(8,128)(2,1)S(1)}, u32[]{:S(2)}, u32[]{:S(2)}) collective-permute-start(bf16[64,128]{1,0:T(8,128)(2,1)S(1)} %get-tuple-element.82), channel_id=1, source_target_pairs={{0,1},{1,0},{2,3},{3,2},{4,5},{5,4},{6,7},{7,6},{8,9},{9,8},{10,11... | collective-permute-start | bytes 49160 | tf_op jit(solution)/shard_map/ppermute | solution.py:296
  23.9 1.3 %ready.7 = (bf16[2688,1024]{1,0:T(8,128)(2,1)S(1)}, f32[64,1024]{1,0:T(8,128)S(1)}) custom-call(s32[2]{0:T(128)S(4)} %get-tuple-element.46.refs_0_, s32[514]{0:T(1024)S(4)} %make_table.1.refs_1_, bf16[64,1024]{1,0:T(8,128)(2,1)S(1)} %get-tuple-element.75.refs_2_, bf16[8,8,128,128]{3,2,1,0:T(8,128)(2,1)S(1)} %copy-done, ...), custom_call_target="tpu_custom_call", output_to_operand_aliasing={{0}: (5, {})} | custom-call | tf_op jit(solution)/shard_map/ready/pallas_call | solution.py:274
  25.2 0.0 collective-permute-done.12.in_0
  25.2 0.1 collective-permute-done.13.in_1
  25.3 0.0 collective-permute-done.14.in_2
  25.3 0.0 collective-permute-done.15.in_3
  25.3 1.0 %finish.7 = f32[64,1024]{1,0:T(8,128)} custom-call(s32[8]{0:T(128)S(4)} %get-tuple-element.44.wet, s32[4]{0:T(128)S(4)} %get-tuple-element.45.send, f32[64,1024]{1,0:T(8,128)S(1)} %get-tuple-element.77.partial, bf16[2688,1024]{1,0:T(8,128)(2,1)S(1)} %get-tuple-element.78.dense, bf16[64,128]{1,0:T(8,128)(2,1)S(1)} %collective-permute-done.12.in_0, ...), custom_call_target="tpu_custom_call" | custom-call | tf_op jit(solution)/shard_map/finish/pallas_call | solution.py:285
Async XLA Ops:
  0.0 5.9 %copy-start.1 = (bf16[8,8,128,128]{3,2,1,0:T(8,128)(2,1)S(1)}, bf16[8,8,128,128]{3,2,1,0:T(8,128)(2,1)}, u32[]{:S(2)}) copy-start(bf16[8,8,128,128]{3,2,1,0:T(8,128)(2,1)} %refs_4_.7) | copy-start | bytes 6291460
  0.0 5.9 %copy-start = (bf16[8,8,128,128]{3,2,1,0:T(8,128)(2,1)S(1)}, bf16[8,8,128,128]{3,2,1,0:T(8,128)(2,1)}, u32[]{:S(2)}) copy-start(bf16[8,8,128,128]{3,2,1,0:T(8,128)(2,1)} %refs_3_.7) | copy-start | bytes 6291460
  0.0 5.9 %copy-start.3 = (bf16[8,8,128,128]{3,2,1,0:T(8,128)(2,1)S(1)}, bf16[8,8,128,128]{3,2,1,0:T(8,128)(2,1)}, u32[]{:S(2)}) copy-start(bf16[8,8,128,128]{3,2,1,0:T(8,128)(2,1)} %refs_4_.6) | copy-start | bytes 6291460
  0.0 5.9 %copy-start.2 = (bf16[8,8,128,128]{3,2,1,0:T(8,128)(2,1)S(1)}, bf16[8,8,128,128]{3,2,1,0:T(8,128)(2,1)}, u32[]{:S(2)}) copy-start(bf16[8,8,128,128]{3,2,1,0:T(8,128)(2,1)} %refs_3_.6) | copy-start | bytes 6291460
  1.3 6.6 %collective-permute-start = (bf16[64,128]{1,0:T(8,128)(2,1)S(1)}, bf16[64,128]{1,0:T(8,128)(2,1)S(1)}, u32[]{:S(2)}, u32[]{:S(2)}) collective-permute-start(bf16[64,128]{1,0:T(8,128)(2,1)S(1)} %get-tuple-element.55), channel_id=1, source_target_pairs={{0,16},{1,2},{2,1},{3,4},{4,3},{5,6},{6,5},{7,8},{8,7},{9,10},{10,... | collective-permute-start | bytes 49160 | tf_op jit(solution)/shard_map/ppermute | solution.py:296
  4.3 3.7 %collective-permute-start.1 = (bf16[64,128]{1,0:T(8,128)(2,1)S(1)}, bf16[64,128]{1,0:T(8,128)(2,1)S(1)}, u32[]{:S(2)}, u32[]{:S(2)}) collective-permute-start(bf16[64,128]{1,0:T(8,128)(2,1)S(1)} %get-tuple-element.56), channel_id=1, source_target_pairs={{0,4},{1,5},{2,6},{3,7},{4,0},{5,1},{6,2},{7,3},{8,12},{9,13},{10,... | collective-permute-start | bytes 49160 | tf_op jit(solution)/shard_map/ppermute | solution.py:296
  5.2 2.8 %collective-permute-start.2 = (bf16[64,128]{1,0:T(8,128)(2,1)S(1)}, bf16[64,128]{1,0:T(8,128)(2,1)S(1)}, u32[]{:S(2)}, u32[]{:S(2)}) collective-permute-start(bf16[64,128]{1,0:T(8,128)(2,1)S(1)} %get-tuple-element.57), channel_id=1, source_target_pairs={{0,1},{1,0},{2,3},{3,2},{4,8},{5,9},{6,10},{7,11},{8,4},{9,5},{10,... | collective-permute-start | bytes 49160 | tf_op jit(solution)/shard_map/ppermute | solution.py:296
  5.7 2.3 %collective-permute-start.3 = (bf16[64,128]{1,0:T(8,128)(2,1)S(1)}, bf16[64,128]{1,0:T(8,128)(2,1)S(1)}, u32[]{:S(2)}, u32[]{:S(2)}) collective-permute-start(bf16[64,128]{1,0:T(8,128)(2,1)S(1)} %get-tuple-element.58), channel_id=1, source_target_pairs={{0,1},{1,0},{2,3},{3,2},{4,5},{5,4},{6,7},{7,6},{8,9},{9,8},{10,11... | collective-permute-start | bytes 49160 | tf_op jit(solution)/shard_map/ppermute | solution.py:296
  8.4 5.1 %collective-permute-start.4 = (bf16[64,128]{1,0:T(8,128)(2,1)S(1)}, bf16[64,128]{1,0:T(8,128)(2,1)S(1)}, u32[]{:S(2)}, u32[]{:S(2)}) collective-permute-start(bf16[64,128]{1,0:T(8,128)(2,1)S(1)} %get-tuple-element.63), channel_id=1, source_target_pairs={{0,16},{1,2},{2,1},{3,4},{4,3},{5,6},{6,5},{7,8},{8,7},{9,10},{10,... | collective-permute-start | bytes 49160 | tf_op jit(solution)/shard_map/ppermute | solution.py:296
  9.7 3.8 %collective-permute-start.5 = (bf16[64,128]{1,0:T(8,128)(2,1)S(1)}, bf16[64,128]{1,0:T(8,128)(2,1)S(1)}, u32[]{:S(2)}, u32[]{:S(2)}) collective-permute-start(bf16[64,128]{1,0:T(8,128)(2,1)S(1)} %get-tuple-element.64), channel_id=1, source_target_pairs={{0,4},{1,5},{2,6},{3,7},{4,0},{5,1},{6,2},{7,3},{8,12},{9,13},{10,... | collective-permute-start | bytes 49160 | tf_op jit(solution)/shard_map/ppermute | solution.py:296
  11.5 2.1 %collective-permute-start.6 = (bf16[64,128]{1,0:T(8,128)(2,1)S(1)}, bf16[64,128]{1,0:T(8,128)(2,1)S(1)}, u32[]{:S(2)}, u32[]{:S(2)}) collective-permute-start(bf16[64,128]{1,0:T(8,128)(2,1)S(1)} %get-tuple-element.65), channel_id=1, source_target_pairs={{0,1},{1,0},{2,3},{3,2},{4,8},{5,9},{6,10},{7,11},{8,4},{9,5},{10,... | collective-permute-start | bytes 49160 | tf_op jit(solution)/shard_map/ppermute | solution.py:296
  12.0 1.6 %collective-permute-start.7 = (bf16[64,128]{1,0:T(8,128)(2,1)S(1)}, bf16[64,128]{1,0:T(8,128)(2,1)S(1)}, u32[]{:S(2)}, u32[]{:S(2)}) collective-permute-start(bf16[64,128]{1,0:T(8,128)(2,1)S(1)} %get-tuple-element.66), channel_id=1, source_target_pairs={{0,1},{1,0},{2,3},{3,2},{4,5},{5,4},{6,7},{7,6},{8,9},{9,8},{10,11... | collective-permute-start | bytes 49160 | tf_op jit(solution)/shard_map/ppermute | solution.py:296
  13.9 5.6 %collective-permute-start.8 = (bf16[64,128]{1,0:T(8,128)(2,1)S(1)}, bf16[64,128]{1,0:T(8,128)(2,1)S(1)}, u32[]{:S(2)}, u32[]{:S(2)}) collective-permute-start(bf16[64,128]{1,0:T(8,128)(2,1)S(1)} %get-tuple-element.71), channel_id=1, source_target_pairs={{0,16},{1,2},{2,1},{3,4},{4,3},{5,6},{6,5},{7,8},{8,7},{9,10},{10,... | collective-permute-start | bytes 49160 | tf_op jit(solution)/shard_map/ppermute | solution.py:296
  15.4 4.1 %collective-permute-start.9 = (bf16[64,128]{1,0:T(8,128)(2,1)S(1)}, bf16[64,128]{1,0:T(8,128)(2,1)S(1)}, u32[]{:S(2)}, u32[]{:S(2)}) collective-permute-start(bf16[64,128]{1,0:T(8,128)(2,1)S(1)} %get-tuple-element.72), channel_id=1, source_target_pairs={{0,4},{1,5},{2,6},{3,7},{4,0},{5,1},{6,2},{7,3},{8,12},{9,13},{10,... | collective-permute-start | bytes 49160 | tf_op jit(solution)/shard_map/ppermute | solution.py:296
  17.5 2.0 %collective-permute-start.10 = (bf16[64,128]{1,0:T(8,128)(2,1)S(1)}, bf16[64,128]{1,0:T(8,128)(2,1)S(1)}, u32[]{:S(2)}, u32[]{:S(2)}) collective-permute-start(bf16[64,128]{1,0:T(8,128)(2,1)S(1)} %get-tuple-element.73), channel_id=1, source_target_pairs={{0,1},{1,0},{2,3},{3,2},{4,8},{5,9},{6,10},{7,11},{8,4},{9,5},{10,... | collective-permute-start | bytes 49160 | tf_op jit(solution)/shard_map/ppermute | solution.py:296
  17.5 2.0 %collective-permute-start.11 = (bf16[64,128]{1,0:T(8,128)(2,1)S(1)}, bf16[64,128]{1,0:T(8,128)(2,1)S(1)}, u32[]{:S(2)}, u32[]{:S(2)}) collective-permute-start(bf16[64,128]{1,0:T(8,128)(2,1)S(1)} %get-tuple-element.74), channel_id=1, source_target_pairs={{0,1},{1,0},{2,3},{3,2},{4,5},{5,4},{6,7},{7,6},{8,9},{9,8},{10,11... | collective-permute-start | bytes 49160 | tf_op jit(solution)/shard_map/ppermute | solution.py:296
  19.9 5.3 %collective-permute-start.12 = (bf16[64,128]{1,0:T(8,128)(2,1)S(1)}, bf16[64,128]{1,0:T(8,128)(2,1)S(1)}, u32[]{:S(2)}, u32[]{:S(2)}) collective-permute-start(bf16[64,128]{1,0:T(8,128)(2,1)S(1)} %get-tuple-element.79), channel_id=1, source_target_pairs={{0,16},{1,2},{2,1},{3,4},{4,3},{5,6},{6,5},{7,8},{8,7},{9,10},{10,... | collective-permute-start | bytes 49160 | tf_op jit(solution)/shard_map/ppermute | solution.py:296
  21.4 3.8 %collective-permute-start.13 = (bf16[64,128]{1,0:T(8,128)(2,1)S(1)}, bf16[64,128]{1,0:T(8,128)(2,1)S(1)}, u32[]{:S(2)}, u32[]{:S(2)}) collective-permute-start(bf16[64,128]{1,0:T(8,128)(2,1)S(1)} %get-tuple-element.80), channel_id=1, source_target_pairs={{0,4},{1,5},{2,6},{3,7},{4,0},{5,1},{6,2},{7,3},{8,12},{9,13},{10,... | collective-permute-start | bytes 49160 | tf_op jit(solution)/shard_map/ppermute | solution.py:296
  23.4 1.9 %collective-permute-start.14 = (bf16[64,128]{1,0:T(8,128)(2,1)S(1)}, bf16[64,128]{1,0:T(8,128)(2,1)S(1)}, u32[]{:S(2)}, u32[]{:S(2)}) collective-permute-start(bf16[64,128]{1,0:T(8,128)(2,1)S(1)} %get-tuple-element.81), channel_id=1, source_target_pairs={{0,1},{1,0},{2,3},{3,2},{4,8},{5,9},{6,10},{7,11},{8,4},{9,5},{10,... | collective-permute-start | bytes 49160 | tf_op jit(solution)/shard_map/ppermute | solution.py:296
  23.4 1.9 %collective-permute-start.15 = (bf16[64,128]{1,0:T(8,128)(2,1)S(1)}, bf16[64,128]{1,0:T(8,128)(2,1)S(1)}, u32[]{:S(2)}, u32[]{:S(2)}) collective-permute-start(bf16[64,128]{1,0:T(8,128)(2,1)S(1)} %get-tuple-element.82), channel_id=1, source_target_pairs={{0,1},{1,0},{2,3},{3,2},{4,5},{5,4},{6,7},{7,6},{8,9},{9,8},{10,11... | collective-permute-start | bytes 49160 | tf_op jit(solution)/shard_map/ppermute | solution.py:296

commit v5 on v4

--- a/solution.py
+++ b/solution.py
@@ -15,6 +15,7 @@
 PARTS = 2
 AHEAD = (0, 4, 4, 4, 0)
 SWAPS = ((1, 1), (STRIDE, 0), (STRIDE, 1), (1, 0))
+ORDERS = ((2, 0, 1, 3), (0, 1, 2, 3), (0, 1, 2, 3), (0, 1, 2, 3))
 
 
 def swap_pairs(count, groups, stride, parity):
@@ -79,7 +80,7 @@
     for copy in copies[:-1]:
         copy.wait()
     lane = lax.broadcasted_iota(jnp.int32, (tracers, block), 1)
-    for n, out in enumerate((out_0, out_1, out_2, out_3)):
+    for n, out in zip(ORDERS[0], (out_0, out_1, out_2, out_3)):
         row = send[direction_of(n)]
         piece = raw[:, pl.ds(pl.multiple_of(row * block, block), block)]
         out[...] = jnp.where(lane < wet[row], piece, 0.0).astype(out.dtype)
@@ -197,11 +198,13 @@
         lay_out(next_a, next_b, month_weights(day, (apply + 1) // 2), table, refs[2], range(ahead))
 
 
-def finish_kernel(last, wet, send, partial, dense, in_0, in_1, in_2, in_3, out, *refs):
+def finish_kernel(apply, wet, send, partial, dense, in_0, in_1, in_2, in_3, out, *refs):
     tracers, points = partial.shape
     block = in_0.shape[1]
     row_blocks = points // block
-    halo = jnp.concatenate([h[...] for h in (in_0, in_1, in_2, in_3)], 1)
+    last = apply + 1 == 2 * STEPS
+    halos = dict(zip(ORDERS[apply], (in_0, in_1, in_2, in_3)))
+    halo = jnp.concatenate([halos[n][...] for n in range(DIRECTIONS)], 1)
     total = partial[...] + jnp.dot(
         halo, dense[pl.ds(points, DIRECTIONS * block), :], preferred_element_type=jnp.float32
     )
@@ -215,7 +218,7 @@
         copy.start()
         copy.wait()
         return
-    for n, outgoing in enumerate(refs):
+    for n, outgoing in zip(ORDERS[apply + 1], refs):
         row = send[direction_of(n)]
         outgoing[...] = out[:, pl.ds(pl.multiple_of(row * block, block), block)]
 
@@ -281,9 +284,10 @@
             name="ready",
         )(*operands)
 
-    def finish(last, partial, dense, halos):
+    def finish(apply, partial, dense, halos):
+        last = apply + 1 == 2 * STEPS
         return pl.pallas_call(
-            functools.partial(finish_kernel, last),
+            functools.partial(finish_kernel, apply),
             out_shape=[partial_shape] if last else [field_shape] + [piece] * DIRECTIONS,
             in_specs=[smem] * 2 + [vmem] * (2 + DIRECTIONS),
             out_specs=[hbm] if last else [vmem] * (1 + DIRECTIONS),
@@ -293,9 +297,9 @@
         )(wet, send, partial, dense, *halos)
 
     for apply in range(2 * STEPS):
-        halos = [lax.ppermute(p, ("groups", "rows"), s) for p, s in zip(outgoing, swaps)]
+        halos = [lax.ppermute(p, ("groups", "rows"), swaps[n]) for p, n in zip(outgoing, ORDERS[apply])]
         dense, partial, *begun = ready(apply, field, dense, later)
-        field, *outgoing = finish(apply + 1 == 2 * STEPS, partial, dense, halos)
+        field, *outgoing = finish(apply, partial, dense, halos)
         dense, later = begun[0] if begun else None, dense
     return field
 

time: 26.6 us -> 26.7 us (level); the launches traced: 26.3 us -> 26.7 us
  starting transfers between devices: 16.2 us -> 14 us
  Pallas kernels: 9.57 us -> 11.2 us
  waiting for transfers between devices: 0.31 us -> 1.37 us
    ppermute x16, starting transfers between devices: 16.2 us -> 14 us  [on_device(): lax.ppermute(p, ('groups', 'rows'), swaps[n])]
    pallas_call x4, Pallas kernels: 6.22 us -> 7.91 us  [ready(): pl.pallas_call(functools.partial(ready_kernel, apply), out_shape=[dense_s...]
    ppermute x16, waiting for transfers between devices: 0.31 us -> 1.37 us  [on_device(): lax.ppermute(p, ('groups', 'rows'), swaps[n])]
  transfers between devices with their start and end apart: 16 -> 16, of which waited for: 2 -> 1; matrix products, arithmetic and copies ran while one was open for 0% -> 0% of each run, Pallas kernels for 24% -> 30%
where the time goes in v5:
time: 26.7 us
  starting transfers between devices  14 us (52%)
  Pallas kernels  11.2 us (42%)
  waiting for transfers between devices  1.37 us (5%)
    ppermute x16, starting transfers between devices, on_device(): lax.ppermute(p, ('groups', 'rows'), swaps[n])  14 us
    pallas_call x4, Pallas kernels, ready(): pl.pallas_call(functools.partial(ready_kernel, apply), out_shape=[dense_s...  7.91 us
    pallas_call x4, Pallas kernels, finish(): pl.pallas_call(functools.partial(finish_kernel, apply), out_shape=[partia...  1.98 us
    ppermute x16, waiting for transfers between devices, on_device(): lax.ppermute(p, ('groups', 'rows'), swaps[n])  1.37 us
    pallas_call x1, Pallas kernels, on_device(): pl.pallas_call(prologue_kernel, out_shape=[piece] * DIRECTIONS + [field_s...  1.26 us
  transfers between devices with their start and end apart: 16, of which 1 were waited for; matrix products, arithmetic and copies ran while one was open for 0% of the time, Pallas kernels for 30%

profile of v5, /device:TPU:0, one launch (start us, length us, event | category | flops | bytes accessed | tf_op | source)
XLA Modules:
  0.0 26.7 jit_solution(14984501852170326922)
XLA Ops:
  0.0 0.0 copy-start.1
  0.0 0.0 copy-start
  0.0 0.0 copy-start.3
  0.0 0.0 copy-start.2
  0.0 1.3 %prologue.1 = (bf16[64,128]{1,0:T(8,128)(2,1)S(1)}, bf16[64,128]{1,0:T(8,128)(2,1)S(1)}, bf16[64,128]{1,0:T(8,128)(2,1)S(1)}, bf16[64,128]{1,0:T(8,128)(2,1)S(1)...) custom-call(f32[64,1024]{1,0:T(8,128)} %tracer.1, ...), custom_call_target="tpu_custom_call" | custom-call | tf_op jit(solution)/shard_map/prologue/pallas_call | solution.py:246
  1.3 0.5 %collective-permute-start = (bf16[64,128]{1,0:T(8,128)(2,1)S(1)}, bf16[64,128]{1,0:T(8,128)(2,1)S(1)}, u32[]{:S(2)}, u32[]{:S(2)}) collective-permute-start(bf16[64,128]{1,0:T(8,128)(2,1)S(1)} %get-tuple-element.55), channel_id=1, source_target_pairs={{0,1},{1,0},{2,3},{3,2},{4,8},{5,9},{6,10},{7,11},{8,4},{9,5},{10,... | collective-permute-start | bytes 49160 | tf_op jit(solution)/shard_map/ppermute | solution.py:300
  1.8 2.6 %collective-permute-start.1 = (bf16[64,128]{1,0:T(8,128)(2,1)S(1)}, bf16[64,128]{1,0:T(8,128)(2,1)S(1)}, u32[]{:S(2)}, u32[]{:S(2)}) collective-permute-start(bf16[64,128]{1,0:T(8,128)(2,1)S(1)} %get-tuple-element.56), channel_id=1, source_target_pairs={{0,16},{1,2},{2,1},{3,4},{4,3},{5,6},{6,5},{7,8},{8,7},{9,10},{10,... | collective-permute-start | bytes 49160 | tf_op jit(solution)/shard_map/ppermute | solution.py:300
  4.4 1.6 %collective-permute-start.2 = (bf16[64,128]{1,0:T(8,128)(2,1)S(1)}, bf16[64,128]{1,0:T(8,128)(2,1)S(1)}, u32[]{:S(2)}, u32[]{:S(2)}) collective-permute-start(bf16[64,128]{1,0:T(8,128)(2,1)S(1)} %get-tuple-element.57), channel_id=1, source_target_pairs={{0,4},{1,5},{2,6},{3,7},{4,0},{5,1},{6,2},{7,3},{8,12},{9,13},{10,... | collective-permute-start | bytes 49160 | tf_op jit(solution)/shard_map/ppermute | solution.py:300
  6.0 1.4 %collective-permute-start.3 = (bf16[64,128]{1,0:T(8,128)(2,1)S(1)}, bf16[64,128]{1,0:T(8,128)(2,1)S(1)}, u32[]{:S(2)}, u32[]{:S(2)}) collective-permute-start(bf16[64,128]{1,0:T(8,128)(2,1)S(1)} %get-tuple-element.58), channel_id=1, source_target_pairs={{0,1},{1,0},{2,3},{3,2},{4,5},{5,4},{6,7},{7,6},{8,9},{9,8},{10,11... | collective-permute-start | bytes 49160 | tf_op jit(solution)/shard_map/ppermute | solution.py:300
  7.3 0.0 copy-done.1
  7.3 0.0 copy-done
  7.3 0.0 copy-done.3
  7.3 0.0 copy-done.2
  7.3 2.4 %ready.4 = (bf16[2688,1024]{1,0:T(8,128)(2,1)S(1)}, f32[64,1024]{1,0:T(8,128)S(1)}, bf16[2688,1024]{1,0:T(8,128)(2,1)S(1)}) custom-call(s32[2]{0:T(128)S(4)} %get-tuple-element.46.refs_0_, s32[514]{0:T(1024)S(4)} %make_table.1.refs_1_, bf16[64,1024]{1,0:T(8,128)(2,1)S(1)} %get-tuple-element.49.refs_2_, ...), custom_call_target="tpu_custom_call", output_to_operand_aliasing={{0}: (5, {}), {2}: (8, {})} | custom-call | tf_op jit(solution)/shard_map/ready/pallas_call | solution.py:277
  9.8 0.0 collective-permute-done.in_0
  9.8 0.0 collective-permute-done.1.in_1
  9.8 0.0 collective-permute-done.2.in_2
  9.8 0.0 collective-permute-done.3.in_3
  9.8 0.3 %finish.4 = (bf16[64,1024]{1,0:T(8,128)(2,1)S(1)}, bf16[64,128]{1,0:T(8,128)(2,1)S(1)}, bf16[64,128]{1,0:T(8,128)(2,1)S(1)}, bf16[64,128]{1,0:T(8,128)(2,1)S(1)}, bf16[64,128]{1,0:T(8,128)(2,1)S(1)}) custom-call(s32[8]{0:T(128)S(4)} %get-tuple-element.44.wet, s32[4]{0:T(128)S(4)} %get-tuple-element.45.send, f32[64,1024]{1,0:T(8,128)S(1)} %get-tuple-element.53.partial, ...), custom_call_target="tpu_custom_call" | custom-call | tf_op jit(solution)/shard_map/finish/pallas_call | solution.py:289
  10.1 1.6 %collective-permute-start.4 = (bf16[64,128]{1,0:T(8,128)(2,1)S(1)}, bf16[64,128]{1,0:T(8,128)(2,1)S(1)}, u32[]{:S(2)}, u32[]{:S(2)}) collective-permute-start(bf16[64,128]{1,0:T(8,128)(2,1)S(1)} %get-tuple-element.63), channel_id=1, source_target_pairs={{0,16},{1,2},{2,1},{3,4},{4,3},{5,6},{6,5},{7,8},{8,7},{9,10},{10,... | collective-permute-start | bytes 49160 | tf_op jit(solution)/shard_map/ppermute | solution.py:300
  11.7 0.0 collective-permute-start.5
  11.7 0.0 collective-permute-start.6
  11.7 0.5 %collective-permute-start.7 = (bf16[64,128]{1,0:T(8,128)(2,1)S(1)}, bf16[64,128]{1,0:T(8,128)(2,1)S(1)}, u32[]{:S(2)}, u32[]{:S(2)}) collective-permute-start(bf16[64,128]{1,0:T(8,128)(2,1)S(1)} %get-tuple-element.66), channel_id=1, source_target_pairs={{0,1},{1,0},{2,3},{3,2},{4,5},{5,4},{6,7},{7,6},{8,9},{9,8},{10,11... | collective-permute-start | bytes 49160 | tf_op jit(solution)/shard_map/ppermute | solution.py:300
  12.2 1.9 %ready.5 = (bf16[2688,1024]{1,0:T(8,128)(2,1)S(1)}, f32[64,1024]{1,0:T(8,128)S(1)}, bf16[2688,1024]{1,0:T(8,128)(2,1)S(1)}) custom-call(s32[2]{0:T(128)S(4)} %get-tuple-element.46.refs_0_, s32[514]{0:T(1024)S(4)} %make_table.1.refs_1_, bf16[64,1024]{1,0:T(8,128)(2,1)S(1)} %get-tuple-element.59.refs_2_, ...), custom_call_target="tpu_custom_call", output_to_operand_aliasing={{0}: (5, {}), {2}: (8, {})} | custom-call | tf_op jit(solution)/shard_map/ready/pallas_call | solution.py:277
  14.1 0.0 collective-permute-done.4.in_0
  14.1 1.3 %collective-permute-done.5.in_1 = bf16[64,128]{1,0:T(8,128)(2,1)S(1)} collective-permute-done((bf16[64,128]{1,0:T(8,128)(2,1)S(1)}, bf16[64,128]{1,0:T(8,128)(2,1)S(1)}, u32[]{:S(2)}, u32[]{:S(2)}) %collective-permute-start.5) | collective-permute-done | bytes 16416 | tf_op jit(solution)/shard_map/ppermute | solution.py:300
  15.4 0.0 collective-permute-done.6.in_2
  15.4 0.0 collective-permute-done.7.in_3
  15.4 0.3 %finish.5 = (bf16[64,1024]{1,0:T(8,128)(2,1)S(1)}, bf16[64,128]{1,0:T(8,128)(2,1)S(1)}, bf16[64,128]{1,0:T(8,128)(2,1)S(1)}, bf16[64,128]{1,0:T(8,128)(2,1)S(1)}, bf16[64,128]{1,0:T(8,128)(2,1)S(1)}) custom-call(s32[8]{0:T(128)S(4)} %get-tuple-element.44.wet, s32[4]{0:T(128)S(4)} %get-tuple-element.45.send, f32[64,1024]{1,0:T(8,128)S(1)} %get-tuple-element.61.partial, ...), custom_call_target="tpu_custom_call" | custom-call | tf_op jit(solution)/shard_map/finish/pallas_call | solution.py:289
  15.8 0.6 %collective-permute-start.8 = (bf16[64,128]{1,0:T(8,128)(2,1)S(1)}, bf16[64,128]{1,0:T(8,128)(2,1)S(1)}, u32[]{:S(2)}, u32[]{:S(2)}) collective-permute-start(bf16[64,128]{1,0:T(8,128)(2,1)S(1)} %get-tuple-element.71), channel_id=1, source_target_pairs={{0,16},{1,2},{2,1},{3,4},{4,3},{5,6},{6,5},{7,8},{8,7},{9,10},{10,... | collective-permute-start | bytes 49160 | tf_op jit(solution)/shard_map/ppermute | solution.py:300
  16.4 1.6 %collective-permute-start.9 = (bf16[64,128]{1,0:T(8,128)(2,1)S(1)}, bf16[64,128]{1,0:T(8,128)(2,1)S(1)}, u32[]{:S(2)}, u32[]{:S(2)}) collective-permute-start(bf16[64,128]{1,0:T(8,128)(2,1)S(1)} %get-tuple-element.72), channel_id=1, source_target_pairs={{0,4},{1,5},{2,6},{3,7},{4,0},{5,1},{6,2},{7,3},{8,12},{9,13},{10,... | collective-permute-start | bytes 49160 | tf_op jit(solution)/shard_map/ppermute | solution.py:300
  17.9 0.0 collective-permute-start.10
  17.9 0.5 %collective-permute-start.11 = (bf16[64,128]{1,0:T(8,128)(2,1)S(1)}, bf16[64,128]{1,0:T(8,128)(2,1)S(1)}, u32[]{:S(2)}, u32[]{:S(2)}) collective-permute-start(bf16[64,128]{1,0:T(8,128)(2,1)S(1)} %get-tuple-element.74), channel_id=1, source_target_pairs={{0,1},{1,0},{2,3},{3,2},{4,5},{5,4},{6,7},{7,6},{8,9},{9,8},{10,11... | collective-permute-start | bytes 49160 | tf_op jit(solution)/shard_map/ppermute | solution.py:300
  18.4 1.9 %ready.6 = (bf16[2688,1024]{1,0:T(8,128)(2,1)S(1)}, f32[64,1024]{1,0:T(8,128)S(1)}, bf16[2688,1024]{1,0:T(8,128)(2,1)S(1)}) custom-call(s32[2]{0:T(128)S(4)} %get-tuple-element.46.refs_0_, s32[514]{0:T(1024)S(4)} %make_table.1.refs_1_, bf16[64,1024]{1,0:T(8,128)(2,1)S(1)} %get-tuple-element.67.refs_2_, ...), custom_call_target="tpu_custom_call", output_to_operand_aliasing={{0}: (5, {}), {2}: (8, {})} | custom-call | tf_op jit(solution)/shard_map/ready/pallas_call | solution.py:277
  20.4 0.0 collective-permute-done.8.in_0
  20.4 0.0 collective-permute-done.9.in_1
  20.4 0.0 collective-permute-done.10.in_2
  20.4 0.0 collective-permute-done.11.in_3
  20.4 0.3 %finish.6 = (bf16[64,1024]{1,0:T(8,128)(2,1)S(1)}, bf16[64,128]{1,0:T(8,128)(2,1)S(1)}, bf16[64,128]{1,0:T(8,128)(2,1)S(1)}, bf16[64,128]{1,0:T(8,128)(2,1)S(1)}, bf16[64,128]{1,0:T(8,128)(2,1)S(1)}) custom-call(s32[8]{0:T(128)S(4)} %get-tuple-element.44.wet, s32[4]{0:T(128)S(4)} %get-tuple-element.45.send, f32[64,1024]{1,0:T(8,128)S(1)} %get-tuple-element.69.partial, ...), custom_call_target="tpu_custom_call" | custom-call | tf_op jit(solution)/shard_map/finish/pallas_call | solution.py:289
  20.7 1.3 %collective-permute-start.12 = (bf16[64,128]{1,0:T(8,128)(2,1)S(1)}, bf16[64,128]{1,0:T(8,128)(2,1)S(1)}, u32[]{:S(2)}, u32[]{:S(2)}) collective-permute-start(bf16[64,128]{1,0:T(8,128)(2,1)S(1)} %get-tuple-element.79), channel_id=1, source_target_pairs={{0,16},{1,2},{2,1},{3,4},{4,3},{5,6},{6,5},{7,8},{8,7},{9,10},{10,... | collective-permute-start | bytes 49160 | tf_op jit(solution)/shard_map/ppermute | solution.py:300
  22.0 1.5 %collective-permute-start.13 = (bf16[64,128]{1,0:T(8,128)(2,1)S(1)}, bf16[64,128]{1,0:T(8,128)(2,1)S(1)}, u32[]{:S(2)}, u32[]{:S(2)}) collective-permute-start(bf16[64,128]{1,0:T(8,128)(2,1)S(1)} %get-tuple-element.80), channel_id=1, source_target_pairs={{0,4},{1,5},{2,6},{3,7},{4,0},{5,1},{6,2},{7,3},{8,12},{9,13},{10,... | collective-permute-start | bytes 49160 | tf_op jit(solution)/shard_map/ppermute | solution.py:300
  23.5 0.0 collective-permute-start.14
  23.5 0.5 %collective-permute-start.15 = (bf16[64,128]{1,0:T(8,128)(2,1)S(1)}, bf16[64,128]{1,0:T(8,128)(2,1)S(1)}, u32[]{:S(2)}, u32[]{:S(2)}) collective-permute-start(bf16[64,128]{1,0:T(8,128)(2,1)S(1)} %get-tuple-element.82), channel_id=1, source_target_pairs={{0,1},{1,0},{2,3},{3,2},{4,5},{5,4},{6,7},{7,6},{8,9},{9,8},{10,11... | collective-permute-start | bytes 49160 | tf_op jit(solution)/shard_map/ppermute | solution.py:300
  24.0 1.7 %ready.7 = (bf16[2688,1024]{1,0:T(8,128)(2,1)S(1)}, f32[64,1024]{1,0:T(8,128)S(1)}) custom-call(s32[2]{0:T(128)S(4)} %get-tuple-element.46.refs_0_, s32[514]{0:T(1024)S(4)} %make_table.1.refs_1_, bf16[64,1024]{1,0:T(8,128)(2,1)S(1)} %get-tuple-element.75.refs_2_, bf16[8,8,128,128]{3,2,1,0:T(8,128)(2,1)S(1)} %copy-done, ...), custom_call_target="tpu_custom_call", output_to_operand_aliasing={{0}: (5, {})} | custom-call | tf_op jit(solution)/shard_map/ready/pallas_call | solution.py:277
  25.7 0.0 collective-permute-done.12.in_0
  25.7 0.0 collective-permute-done.13.in_1
  25.7 0.0 collective-permute-done.14.in_2
  25.7 0.0 collective-permute-done.15.in_3
  25.7 1.0 %finish.7 = f32[64,1024]{1,0:T(8,128)} custom-call(s32[8]{0:T(128)S(4)} %get-tuple-element.44.wet, s32[4]{0:T(128)S(4)} %get-tuple-element.45.send, f32[64,1024]{1,0:T(8,128)S(1)} %get-tuple-element.77.partial, bf16[2688,1024]{1,0:T(8,128)(2,1)S(1)} %get-tuple-element.78.dense, bf16[64,128]{1,0:T(8,128)(2,1)S(1)} %collective-permute-done.12.in_0, ...), custom_call_target="tpu_custom_call" | custom-call | tf_op jit(solution)/shard_map/finish/pallas_call | solution.py:289
  (1 shorter events, 0.0 us)
Async XLA Ops:
  0.0 7.3 %copy-start.1 = (bf16[8,8,128,128]{3,2,1,0:T(8,128)(2,1)S(1)}, bf16[8,8,128,128]{3,2,1,0:T(8,128)(2,1)}, u32[]{:S(2)}) copy-start(bf16[8,8,128,128]{3,2,1,0:T(8,128)(2,1)} %refs_4_.7) | copy-start | bytes 6291460
  0.0 7.3 %copy-start = (bf16[8,8,128,128]{3,2,1,0:T(8,128)(2,1)S(1)}, bf16[8,8,128,128]{3,2,1,0:T(8,128)(2,1)}, u32[]{:S(2)}) copy-start(bf16[8,8,128,128]{3,2,1,0:T(8,128)(2,1)} %refs_3_.7) | copy-start | bytes 6291460
  0.0 7.3 %copy-start.3 = (bf16[8,8,128,128]{3,2,1,0:T(8,128)(2,1)S(1)}, bf16[8,8,128,128]{3,2,1,0:T(8,128)(2,1)}, u32[]{:S(2)}) copy-start(bf16[8,8,128,128]{3,2,1,0:T(8,128)(2,1)} %refs_4_.6) | copy-start | bytes 6291460
  0.0 7.3 %copy-start.2 = (bf16[8,8,128,128]{3,2,1,0:T(8,128)(2,1)S(1)}, bf16[8,8,128,128]{3,2,1,0:T(8,128)(2,1)}, u32[]{:S(2)}) copy-start(bf16[8,8,128,128]{3,2,1,0:T(8,128)(2,1)} %refs_3_.6) | copy-start | bytes 6291460
  1.3 8.5 %collective-permute-start = (bf16[64,128]{1,0:T(8,128)(2,1)S(1)}, bf16[64,128]{1,0:T(8,128)(2,1)S(1)}, u32[]{:S(2)}, u32[]{:S(2)}) collective-permute-start(bf16[64,128]{1,0:T(8,128)(2,1)S(1)} %get-tuple-element.55), channel_id=1, source_target_pairs={{0,1},{1,0},{2,3},{3,2},{4,8},{5,9},{6,10},{7,11},{8,4},{9,5},{10,... | collective-permute-start | bytes 49160 | tf_op jit(solution)/shard_map/ppermute | solution.py:300
  1.8 8.0 %collective-permute-start.1 = (bf16[64,128]{1,0:T(8,128)(2,1)S(1)}, bf16[64,128]{1,0:T(8,128)(2,1)S(1)}, u32[]{:S(2)}, u32[]{:S(2)}) collective-permute-start(bf16[64,128]{1,0:T(8,128)(2,1)S(1)} %get-tuple-element.56), channel_id=1, source_target_pairs={{0,16},{1,2},{2,1},{3,4},{4,3},{5,6},{6,5},{7,8},{8,7},{9,10},{10,... | collective-permute-start | bytes 49160 | tf_op jit(solution)/shard_map/ppermute | solution.py:300
  4.4 5.4 %collective-permute-start.2 = (bf16[64,128]{1,0:T(8,128)(2,1)S(1)}, bf16[64,128]{1,0:T(8,128)(2,1)S(1)}, u32[]{:S(2)}, u32[]{:S(2)}) collective-permute-start(bf16[64,128]{1,0:T(8,128)(2,1)S(1)} %get-tuple-element.57), channel_id=1, source_target_pairs={{0,4},{1,5},{2,6},{3,7},{4,0},{5,1},{6,2},{7,3},{8,12},{9,13},{10,... | collective-permute-start | bytes 49160 | tf_op jit(solution)/shard_map/ppermute | solution.py:300
  6.0 3.8 %collective-permute-start.3 = (bf16[64,128]{1,0:T(8,128)(2,1)S(1)}, bf16[64,128]{1,0:T(8,128)(2,1)S(1)}, u32[]{:S(2)}, u32[]{:S(2)}) collective-permute-start(bf16[64,128]{1,0:T(8,128)(2,1)S(1)} %get-tuple-element.58), channel_id=1, source_target_pairs={{0,1},{1,0},{2,3},{3,2},{4,5},{5,4},{6,7},{7,6},{8,9},{9,8},{10,11... | collective-permute-start | bytes 49160 | tf_op jit(solution)/shard_map/ppermute | solution.py:300
  10.1 4.0 %collective-permute-start.4 = (bf16[64,128]{1,0:T(8,128)(2,1)S(1)}, bf16[64,128]{1,0:T(8,128)(2,1)S(1)}, u32[]{:S(2)}, u32[]{:S(2)}) collective-permute-start(bf16[64,128]{1,0:T(8,128)(2,1)S(1)} %get-tuple-element.63), channel_id=1, source_target_pairs={{0,16},{1,2},{2,1},{3,4},{4,3},{5,6},{6,5},{7,8},{8,7},{9,10},{10,... | collective-permute-start | bytes 49160 | tf_op jit(solution)/shard_map/ppermute | solution.py:300
  11.7 3.7 %collective-permute-start.5 = (bf16[64,128]{1,0:T(8,128)(2,1)S(1)}, bf16[64,128]{1,0:T(8,128)(2,1)S(1)}, u32[]{:S(2)}, u32[]{:S(2)}) collective-permute-start(bf16[64,128]{1,0:T(8,128)(2,1)S(1)} %get-tuple-element.64), channel_id=1, source_target_pairs={{0,4},{1,5},{2,6},{3,7},{4,0},{5,1},{6,2},{7,3},{8,12},{9,13},{10,... | collective-permute-start | bytes 49160 | tf_op jit(solution)/shard_map/ppermute | solution.py:300
  11.7 3.7 %collective-permute-start.6 = (bf16[64,128]{1,0:T(8,128)(2,1)S(1)}, bf16[64,128]{1,0:T(8,128)(2,1)S(1)}, u32[]{:S(2)}, u32[]{:S(2)}) collective-permute-start(bf16[64,128]{1,0:T(8,128)(2,1)S(1)} %get-tuple-element.65), channel_id=1, source_target_pairs={{0,1},{1,0},{2,3},{3,2},{4,8},{5,9},{6,10},{7,11},{8,4},{9,5},{10,... | collective-permute-start | bytes 49160 | tf_op jit(solution)/shard_map/ppermute | solution.py:300
  11.7 3.7 %collective-permute-start.7 = (bf16[64,128]{1,0:T(8,128)(2,1)S(1)}, bf16[64,128]{1,0:T(8,128)(2,1)S(1)}, u32[]{:S(2)}, u32[]{:S(2)}) collective-permute-start(bf16[64,128]{1,0:T(8,128)(2,1)S(1)} %get-tuple-element.66), channel_id=1, source_target_pairs={{0,1},{1,0},{2,3},{3,2},{4,5},{5,4},{6,7},{7,6},{8,9},{9,8},{10,11... | collective-permute-start | bytes 49160 | tf_op jit(solution)/shard_map/ppermute | solution.py:300
  15.8 4.6 %collective-permute-start.8 = (bf16[64,128]{1,0:T(8,128)(2,1)S(1)}, bf16[64,128]{1,0:T(8,128)(2,1)S(1)}, u32[]{:S(2)}, u32[]{:S(2)}) collective-permute-start(bf16[64,128]{1,0:T(8,128)(2,1)S(1)} %get-tuple-element.71), channel_id=1, source_target_pairs={{0,16},{1,2},{2,1},{3,4},{4,3},{5,6},{6,5},{7,8},{8,7},{9,10},{10,... | collective-permute-start | bytes 49160 | tf_op jit(solution)/shard_map/ppermute | solution.py:300
  16.4 4.0 %collective-permute-start.9 = (bf16[64,128]{1,0:T(8,128)(2,1)S(1)}, bf16[64,128]{1,0:T(8,128)(2,1)S(1)}, u32[]{:S(2)}, u32[]{:S(2)}) collective-permute-start(bf16[64,128]{1,0:T(8,128)(2,1)S(1)} %get-tuple-element.72), channel_id=1, source_target_pairs={{0,4},{1,5},{2,6},{3,7},{4,0},{5,1},{6,2},{7,3},{8,12},{9,13},{10,... | collective-permute-start | bytes 49160 | tf_op jit(solution)/shard_map/ppermute | solution.py:300
  17.9 2.5 %collective-permute-start.10 = (bf16[64,128]{1,0:T(8,128)(2,1)S(1)}, bf16[64,128]{1,0:T(8,128)(2,1)S(1)}, u32[]{:S(2)}, u32[]{:S(2)}) collective-permute-start(bf16[64,128]{1,0:T(8,128)(2,1)S(1)} %get-tuple-element.73), channel_id=1, source_target_pairs={{0,1},{1,0},{2,3},{3,2},{4,8},{5,9},{6,10},{7,11},{8,4},{9,5},{10,... | collective-permute-start | bytes 49160 | tf_op jit(solution)/shard_map/ppermute | solution.py:300
  17.9 2.5 %collective-permute-start.11 = (bf16[64,128]{1,0:T(8,128)(2,1)S(1)}, bf16[64,128]{1,0:T(8,128)(2,1)S(1)}, u32[]{:S(2)}, u32[]{:S(2)}) collective-permute-start(bf16[64,128]{1,0:T(8,128)(2,1)S(1)} %get-tuple-element.74), channel_id=1, source_target_pairs={{0,1},{1,0},{2,3},{3,2},{4,5},{5,4},{6,7},{7,6},{8,9},{9,8},{10,11... | collective-permute-start | bytes 49160 | tf_op jit(solution)/shard_map/ppermute | solution.py:300
  20.7 4.9 %collective-permute-start.12 = (bf16[64,128]{1,0:T(8,128)(2,1)S(1)}, bf16[64,128]{1,0:T(8,128)(2,1)S(1)}, u32[]{:S(2)}, u32[]{:S(2)}) collective-permute-start(bf16[64,128]{1,0:T(8,128)(2,1)S(1)} %get-tuple-element.79), channel_id=1, source_target_pairs={{0,16},{1,2},{2,1},{3,4},{4,3},{5,6},{6,5},{7,8},{8,7},{9,10},{10,... | collective-permute-start | bytes 49160 | tf_op jit(solution)/shard_map/ppermute | solution.py:300
  22.0 3.7 %collective-permute-start.13 = (bf16[64,128]{1,0:T(8,128)(2,1)S(1)}, bf16[64,128]{1,0:T(8,128)(2,1)S(1)}, u32[]{:S(2)}, u32[]{:S(2)}) collective-permute-start(bf16[64,128]{1,0:T(8,128)(2,1)S(1)} %get-tuple-element.80), channel_id=1, source_target_pairs={{0,4},{1,5},{2,6},{3,7},{4,0},{5,1},{6,2},{7,3},{8,12},{9,13},{10,... | collective-permute-start | bytes 49160 | tf_op jit(solution)/shard_map/ppermute | solution.py:300
  23.5 2.3 %collective-permute-start.14 = (bf16[64,128]{1,0:T(8,128)(2,1)S(1)}, bf16[64,128]{1,0:T(8,128)(2,1)S(1)}, u32[]{:S(2)}, u32[]{:S(2)}) collective-permute-start(bf16[64,128]{1,0:T(8,128)(2,1)S(1)} %get-tuple-element.81), channel_id=1, source_target_pairs={{0,1},{1,0},{2,3},{3,2},{4,8},{5,9},{6,10},{7,11},{8,4},{9,5},{10,... | collective-permute-start | bytes 49160 | tf_op jit(solution)/shard_map/ppermute | solution.py:300
  23.5 2.3 %collective-permute-start.15 = (bf16[64,128]{1,0:T(8,128)(2,1)S(1)}, bf16[64,128]{1,0:T(8,128)(2,1)S(1)}, u32[]{:S(2)}, u32[]{:S(2)}) collective-permute-start(bf16[64,128]{1,0:T(8,128)(2,1)S(1)} %get-tuple-element.82), channel_id=1, source_target_pairs={{0,1},{1,0},{2,3},{3,2},{4,5},{5,4},{6,7},{7,6},{8,9},{9,8},{10,11... | collective-permute-start | bytes 49160 | tf_op jit(solution)/shard_map/ppermute | solution.py:300

commit v6 on v4

--- a/solution.py
+++ b/solution.py
@@ -11,7 +11,7 @@
 DAYS = 30
 STRIDE = 4
 DIRECTIONS = 4
-GROUP = 3
+GROUP = 2
 PARTS = 2
 AHEAD = (0, 4, 4, 4, 0)
 SWAPS = ((1, 1), (STRIDE, 0), (STRIDE, 1), (1, 0))

time: 26.6 us -> 26.2 us (0.985)
  starting transfers between devices: 16.2 us -> 15.4 us
  Pallas kernels: 9.57 us -> 10 us
    ppermute x16, starting transfers between devices: 16.2 us -> 15.4 us  [on_device(): lax.ppermute(p, ('groups', 'rows'), s)]
    pallas_call x4, Pallas kernels: 6.22 us -> 6.67 us  [ready(): pl.pallas_call(functools.partial(ready_kernel, apply), out_shape=[dense_s...]
  transfers between devices with their start and end apart: 16 -> 16, of which waited for: 2 -> 1; matrix products, arithmetic and copies ran while one was open for 0% -> 0% of each run, Pallas kernels for 24% -> 26%
where the time goes in v6:
time: 26.2 us; the launch traced here: 26 us
  starting transfers between devices  15.4 us (59%)
  Pallas kernels  10 us (38%)
  waiting for transfers between devices  0.28 us (1%)
    ppermute x16, starting transfers between devices, on_device(): lax.ppermute(p, ('groups', 'rows'), s)  15.4 us
    pallas_call x4, Pallas kernels, ready(): pl.pallas_call(functools.partial(ready_kernel, apply), out_shape=[dense_s...  6.67 us
    pallas_call x4, Pallas kernels, finish(): pl.pallas_call(functools.partial(finish_kernel, last), out_shape=[partial...  1.98 us
    pallas_call x1, Pallas kernels, on_device(): pl.pallas_call(prologue_kernel, out_shape=[piece] * DIRECTIONS + [field_s...  1.26 us
  transfers between devices with their start and end apart: 16, of which 1 were waited for; matrix products, arithmetic and copies ran while one was open for 0% of the time, Pallas kernels for 26%

profile of v6, /device:TPU:0, one launch (start us, length us, event | category | flops | bytes accessed | tf_op | source)
XLA Modules:
  0.0 26.0 jit_solution(12818993257670055138)
XLA Ops:
  0.0 0.0 copy-start.1
  0.0 0.0 copy-start
  0.0 0.0 copy-start.3
  0.0 0.0 copy-start.2
  0.0 1.3 %prologue.1 = (bf16[64,128]{1,0:T(8,128)(2,1)S(1)}, bf16[64,128]{1,0:T(8,128)(2,1)S(1)}, bf16[64,128]{1,0:T(8,128)(2,1)S(1)}, bf16[64,128]{1,0:T(8,128)(2,1)S(1)...) custom-call(f32[64,1024]{1,0:T(8,128)} %tracer.1, ...), custom_call_target="tpu_custom_call" | custom-call | tf_op jit(solution)/shard_map/prologue/pallas_call | solution.py:243
  1.3 3.0 %collective-permute-start = (bf16[64,128]{1,0:T(8,128)(2,1)S(1)}, bf16[64,128]{1,0:T(8,128)(2,1)S(1)}, u32[]{:S(2)}, u32[]{:S(2)}) collective-permute-start(bf16[64,128]{1,0:T(8,128)(2,1)S(1)} %get-tuple-element.55), channel_id=1, source_target_pairs={{0,16},{1,2},{2,1},{3,4},{4,3},{5,6},{6,5},{7,8},{8,7},{9,10},{10,... | collective-permute-start | bytes 49160 | tf_op jit(solution)/shard_map/ppermute | solution.py:296
  4.3 0.9 %collective-permute-start.1 = (bf16[64,128]{1,0:T(8,128)(2,1)S(1)}, bf16[64,128]{1,0:T(8,128)(2,1)S(1)}, u32[]{:S(2)}, u32[]{:S(2)}) collective-permute-start(bf16[64,128]{1,0:T(8,128)(2,1)S(1)} %get-tuple-element.56), channel_id=1, source_target_pairs={{0,4},{1,5},{2,6},{3,7},{4,0},{5,1},{6,2},{7,3},{8,12},{9,13},{10,... | collective-permute-start | bytes 49160 | tf_op jit(solution)/shard_map/ppermute | solution.py:296
  5.2 0.5 %collective-permute-start.2 = (bf16[64,128]{1,0:T(8,128)(2,1)S(1)}, bf16[64,128]{1,0:T(8,128)(2,1)S(1)}, u32[]{:S(2)}, u32[]{:S(2)}) collective-permute-start(bf16[64,128]{1,0:T(8,128)(2,1)S(1)} %get-tuple-element.57), channel_id=1, source_target_pairs={{0,1},{1,0},{2,3},{3,2},{4,8},{5,9},{6,10},{7,11},{8,4},{9,5},{10,... | collective-permute-start | bytes 49160 | tf_op jit(solution)/shard_map/ppermute | solution.py:296
  5.7 0.0 collective-permute-start.3
  5.7 0.1 make_table.1.refs_1_
  5.9 0.0 copy-done.1
  5.9 0.0 copy-done
  5.9 0.0 copy-done.3
  5.9 0.0 copy-done.2
  5.9 2.1 %ready.4 = (bf16[2688,1024]{1,0:T(8,128)(2,1)S(1)}, f32[64,1024]{1,0:T(8,128)S(1)}, bf16[2688,1024]{1,0:T(8,128)(2,1)S(1)}) custom-call(s32[2]{0:T(128)S(4)} %get-tuple-element.46.refs_0_, s32[514]{0:T(1024)S(4)} %make_table.1.refs_1_, bf16[64,1024]{1,0:T(8,128)(2,1)S(1)} %get-tuple-element.49.refs_2_, ...), custom_call_target="tpu_custom_call", output_to_operand_aliasing={{0}: (5, {}), {2}: (8, {})} | custom-call | tf_op jit(solution)/shard_map/ready/pallas_call | solution.py:274
  8.0 0.0 collective-permute-done.in_0
  8.0 0.0 collective-permute-done.1.in_1
  8.0 0.0 collective-permute-done.2.in_2
  8.0 0.0 collective-permute-done.3.in_3
  8.1 0.3 %finish.4 = (bf16[64,1024]{1,0:T(8,128)(2,1)S(1)}, bf16[64,128]{1,0:T(8,128)(2,1)S(1)}, bf16[64,128]{1,0:T(8,128)(2,1)S(1)}, bf16[64,128]{1,0:T(8,128)(2,1)S(1)}, bf16[64,128]{1,0:T(8,128)(2,1)S(1)}) custom-call(s32[8]{0:T(128)S(4)} %get-tuple-element.44.wet, s32[4]{0:T(128)S(4)} %get-tuple-element.45.send, f32[64,1024]{1,0:T(8,128)S(1)} %get-tuple-element.53.partial, ...), custom_call_target="tpu_custom_call" | custom-call | tf_op jit(solution)/shard_map/finish/pallas_call | solution.py:285
  8.4 1.4 %collective-permute-start.4 = (bf16[64,128]{1,0:T(8,128)(2,1)S(1)}, bf16[64,128]{1,0:T(8,128)(2,1)S(1)}, u32[]{:S(2)}, u32[]{:S(2)}) collective-permute-start(bf16[64,128]{1,0:T(8,128)(2,1)S(1)} %get-tuple-element.63), channel_id=1, source_target_pairs={{0,16},{1,2},{2,1},{3,4},{4,3},{5,6},{6,5},{7,8},{8,7},{9,10},{10,... | collective-permute-start | bytes 49160 | tf_op jit(solution)/shard_map/ppermute | solution.py:296
  9.8 1.3 %collective-permute-start.5 = (bf16[64,128]{1,0:T(8,128)(2,1)S(1)}, bf16[64,128]{1,0:T(8,128)(2,1)S(1)}, u32[]{:S(2)}, u32[]{:S(2)}) collective-permute-start(bf16[64,128]{1,0:T(8,128)(2,1)S(1)} %get-tuple-element.64), channel_id=1, source_target_pairs={{0,4},{1,5},{2,6},{3,7},{4,0},{5,1},{6,2},{7,3},{8,12},{9,13},{10,... | collective-permute-start | bytes 49160 | tf_op jit(solution)/shard_map/ppermute | solution.py:296
  11.1 0.9 %collective-permute-start.6 = (bf16[64,128]{1,0:T(8,128)(2,1)S(1)}, bf16[64,128]{1,0:T(8,128)(2,1)S(1)}, u32[]{:S(2)}, u32[]{:S(2)}) collective-permute-start(bf16[64,128]{1,0:T(8,128)(2,1)S(1)} %get-tuple-element.65), channel_id=1, source_target_pairs={{0,1},{1,0},{2,3},{3,2},{4,8},{5,9},{6,10},{7,11},{8,4},{9,5},{10,... | collective-permute-start | bytes 49160 | tf_op jit(solution)/shard_map/ppermute | solution.py:296
  12.0 0.0 collective-permute-start.7
  12.0 1.6 %ready.5 = (bf16[2688,1024]{1,0:T(8,128)(2,1)S(1)}, f32[64,1024]{1,0:T(8,128)S(1)}, bf16[2688,1024]{1,0:T(8,128)(2,1)S(1)}) custom-call(s32[2]{0:T(128)S(4)} %get-tuple-element.46.refs_0_, s32[514]{0:T(1024)S(4)} %make_table.1.refs_1_, bf16[64,1024]{1,0:T(8,128)(2,1)S(1)} %get-tuple-element.59.refs_2_, ...), custom_call_target="tpu_custom_call", output_to_operand_aliasing={{0}: (5, {}), {2}: (8, {})} | custom-call | tf_op jit(solution)/shard_map/ready/pallas_call | solution.py:274
  13.6 0.0 collective-permute-done.4.in_0
  13.6 0.0 collective-permute-done.5.in_1
  13.6 0.0 collective-permute-done.6.in_2
  13.6 0.0 collective-permute-done.7.in_3
  13.6 0.3 %finish.5 = (bf16[64,1024]{1,0:T(8,128)(2,1)S(1)}, bf16[64,128]{1,0:T(8,128)(2,1)S(1)}, bf16[64,128]{1,0:T(8,128)(2,1)S(1)}, bf16[64,128]{1,0:T(8,128)(2,1)S(1)}, bf16[64,128]{1,0:T(8,128)(2,1)S(1)}) custom-call(s32[8]{0:T(128)S(4)} %get-tuple-element.44.wet, s32[4]{0:T(128)S(4)} %get-tuple-element.45.send, f32[64,1024]{1,0:T(8,128)S(1)} %get-tuple-element.61.partial, ...), custom_call_target="tpu_custom_call" | custom-call | tf_op jit(solution)/shard_map/finish/pallas_call | solution.py:285
  14.0 1.2 %collective-permute-start.8 = (bf16[64,128]{1,0:T(8,128)(2,1)S(1)}, bf16[64,128]{1,0:T(8,128)(2,1)S(1)}, u32[]{:S(2)}, u32[]{:S(2)}) collective-permute-start(bf16[64,128]{1,0:T(8,128)(2,1)S(1)} %get-tuple-element.71), channel_id=1, source_target_pairs={{0,16},{1,2},{2,1},{3,4},{4,3},{5,6},{6,5},{7,8},{8,7},{9,10},{10,... | collective-permute-start | bytes 49160 | tf_op jit(solution)/shard_map/ppermute | solution.py:296
  15.2 2.0 %collective-permute-start.9 = (bf16[64,128]{1,0:T(8,128)(2,1)S(1)}, bf16[64,128]{1,0:T(8,128)(2,1)S(1)}, u32[]{:S(2)}, u32[]{:S(2)}) collective-permute-start(bf16[64,128]{1,0:T(8,128)(2,1)S(1)} %get-tuple-element.72), channel_id=1, source_target_pairs={{0,4},{1,5},{2,6},{3,7},{4,0},{5,1},{6,2},{7,3},{8,12},{9,13},{10,... | collective-permute-start | bytes 49160 | tf_op jit(solution)/shard_map/ppermute | solution.py:296
  17.1 0.0 collective-permute-start.10
  17.1 0.5 %collective-permute-start.11 = (bf16[64,128]{1,0:T(8,128)(2,1)S(1)}, bf16[64,128]{1,0:T(8,128)(2,1)S(1)}, u32[]{:S(2)}, u32[]{:S(2)}) collective-permute-start(bf16[64,128]{1,0:T(8,128)(2,1)S(1)} %get-tuple-element.74), channel_id=1, source_target_pairs={{0,1},{1,0},{2,3},{3,2},{4,5},{5,4},{6,7},{7,6},{8,9},{9,8},{10,11... | collective-permute-start | bytes 49160 | tf_op jit(solution)/shard_map/ppermute | solution.py:296
  17.7 1.6 %ready.6 = (bf16[2688,1024]{1,0:T(8,128)(2,1)S(1)}, f32[64,1024]{1,0:T(8,128)S(1)}, bf16[2688,1024]{1,0:T(8,128)(2,1)S(1)}) custom-call(s32[2]{0:T(128)S(4)} %get-tuple-element.46.refs_0_, s32[514]{0:T(1024)S(4)} %make_table.1.refs_1_, bf16[64,1024]{1,0:T(8,128)(2,1)S(1)} %get-tuple-element.67.refs_2_, ...), custom_call_target="tpu_custom_call", output_to_operand_aliasing={{0}: (5, {}), {2}: (8, {})} | custom-call | tf_op jit(solution)/shard_map/ready/pallas_call | solution.py:274
  19.3 0.0 collective-permute-done.8.in_0
  19.3 0.0 collective-permute-done.9.in_1
  19.3 0.0 collective-permute-done.10.in_2
  19.3 0.0 collective-permute-done.11.in_3
  19.3 0.3 %finish.6 = (bf16[64,1024]{1,0:T(8,128)(2,1)S(1)}, bf16[64,128]{1,0:T(8,128)(2,1)S(1)}, bf16[64,128]{1,0:T(8,128)(2,1)S(1)}, bf16[64,128]{1,0:T(8,128)(2,1)S(1)}, bf16[64,128]{1,0:T(8,128)(2,1)S(1)}) custom-call(s32[8]{0:T(128)S(4)} %get-tuple-element.44.wet, s32[4]{0:T(128)S(4)} %get-tuple-element.45.send, f32[64,1024]{1,0:T(8,128)S(1)} %get-tuple-element.69.partial, ...), custom_call_target="tpu_custom_call" | custom-call | tf_op jit(solution)/shard_map/finish/pallas_call | solution.py:285
  19.6 1.6 %collective-permute-start.12 = (bf16[64,128]{1,0:T(8,128)(2,1)S(1)}, bf16[64,128]{1,0:T(8,128)(2,1)S(1)}, u32[]{:S(2)}, u32[]{:S(2)}) collective-permute-start(bf16[64,128]{1,0:T(8,128)(2,1)S(1)} %get-tuple-element.79), channel_id=1, source_target_pairs={{0,16},{1,2},{2,1},{3,4},{4,3},{5,6},{6,5},{7,8},{8,7},{9,10},{10,... | collective-permute-start | bytes 49160 | tf_op jit(solution)/shard_map/ppermute | solution.py:296
  21.2 1.6 %collective-permute-start.13 = (bf16[64,128]{1,0:T(8,128)(2,1)S(1)}, bf16[64,128]{1,0:T(8,128)(2,1)S(1)}, u32[]{:S(2)}, u32[]{:S(2)}) collective-permute-start(bf16[64,128]{1,0:T(8,128)(2,1)S(1)} %get-tuple-element.80), channel_id=1, source_target_pairs={{0,4},{1,5},{2,6},{3,7},{4,0},{5,1},{6,2},{7,3},{8,12},{9,13},{10,... | collective-permute-start | bytes 49160 | tf_op jit(solution)/shard_map/ppermute | solution.py:296
  22.8 0.0 collective-permute-start.14
  22.8 0.5 %collective-permute-start.15 = (bf16[64,128]{1,0:T(8,128)(2,1)S(1)}, bf16[64,128]{1,0:T(8,128)(2,1)S(1)}, u32[]{:S(2)}, u32[]{:S(2)}) collective-permute-start(bf16[64,128]{1,0:T(8,128)(2,1)S(1)} %get-tuple-element.82), channel_id=1, source_target_pairs={{0,1},{1,0},{2,3},{3,2},{4,5},{5,4},{6,7},{7,6},{8,9},{9,8},{10,11... | collective-permute-start | bytes 49160 | tf_op jit(solution)/shard_map/ppermute | solution.py:296
  23.3 1.4 %ready.7 = (bf16[2688,1024]{1,0:T(8,128)(2,1)S(1)}, f32[64,1024]{1,0:T(8,128)S(1)}) custom-call(s32[2]{0:T(128)S(4)} %get-tuple-element.46.refs_0_, s32[514]{0:T(1024)S(4)} %make_table.1.refs_1_, bf16[64,1024]{1,0:T(8,128)(2,1)S(1)} %get-tuple-element.75.refs_2_, bf16[8,8,128,128]{3,2,1,0:T(8,128)(2,1)S(1)} %copy-done, ...), custom_call_target="tpu_custom_call", output_to_operand_aliasing={{0}: (5, {})} | custom-call | tf_op jit(solution)/shard_map/ready/pallas_call | solution.py:274
  24.7 0.0 collective-permute-done.12.in_0
  24.7 0.2 collective-permute-done.13.in_1
  24.9 0.0 collective-permute-done.14.in_2
  24.9 0.0 collective-permute-done.15.in_3
  24.9 1.0 %finish.7 = f32[64,1024]{1,0:T(8,128)} custom-call(s32[8]{0:T(128)S(4)} %get-tuple-element.44.wet, s32[4]{0:T(128)S(4)} %get-tuple-element.45.send, f32[64,1024]{1,0:T(8,128)S(1)} %get-tuple-element.77.partial, bf16[2688,1024]{1,0:T(8,128)(2,1)S(1)} %get-tuple-element.78.dense, bf16[64,128]{1,0:T(8,128)(2,1)S(1)} %collective-permute-done.12.in_0, ...), custom_call_target="tpu_custom_call" | custom-call | tf_op jit(solution)/shard_map/finish/pallas_call | solution.py:285
Async XLA Ops:
  0.0 5.9 %copy-start.1 = (bf16[8,8,128,128]{3,2,1,0:T(8,128)(2,1)S(1)}, bf16[8,8,128,128]{3,2,1,0:T(8,128)(2,1)}, u32[]{:S(2)}) copy-start(bf16[8,8,128,128]{3,2,1,0:T(8,128)(2,1)} %refs_4_.7) | copy-start | bytes 6291460
  0.0 5.9 %copy-start = (bf16[8,8,128,128]{3,2,1,0:T(8,128)(2,1)S(1)}, bf16[8,8,128,128]{3,2,1,0:T(8,128)(2,1)}, u32[]{:S(2)}) copy-start(bf16[8,8,128,128]{3,2,1,0:T(8,128)(2,1)} %refs_3_.7) | copy-start | bytes 6291460
  0.0 5.9 %copy-start.3 = (bf16[8,8,128,128]{3,2,1,0:T(8,128)(2,1)S(1)}, bf16[8,8,128,128]{3,2,1,0:T(8,128)(2,1)}, u32[]{:S(2)}) copy-start(bf16[8,8,128,128]{3,2,1,0:T(8,128)(2,1)} %refs_4_.6) | copy-start | bytes 6291460
  0.0 5.9 %copy-start.2 = (bf16[8,8,128,128]{3,2,1,0:T(8,128)(2,1)S(1)}, bf16[8,8,128,128]{3,2,1,0:T(8,128)(2,1)}, u32[]{:S(2)}) copy-start(bf16[8,8,128,128]{3,2,1,0:T(8,128)(2,1)} %refs_3_.6) | copy-start | bytes 6291460
  1.3 6.7 %collective-permute-start = (bf16[64,128]{1,0:T(8,128)(2,1)S(1)}, bf16[64,128]{1,0:T(8,128)(2,1)S(1)}, u32[]{:S(2)}, u32[]{:S(2)}) collective-permute-start(bf16[64,128]{1,0:T(8,128)(2,1)S(1)} %get-tuple-element.55), channel_id=1, source_target_pairs={{0,16},{1,2},{2,1},{3,4},{4,3},{5,6},{6,5},{7,8},{8,7},{9,10},{10,... | collective-permute-start | bytes 49160 | tf_op jit(solution)/shard_map/ppermute | solution.py:296
  4.3 3.7 %collective-permute-start.1 = (bf16[64,128]{1,0:T(8,128)(2,1)S(1)}, bf16[64,128]{1,0:T(8,128)(2,1)S(1)}, u32[]{:S(2)}, u32[]{:S(2)}) collective-permute-start(bf16[64,128]{1,0:T(8,128)(2,1)S(1)} %get-tuple-element.56), channel_id=1, source_target_pairs={{0,4},{1,5},{2,6},{3,7},{4,0},{5,1},{6,2},{7,3},{8,12},{9,13},{10,... | collective-permute-start | bytes 49160 | tf_op jit(solution)/shard_map/ppermute | solution.py:296
  5.2 2.8 %collective-permute-start.2 = (bf16[64,128]{1,0:T(8,128)(2,1)S(1)}, bf16[64,128]{1,0:T(8,128)(2,1)S(1)}, u32[]{:S(2)}, u32[]{:S(2)}) collective-permute-start(bf16[64,128]{1,0:T(8,128)(2,1)S(1)} %get-tuple-element.57), channel_id=1, source_target_pairs={{0,1},{1,0},{2,3},{3,2},{4,8},{5,9},{6,10},{7,11},{8,4},{9,5},{10,... | collective-permute-start | bytes 49160 | tf_op jit(solution)/shard_map/ppermute | solution.py:296
  5.7 2.3 %collective-permute-start.3 = (bf16[64,128]{1,0:T(8,128)(2,1)S(1)}, bf16[64,128]{1,0:T(8,128)(2,1)S(1)}, u32[]{:S(2)}, u32[]{:S(2)}) collective-permute-start(bf16[64,128]{1,0:T(8,128)(2,1)S(1)} %get-tuple-element.58), channel_id=1, source_target_pairs={{0,1},{1,0},{2,3},{3,2},{4,5},{5,4},{6,7},{7,6},{8,9},{9,8},{10,11... | collective-permute-start | bytes 49160 | tf_op jit(solution)/shard_map/ppermute | solution.py:296
  8.4 5.2 %collective-permute-start.4 = (bf16[64,128]{1,0:T(8,128)(2,1)S(1)}, bf16[64,128]{1,0:T(8,128)(2,1)S(1)}, u32[]{:S(2)}, u32[]{:S(2)}) collective-permute-start(bf16[64,128]{1,0:T(8,128)(2,1)S(1)} %get-tuple-element.63), channel_id=1, source_target_pairs={{0,16},{1,2},{2,1},{3,4},{4,3},{5,6},{6,5},{7,8},{8,7},{9,10},{10,... | collective-permute-start | bytes 49160 | tf_op jit(solution)/shard_map/ppermute | solution.py:296
  9.8 3.8 %collective-permute-start.5 = (bf16[64,128]{1,0:T(8,128)(2,1)S(1)}, bf16[64,128]{1,0:T(8,128)(2,1)S(1)}, u32[]{:S(2)}, u32[]{:S(2)}) collective-permute-start(bf16[64,128]{1,0:T(8,128)(2,1)S(1)} %get-tuple-element.64), channel_id=1, source_target_pairs={{0,4},{1,5},{2,6},{3,7},{4,0},{5,1},{6,2},{7,3},{8,12},{9,13},{10,... | collective-permute-start | bytes 49160 | tf_op jit(solution)/shard_map/ppermute | solution.py:296
  11.1 2.5 %collective-permute-start.6 = (bf16[64,128]{1,0:T(8,128)(2,1)S(1)}, bf16[64,128]{1,0:T(8,128)(2,1)S(1)}, u32[]{:S(2)}, u32[]{:S(2)}) collective-permute-start(bf16[64,128]{1,0:T(8,128)(2,1)S(1)} %get-tuple-element.65), channel_id=1, source_target_pairs={{0,1},{1,0},{2,3},{3,2},{4,8},{5,9},{6,10},{7,11},{8,4},{9,5},{10,... | collective-permute-start | bytes 49160 | tf_op jit(solution)/shard_map/ppermute | solution.py:296
  12.0 1.6 %collective-permute-start.7 = (bf16[64,128]{1,0:T(8,128)(2,1)S(1)}, bf16[64,128]{1,0:T(8,128)(2,1)S(1)}, u32[]{:S(2)}, u32[]{:S(2)}) collective-permute-start(bf16[64,128]{1,0:T(8,128)(2,1)S(1)} %get-tuple-element.66), channel_id=1, source_target_pairs={{0,1},{1,0},{2,3},{3,2},{4,5},{5,4},{6,7},{7,6},{8,9},{9,8},{10,11... | collective-permute-start | bytes 49160 | tf_op jit(solution)/shard_map/ppermute | solution.py:296
  14.0 5.3 %collective-permute-start.8 = (bf16[64,128]{1,0:T(8,128)(2,1)S(1)}, bf16[64,128]{1,0:T(8,128)(2,1)S(1)}, u32[]{:S(2)}, u32[]{:S(2)}) collective-permute-start(bf16[64,128]{1,0:T(8,128)(2,1)S(1)} %get-tuple-element.71), channel_id=1, source_target_pairs={{0,16},{1,2},{2,1},{3,4},{4,3},{5,6},{6,5},{7,8},{8,7},{9,10},{10,... | collective-permute-start | bytes 49160 | tf_op jit(solution)/shard_map/ppermute | solution.py:296
  15.2 4.1 %collective-permute-start.9 = (bf16[64,128]{1,0:T(8,128)(2,1)S(1)}, bf16[64,128]{1,0:T(8,128)(2,1)S(1)}, u32[]{:S(2)}, u32[]{:S(2)}) collective-permute-start(bf16[64,128]{1,0:T(8,128)(2,1)S(1)} %get-tuple-element.72), channel_id=1, source_target_pairs={{0,4},{1,5},{2,6},{3,7},{4,0},{5,1},{6,2},{7,3},{8,12},{9,13},{10,... | collective-permute-start | bytes 49160 | tf_op jit(solution)/shard_map/ppermute | solution.py:296
  17.1 2.1 %collective-permute-start.10 = (bf16[64,128]{1,0:T(8,128)(2,1)S(1)}, bf16[64,128]{1,0:T(8,128)(2,1)S(1)}, u32[]{:S(2)}, u32[]{:S(2)}) collective-permute-start(bf16[64,128]{1,0:T(8,128)(2,1)S(1)} %get-tuple-element.73), channel_id=1, source_target_pairs={{0,1},{1,0},{2,3},{3,2},{4,8},{5,9},{6,10},{7,11},{8,4},{9,5},{10,... | collective-permute-start | bytes 49160 | tf_op jit(solution)/shard_map/ppermute | solution.py:296
  17.1 2.2 %collective-permute-start.11 = (bf16[64,128]{1,0:T(8,128)(2,1)S(1)}, bf16[64,128]{1,0:T(8,128)(2,1)S(1)}, u32[]{:S(2)}, u32[]{:S(2)}) collective-permute-start(bf16[64,128]{1,0:T(8,128)(2,1)S(1)} %get-tuple-element.74), channel_id=1, source_target_pairs={{0,1},{1,0},{2,3},{3,2},{4,5},{5,4},{6,7},{7,6},{8,9},{9,8},{10,11... | collective-permute-start | bytes 49160 | tf_op jit(solution)/shard_map/ppermute | solution.py:296
  19.6 5.1 %collective-permute-start.12 = (bf16[64,128]{1,0:T(8,128)(2,1)S(1)}, bf16[64,128]{1,0:T(8,128)(2,1)S(1)}, u32[]{:S(2)}, u32[]{:S(2)}) collective-permute-start(bf16[64,128]{1,0:T(8,128)(2,1)S(1)} %get-tuple-element.79), channel_id=1, source_target_pairs={{0,16},{1,2},{2,1},{3,4},{4,3},{5,6},{6,5},{7,8},{8,7},{9,10},{10,... | collective-permute-start | bytes 49160 | tf_op jit(solution)/shard_map/ppermute | solution.py:296
  21.2 3.7 %collective-permute-start.13 = (bf16[64,128]{1,0:T(8,128)(2,1)S(1)}, bf16[64,128]{1,0:T(8,128)(2,1)S(1)}, u32[]{:S(2)}, u32[]{:S(2)}) collective-permute-start(bf16[64,128]{1,0:T(8,128)(2,1)S(1)} %get-tuple-element.80), channel_id=1, source_target_pairs={{0,4},{1,5},{2,6},{3,7},{4,0},{5,1},{6,2},{7,3},{8,12},{9,13},{10,... | collective-permute-start | bytes 49160 | tf_op jit(solution)/shard_map/ppermute | solution.py:296
  22.8 2.1 %collective-permute-start.14 = (bf16[64,128]{1,0:T(8,128)(2,1)S(1)}, bf16[64,128]{1,0:T(8,128)(2,1)S(1)}, u32[]{:S(2)}, u32[]{:S(2)}) collective-permute-start(bf16[64,128]{1,0:T(8,128)(2,1)S(1)} %get-tuple-element.81), channel_id=1, source_target_pairs={{0,1},{1,0},{2,3},{3,2},{4,8},{5,9},{6,10},{7,11},{8,4},{9,5},{10,... | collective-permute-start | bytes 49160 | tf_op jit(solution)/shard_map/ppermute | solution.py:296
  22.8 2.1 %collective-permute-start.15 = (bf16[64,128]{1,0:T(8,128)(2,1)S(1)}, bf16[64,128]{1,0:T(8,128)(2,1)S(1)}, u32[]{:S(2)}, u32[]{:S(2)}) collective-permute-start(bf16[64,128]{1,0:T(8,128)(2,1)S(1)} %get-tuple-element.82), channel_id=1, source_target_pairs={{0,1},{1,0},{2,3},{3,2},{4,5},{5,4},{6,7},{7,6},{8,9},{9,8},{10,11... | collective-permute-start | bytes 49160 | tf_op jit(solution)/shard_map/ppermute | solution.py:296
